TPU v7x, 32 devices: a whole 2x2x4 slice. The times are simulated.
32 devices in a mesh: dp: 16 (over z, x, core), tensor: 2 (over y).
Axes of the slice: x: 2, y: 2, z: 4, core: 2. Of those that a mesh axis runs over, the one named last changes fastest.
Arguments:
- tokens: bfloat16 [16384, 1024], P(('dp', 'tensor')), may hold values from -6 to 6
- lengths: int32 [16, 6], P('dp'), may hold values from 0 to 512, as said below
- project_weight: bfloat16 [3, 1024, 1024], P(None, 'dp', 'tensor'), may hold values from -0.25 to 0.25
- project_bias: float32 [2, 1024], P(None, 'tensor'), may hold values from -3 to 3
- output_weight: bfloat16 [1024, 1024], P('tensor', 'dp'), may hold values from -0.5 to 0.5
- output_bias: float32 [1024], replicated, may hold values from -2 to 2
- first_gain: float32 [1024], replicated, may hold values from 0.1 to 1.9
- first_shift: float32 [1024], replicated, may hold values from -3 to 3
- expand_weight: bfloat16 [1024, 4096], P('dp', 'tensor'), may hold values from -0.1875 to 0.1875
- expand_bias: float32 [4096], P('tensor'), may hold values from -3 to 3
- shrink_weight: bfloat16 [4096, 1024], P('tensor', 'dp'), may hold values from -0.125 to 0.125
- shrink_bias: float32 [1024], replicated, may hold values from -2 to 2
- second_gain: float32 [1024], replicated, may hold values from 0.1 to 1.9
- second_shift: float32 [1024], replicated, may hold values from -3 to 3
- cotangent: bfloat16 [16384, 1024], P(('dp', 'tensor')), may hold values from -6 to 6
Outputs:
- layer_output: bfloat16 [16384, 1024], P(('dp', 'tensor'))
- grad_tokens: bfloat16 [16384, 1024], P(('dp', 'tensor'))
- grad_project_weight: float32 [3, 1024, 1024], P(None, 'dp', 'tensor')
- grad_project_bias: float32 [2, 1024], P(None, 'tensor')
- grad_output_weight: float32 [1024, 1024], P('tensor', 'dp')
- grad_output_bias: float32 [1024], replicated
- grad_first_gain: float32 [1024], replicated
- grad_first_shift: float32 [1024], replicated
- grad_expand_weight: float32 [1024, 4096], P('dp', 'tensor')
- grad_expand_bias: float32 [4096], P('tensor')
- grad_shrink_weight: float32 [4096, 1024], P('tensor', 'dp')
- grad_shrink_bias: float32 [1024], replicated
- grad_second_gain: float32 [1024], replicated
- grad_second_shift: float32 [1024], replicated
Inputs may be any that keep to these rules, and one draw needn't show every extreme that they name: In each buffer the lengths sum to between 512 and 1024; one buffer is filled to exactly 1024 and begins with a sequence of 512. Zero lengths come only after the last nonzero one.
All inputs are finite; a program needn't handle non-finite values.
Results may differ from a plain program's by a relative error of at most 0.023.
Values may be sent and summed in bfloat16 or wider, within the bound.
No kernel may reach another device: no remote copies, remote signals or barrier semaphores. Data moves between devices by JAX's collectives and lax.ppermute only.
A program may use at most 192 MiB of HBM per device.

v0:
```python
from functools import partial

import jax
import jax.numpy as jnp
from jax import lax
from jax.sharding import PartitionSpec as P

HEAD_DIM = 64
BLOCK = 512


norm_eps = 1e-05
big_negative = -1e30
exact_gelu = partial(jax.nn.gelu, approximate=False)


def layer_norm(rows, gain_vec, shift_vec):
    average = jnp.mean(rows, axis=-1, keepdims=True)
    centered = rows - average
    variance = jnp.mean(centered * centered, axis=-1, keepdims=True)
    return centered * lax.rsqrt(variance + norm_eps) * gain_vec + shift_vec


def on_device(
    tokens,
    lengths,
    project_weight,
    project_bias,
    output_weight,
    output_bias,
    first_gain,
    first_shift,
    expand_weight,
    expand_bias,
    shrink_weight,
    shrink_bias,
    second_gain,
    second_shift,
    cotangent,
):
    f32 = jnp.float32
    bf16 = jnp.bfloat16
    local_rows = tokens.shape[0]
    buffer_rows = local_rows * lax.axis_size("tensor")
    first_row = lax.axis_index("tensor") * local_rows
    block_count = buffer_rows // BLOCK
    score_scale = HEAD_DIM ** (-0.5)
    ends = jnp.cumsum(lengths[0], dtype=jnp.int32)
    positions = lax.iota(jnp.int32, buffer_rows)
    segment = jnp.sum(
        (positions[:, None] >= ends[None, :]).astype(jnp.int32), axis=1, dtype=jnp.int32
    )
    local_valid = first_row + lax.iota(jnp.int32, local_rows) < ends[-1]
    whole_tokens = lax.all_gather(tokens, "tensor", axis=0, tiled=True)
    gathered = (
        lax.all_gather(project_weight, "dp", axis=1, tiled=True),
        lax.all_gather(output_weight, "dp", axis=1, tiled=True),
        lax.all_gather(expand_weight, "dp", axis=0, tiled=True),
        lax.all_gather(shrink_weight, "dp", axis=1, tiled=True),
    )
    proj_full, mix_full, expand_full, shrink_full = gathered
    bias_rows = jnp.stack([project_bias[0], jnp.zeros_like(project_bias[0]), project_bias[1]])
    projected = jnp.einsum("rd,cde->rce", whole_tokens, proj_full, preferred_element_type=f32)
    projected = (projected + bias_rows[None]).astype(bf16)
    local_heads = projected.shape[2] // HEAD_DIM
    query_heads = projected[:, 0].reshape(buffer_rows, local_heads, HEAD_DIM)
    key_heads = projected[:, 1].reshape(buffer_rows, local_heads, HEAD_DIM)
    value_heads = projected[:, 2].reshape(buffer_rows, local_heads, HEAD_DIM)

    def attend_block(index):
        begin_row = index * BLOCK
        query_block = lax.dynamic_slice_in_dim(query_heads, begin_row, BLOCK, 0)
        segment_block = lax.dynamic_slice_in_dim(segment, begin_row, BLOCK, 0)
        scores = (
            jnp.einsum("qhd,khd->hqk", query_block, key_heads, preferred_element_type=f32)
            * score_scale
        )
        same = segment_block[:, None] == segment[None, :]
        masked = jnp.where(same[None], scores, big_negative)
        top_score = jnp.max(masked, axis=-1, keepdims=True)
        weights = jnp.exp(masked - top_score)
        totals = jnp.sum(weights, axis=-1, keepdims=True)
        probs_low = (weights / totals).astype(bf16)
        mixed_block = jnp.einsum("hqk,khd->qhd", probs_low, value_heads, preferred_element_type=f32)
        return (mixed_block.astype(bf16), top_score + jnp.log(totals))

    mixed_blocks, log_totals = lax.map(attend_block, jnp.arange(block_count, dtype=jnp.int32))
    mixed = mixed_blocks.reshape(buffer_rows, local_heads * HEAD_DIM)
    rows_in = mixed
    attn_local = (
        lax.psum_scatter(
            jnp.dot(rows_in, mix_full, preferred_element_type=f32).astype(jnp.bfloat16),
            "tensor",
            scatter_dimension=0,
            tiled=True,
        ).astype(jnp.float32)
        + output_bias
    )
    first_out, first_pull = jax.vjp(
        layer_norm, tokens.astype(f32) + attn_local, first_gain, first_shift
    )
    first_low = first_out.astype(bf16)
    whole_first = lax.all_gather(first_low, "tensor", axis=0, tiled=True)
    upper = jnp.dot(whole_first, expand_full, preferred_element_type=f32) + expand_bias
    active_full, gelu_pull = jax.vjp(exact_gelu, upper)
    active = active_full.astype(bf16)
    rows_in = lax.slice_in_dim(active, 0, local_rows * lax.axis_size("tensor"), axis=0)
    branch = (
        lax.psum_scatter(
            jnp.dot(rows_in, shrink_full, preferred_element_type=f32).astype(jnp.bfloat16),
            "tensor",
            scatter_dimension=0,
            tiled=True,
        ).astype(jnp.float32)
        + shrink_bias
    )
    second_out, second_pull = jax.vjp(layer_norm, first_out + branch, second_gain, second_shift)
    layer_output = jnp.where(local_valid[:, None], second_out, 0.0).astype(bf16)
    output_grad = jnp.where(local_valid[:, None], cotangent.astype(f32), 0.0)
    grad_second_in, grad_second_gain, grad_second_shift = second_pull(output_grad)
    branch_grad = grad_second_in.astype(bf16)
    grad_shrink_bias = jnp.sum(branch_grad, axis=0, dtype=f32)
    gathered = (
        lax.all_gather(project_weight, "dp", axis=1, tiled=True),
        lax.all_gather(output_weight, "dp", axis=1, tiled=True),
        lax.all_gather(expand_weight, "dp", axis=0, tiled=True),
        lax.all_gather(shrink_weight, "dp", axis=1, tiled=True),
    )
    proj_full, mix_full, expand_full, shrink_full = gathered
    whole_branch_grad = lax.all_gather(branch_grad, "tensor", axis=0, tiled=True)
    grad_shrink_local = jnp.einsum(
        "rf,rd->fd", active, whole_branch_grad, preferred_element_type=f32
    )
    active_grad = jnp.einsum(
        "rd,fd->rf", whole_branch_grad, shrink_full, preferred_element_type=f32
    )
    upper_grad = gelu_pull(active_grad)[0].astype(bf16)
    grad_expand_local = jnp.einsum("rd,rf->df", whole_first, upper_grad, preferred_element_type=f32)
    grad_expand_bias = jnp.sum(upper_grad, axis=0, dtype=f32)
    rows_in = upper_grad
    first_out_grad = (
        lax.psum_scatter(
            jnp.einsum("rf,df->rd", rows_in, expand_full, preferred_element_type=f32).astype(
                jnp.bfloat16
            ),
            "tensor",
            scatter_dimension=0,
            tiled=True,
        ).astype(jnp.float32)
        + grad_second_in
    )
    grad_first_in, grad_first_gain, grad_first_shift = first_pull(first_out_grad)
    whole_attn_grad = lax.all_gather(grad_first_in.astype(bf16), "tensor", axis=0, tiled=True)
    grad_output_bias = jnp.sum(whole_attn_grad, axis=0, dtype=f32)
    grad_output_local = jnp.einsum("re,rd->ed", mixed, whole_attn_grad, preferred_element_type=f32)
    mixed_grad = jnp.einsum(
        "rd,ed->re", whole_attn_grad, mix_full, preferred_element_type=f32
    ).astype(bf16)
    mixed_grad_heads = mixed_grad.reshape(buffer_rows, local_heads, HEAD_DIM)

    def attend_back(carry, index):
        key_grad, value_grad = carry
        begin_row = index * BLOCK
        query_block = lax.dynamic_slice_in_dim(query_heads, begin_row, BLOCK, 0)
        segment_block = lax.dynamic_slice_in_dim(segment, begin_row, BLOCK, 0)
        grad_block = lax.dynamic_slice_in_dim(mixed_grad_heads, begin_row, BLOCK, 0)
        scores = (
            jnp.einsum("qhd,khd->hqk", query_block, key_heads, preferred_element_type=f32)
            * score_scale
        )
        same = segment_block[:, None] == segment[None, :]
        masked = jnp.where(same[None], scores, big_negative)
        probs = jnp.exp(masked - log_totals[index])
        probs_low = probs.astype(bf16)
        value_grad = value_grad + jnp.einsum(
            "hqk,qhd->khd", probs_low, grad_block, preferred_element_type=f32
        )
        prob_grad = jnp.einsum("qhd,khd->hqk", grad_block, value_heads, preferred_element_type=f32)
        inner = jnp.sum(probs * prob_grad, axis=-1, keepdims=True)
        score_grad = (probs * (prob_grad - inner)).astype(bf16)
        query_grad = (
            jnp.einsum("hqk,khd->qhd", score_grad, key_heads, preferred_element_type=f32)
            * score_scale
        )
        key_grad = (
            key_grad
            + jnp.einsum("hqk,qhd->khd", score_grad, query_block, preferred_element_type=f32)
            * score_scale
        )
        return ((key_grad, value_grad), query_grad)

    empty_heads = jnp.zeros((buffer_rows, local_heads, HEAD_DIM), f32)
    (key_grad, value_grad), query_grads = lax.scan(
        attend_back, (empty_heads, empty_heads), jnp.arange(block_count, dtype=jnp.int32)
    )
    width_local = local_heads * HEAD_DIM
    projected_grad = jnp.stack(
        [
            query_grads.reshape(buffer_rows, width_local),
            key_grad.reshape(buffer_rows, width_local),
            value_grad.reshape(buffer_rows, width_local),
        ],
        axis=1,
    ).astype(bf16)
    grad_project_local = jnp.einsum(
        "rd,rce->cde", whole_tokens, projected_grad, preferred_element_type=f32
    )
    grad_project_bias = jnp.stack(
        [
            jnp.sum(projected_grad[:, 0], axis=0, dtype=f32),
            jnp.sum(projected_grad[:, 2], axis=0, dtype=f32),
        ]
    )
    rows_in = projected_grad
    token_grad = (
        lax.psum_scatter(
            jnp.einsum("rce,cde->rd", rows_in, proj_full, preferred_element_type=f32).astype(
                jnp.bfloat16
            ),
            "tensor",
            scatter_dimension=0,
            tiled=True,
        ).astype(jnp.float32)
        + grad_first_in
    )
    grad_tokens = token_grad.astype(bf16)
    grad_project_weight, grad_output_weight, grad_expand_weight, grad_shrink_weight = (
        lax.psum_scatter(
            grad_project_local.astype(jnp.bfloat16), "dp", scatter_dimension=1, tiled=True
        ).astype(jnp.float32),
        lax.psum_scatter(
            grad_output_local.astype(jnp.bfloat16), "dp", scatter_dimension=1, tiled=True
        ).astype(jnp.float32),
        lax.psum_scatter(
            grad_expand_local.astype(jnp.bfloat16), "dp", scatter_dimension=0, tiled=True
        ).astype(jnp.float32),
        lax.psum_scatter(
            grad_shrink_local.astype(jnp.bfloat16), "dp", scatter_dimension=1, tiled=True
        ).astype(jnp.float32),
    )
    grad_project_bias, grad_expand_bias, grad_output_bias = lax.psum(
        (grad_project_bias, grad_expand_bias, grad_output_bias), "dp"
    )
    grad_first_gain, grad_first_shift, grad_second_gain, grad_second_shift, grad_shrink_bias = (
        lax.psum(
            (
                grad_first_gain,
                grad_first_shift,
                grad_second_gain,
                grad_second_shift,
                grad_shrink_bias,
            ),
            ("dp", "tensor"),
        )
    )
    return (
        layer_output,
        grad_tokens,
        grad_project_weight,
        grad_project_bias,
        grad_output_weight,
        grad_output_bias,
        grad_first_gain,
        grad_first_shift,
        grad_expand_weight,
        grad_expand_bias,
        grad_shrink_weight,
        grad_shrink_bias,
        grad_second_gain,
        grad_second_shift,
    )


def solution(mesh):
    placed = (
        P(("dp", "tensor"), None),
        P("dp", None),
        P(None, "dp", "tensor"),
        P(None, "tensor"),
        P("tensor", "dp"),
        P(),
        P(),
        P(),
        P("dp", "tensor"),
        P("tensor"),
        P("tensor", "dp"),
        P(),
        P(),
        P(),
        P(("dp", "tensor"), None),
    )
    return jax.shard_map(
        on_device,
        mesh=mesh,
        in_specs=placed,
        out_specs=(
            P(("dp", "tensor"), None),
            P(("dp", "tensor"), None),
            P(None, "dp", "tensor"),
            P(None, "tensor"),
            P("tensor", "dp"),
            P(),
            P(),
            P(),
            P("dp", "tensor"),
            P("tensor"),
            P("tensor", "dp"),
            P(),
            P(),
            P(),
        ),
        check_vma=False,
    )
```

profile of v0, /device:TPU:0, one launch (start us, length us, event | category | flops | bytes accessed | tf_op | source)
XLA Modules:
  0.0 855.4 jit_solution(1296569973650941528)
XLA Ops:
  11.3 34.1 %all-gather.9.cloned.1.call-done = bf16[1024,1024]{1,0:T(8,128)(2,1)} async-done(((bf16[512,1024]{1,0:T(8,128)(2,1)}), bf16[1024,1024]{1,0:T(8,128)(2,1)}) %all-gather.9.cloned.1.call-update) | async-done | bytes 2097168 | tf_op jit(solution)/shard_map/all_gather | solution.py:54
  45.4 47.4 %all-gather.11.cloned.1.call-done = bf16[3,1024,512]{2,1,0:T(8,128)(2,1)} async-done(((bf16[3,64,512]{2,1,0:T(8,128)(2,1)}), bf16[3,1024,512]{2,1,0:T(8,128)(2,1)}) %all-gather.11.cloned.1.call-update) | async-done | bytes 3145744 | tf_op jit(solution)/shard_map/all_gather | solution.py:56
  92.8 6.0 add_convert_fusion.1
  100.5 32.1 %while.27 = (s32[]{:T(128)}, bf16[2,512,8,64]{1,3,2,0:T(8,128)(2,1)S(1)}, f32[2,8,512,1]{2,1,3,0:T(8,128)S(1)}, s32[2]{0:T(128)S(1)}, s32[1024]{0:T(1024)S(1)}, ...) while((s32[]{:T(128)}, ...), condition=%wide.region_5.6_spmd, body=%wide.region_2.5_spmd.sunk | while | flops 1124855808 | bytes 55716040 | solution.py:87
  139.0 30.1 %reduce-scatter.8.cloned.1.call-done = bf16[512,1024]{1,0:T(8,128)(2,1)} async-done(((bf16[1024,1024]{1,0:T(8,128)(2,1)}), bf16[512,1024]{1,0:T(8,128)(2,1)}) %reduce-scatter.8.cloned.1.call-update) | async-done | bytes 1048592 | tf_op jit(solution)/shard_map/reduce_scatter | solution.py:91
  175.1 46.9 %all-gather.17.cloned.1.call-done = bf16[1024,2048]{1,0:T(8,128)(2,1)} async-done(((bf16[64,2048]{1,0:T(8,128)(2,1)}), bf16[1024,2048]{1,0:T(8,128)(2,1)}) %all-gather.17.cloned.1.call-update) | async-done | bytes 4194320 | tf_op jit(solution)/shard_map/all_gather | solution.py:58
  221.9 33.7 %all-gather.15.cloned.1.call-done = bf16[1024,1024]{1,0:T(8,128)(2,1)} async-done(((bf16[512,1024]{1,0:T(8,128)(2,1)}), bf16[1024,1024]{1,0:T(8,128)(2,1)}) %all-gather.15.cloned.1.call-update) | async-done | bytes 2097168 | tf_op jit(solution)/shard_map/all_gather | solution.py:103
  255.6 26.7 %multiply_convert_fusion.1 = (bf16[1024,2048]{1,0:T(8,128)(2,1)}, f32[1024,2048]{1,0:T(8,128)}, f32[1024,2048]{1,0:T(8,128)}) fusion(f32[2048]{0:T(1024)S(1)} %copy-done.45, bf16[1024,1024]{1,0:T(8,128)(2,1)} %all-gather.15.cloned.1.call-done, bf16[1024,2048]{1,0:T(8,128)(2,1)} %all-gather.17.cloned.1.call-done), kind=kOutput, calls=%fused_computation.41 | convolution fusion | flops 4433379328 | bytes 27271168 | tf_op jit(solution)/shard_map/dot_general | solution.py:104
  282.4 26.2 %all-gather.19.cloned.1.call-done = bf16[2048,1024]{0,1:T(8,128)(2,1)} async-done(((bf16[2048,64]{0,1:T(8,128)(2,1)}), bf16[2048,1024]{0,1:T(8,128)(2,1)}) %all-gather.19.cloned.1.call-update) | async-done | bytes 4194320 | tf_op jit(solution)/shard_map/all_gather | solution.py:59
  308.6 9.3 %convolution_convert_fusion.3 = bf16[1024,1024]{1,0:T(8,128)(2,1)} fusion(bf16[1024,2048]{1,0:T(8,128)(2,1)} %get-tuple-element.275, bf16[2048,1024]{0,1:T(8,128)(2,1)} %all-gather.19.cloned.1.call-done), kind=kOutput, calls=%fused_computation.87 | convolution fusion | flops 4296015872 | bytes 10485760 | tf_op jit(solution)/shard_map/dot_general | solution.py:110
  319.3 29.2 %reduce-scatter.10.cloned.1.call-done = bf16[512,1024]{1,0:T(8,128)(2,1)} async-done(((bf16[1024,1024]{1,0:T(8,128)(2,1)}), bf16[512,1024]{1,0:T(8,128)(2,1)}) %reduce-scatter.10.cloned.1.call-update) | async-done | bytes 1048592 | tf_op jit(solution)/shard_map/reduce_scatter | solution.py:109
  358.2 33.2 %all-gather.21.cloned.1.call-done = bf16[1024,1024]{1,0:T(8,128)(2,1)} async-done(((bf16[512,1024]{1,0:T(8,128)(2,1)}), bf16[1024,1024]{1,0:T(8,128)(2,1)}) %all-gather.21.cloned.1.call-update) | async-done | bytes 2097168 | tf_op jit(solution)/shard_map/all_gather | solution.py:130
  391.4 13.9 %convert_reduce_fusion = (f32[2048]{0:T(1024)}, bf16[1024,2048]{1,0:T(8,128)(2,1)S(1)}) fusion(f32[1024,2048]{1,0:T(8,128)} %get-tuple-element.276, f32[1024,2048]{1,0:T(8,128)} %get-tuple-element.287, f32[2048]{0:T(1024)S(1)} %copy-done.45, bf16[1024,1024]{1,0:T(8,128)(2,1)} %all-gather.21.cloned.1.call-done, ...), kind=kOutput, calls=%fused_computation.39 | convolution fusion | flops 4330616832 | bytes 27279360 | tf_op jit(solution)/shard_map/rd,fd->rf/dot_general | solution.py:134
  413.2 31.9 %reduce-scatter.12.cloned.1.call-done = bf16[512,1024]{1,0:T(8,128)(2,1)} async-done(((bf16[1024,1024]{1,0:T(8,128)(2,1)}), bf16[512,1024]{1,0:T(8,128)(2,1)}) %reduce-scatter.12.cloned.1.call-update) | async-done | bytes 1048592 | tf_op jit(solution)/shard_map/reduce_scatter | solution.py:142
  452.8 8.4 convolution_convert_fusion
  462.9 8.3 convolution_convert_fusion.1
  471.2 14.7 %all-gather.23.cloned.1.call-done = bf16[1024,1024]{1,0:T(8,128)(2,1)} async-done(((bf16[512,1024]{1,0:T(8,128)(2,1)}), bf16[1024,1024]{1,0:T(8,128)(2,1)}) %all-gather.23.cloned.1.call-update) | async-done | bytes 2097168 | tf_op jit(solution)/shard_map/all_gather | solution.py:153
  489.9 94.0 %while.28 = (s32[]{:T(128)}, f32[1024,8,64]{0,2,1:T(8,128)}, f32[1024,8,64]{0,2,1:T(8,128)}, bf16[2,512,8,64]{1,3,2,0:T(8,128)(2,1)}, s32[2]{0:T(128)S(1)}, /*in...) while((s32[]{:T(128)}, f32[1024,8,64]{0,2,1:T(8,128)}, ...), condition=%wide.region_19.20_spmd.clone, body=%wide.region_17.19_spmd.clone.sunk | while | flops 2725507072 | bytes 215378544 | solution.py:193
  499.3 11.1 %multiply_reduce_fusion.8 = (f32[8,512]{1,0:T(8,128)S(1)}, f32[8,512,1024]{2,1,0:T(8,128)}) fusion(f32[8,512,1024]{2,1,0:T(8,128)S(1)} %fusion.107, f32[8,512]{1,0:T(8,128)S(1)} %copy-done.18, bf16[1024,8,64]{0,2,1:T(8,128)(2,1)} %copy-done.1, bf16[1024,8,64]{0,2,1:T(8,128)(2,1)} %get-tuple-element.485, s32[]{:T(128)S(6)} %select_n.71, ...), kind=kOutput, calls=%fused_computation.17.clone.1 | convolution fusion | flops 557838336 | bytes 35684356 | tf_op jit(solution)/shard_map/while/body/eval_jaxpr/qhd,khd->hqk/dot_general | solution.py:168
  510.3 9.5 %multiply_convert_fusion.3 = bf16[8,512,1024]{2,1,0:T(8,128)(2,1)} fusion(f32[8,512,1024]{2,1,0:T(8,128)} %get-tuple-element.410, f32[8,512,1024]{2,1,0:T(8,128)S(1)} %fusion.107, f32[8,512]{1,0:T(8,128)S(1)} %get-tuple-element.411), kind=kLoop, calls=%fused_computation.16.clone.1 | loop fusion | flops 12582912 | bytes 41959424 | tf_op jit(solution)/shard_map/while/body/eval_jaxpr/convert_element_type | solution.py:180
  519.8 8.9 %bitcast_add_fusion.5 = f32[1024,8,64]{0,2,1:T(8,128)} fusion(f32[1024,8,64]{0,2,1:T(8,128)} %get-tuple-element.466, f32[8,512,1024]{2,1,0:T(8,128)} %get-tuple-element.410, pred[]{:T(512)S(6)} %compare.3, bf16[1024,8,64]{0,2,1:T(8,128)(2,1)S(1)} %copy-done.11, s32[]{:T(128)S(6)} %select_n.71), kind=kOutput, calls=%fused_computation.21.clone.1 | convolution fusion | flops 542113792 | bytes 21495812 | tf_op jit(solution)/shard_map/while/body/eval_jaxpr/hqk,qhd->khd/dot_general | solution.py:175
  545.4 11.0 %multiply_reduce_fusion.8 = (f32[8,512]{1,0:T(8,128)S(1)}, f32[8,512,1024]{2,1,0:T(8,128)}) fusion(f32[8,512,1024]{2,1,0:T(8,128)S(1)} %fusion.107, f32[8,512]{1,0:T(8,128)S(1)} %copy-done.18, bf16[1024,8,64]{0,2,1:T(8,128)(2,1)} %copy-done.1, bf16[1024,8,64]{0,2,1:T(8,128)(2,1)} %get-tuple-element.485, s32[]{:T(128)S(6)} %select_n.71, ...), kind=kOutput, calls=%fused_computation.17.clone.1 | convolution fusion | flops 557838336 | bytes 35684356 | tf_op jit(solution)/shard_map/while/body/eval_jaxpr/qhd,khd->hqk/dot_general | solution.py:168
  556.4 9.5 %multiply_convert_fusion.3 = bf16[8,512,1024]{2,1,0:T(8,128)(2,1)} fusion(f32[8,512,1024]{2,1,0:T(8,128)} %get-tuple-element.410, f32[8,512,1024]{2,1,0:T(8,128)S(1)} %fusion.107, f32[8,512]{1,0:T(8,128)S(1)} %get-tuple-element.411), kind=kLoop, calls=%fused_computation.16.clone.1 | loop fusion | flops 12582912 | bytes 41959424 | tf_op jit(solution)/shard_map/while/body/eval_jaxpr/convert_element_type | solution.py:180
  565.9 9.7 %bitcast_add_fusion.5 = f32[1024,8,64]{0,2,1:T(8,128)} fusion(f32[1024,8,64]{0,2,1:T(8,128)} %get-tuple-element.466, f32[8,512,1024]{2,1,0:T(8,128)} %get-tuple-element.410, pred[]{:T(512)S(6)} %compare.3, bf16[1024,8,64]{0,2,1:T(8,128)(2,1)S(1)} %copy-done.11, s32[]{:T(128)S(6)} %select_n.71), kind=kOutput, calls=%fused_computation.21.clone.1 | convolution fusion | flops 542113792 | bytes 21495812 | tf_op jit(solution)/shard_map/while/body/eval_jaxpr/hqk,qhd->khd/dot_general | solution.py:175
  595.3 7.5 convert_bitcast_fusion
  602.8 7.8 copy.55
  614.4 7.7 bitcast_convert_fusion
  623.4 41.2 %all-reduce.1 = (f32[1024]{0:T(1024)}, f32[1024]{0:T(1024)}, f32[1024]{0:T(1024)}, f32[1024]{0:T(1024)}, f32[1024]{0:T(1024)}) all-reduce(f32[1024]{0:T(1024)S(1)} %copy-done.33, f32[1024]{0:T(1024)S(1)} %copy-done.34, f32[1024]{0:T(1024)S(1)} %copy-done.32, ...), channel_id=1, replica_groups=mesh['dp'=16,'tensor'=2] {'dp','tensor'}, use_global_device_ids=true, to_apply=%region_29.30 | all-reduce | flops 5120 | bytes 40960 | tf_op jit(solution)/shard_map/psum | solution.py:245
  671.9 60.2 %all-reduce.2 = (f32[2,512]{1,0:T(2,128)}, f32[1024]{0:T(1024)}, f32[2048]{0:T(1024)}) all-reduce(f32[2,512]{1,0:T(2,128)S(1)} %pad_maximum_fusion.4, f32[1024]{0:T(1024)S(1)} %convert_reduce_fusion.1, f32[2048]{0:T(1024)S(1)} %copy-done.36), channel_id=1, replica_groups=mesh['dp'=16,'tensor'=2] {'dp'}, use_global_device_ids=true, to_apply=%region_24.25 | all-reduce | flops 4096 | bytes 32768 | tf_op jit(solution)/shard_map/psum | solution.py:241
  732.1 21.2 %all-reduce.5.cloned.1.call-done = bf16[3,1024,512]{2,0,1:T(4,128)(2,1)} async-done(((bf16[3,1024,512]{2,0,1:T(4,128)(2,1)}), bf16[3,1024,512]{2,0,1:T(4,128)(2,1)}) %all-reduce.5.cloned.1.call-update) | async-done | bytes 3145744
  755.2 57.9 %reduce-scatter.16.cloned.1.call-done = bf16[512,64]{0,1:T(8,128)(2,1)} async-done(((bf16[512,1024]{0,1:T(8,128)(2,1)}), bf16[512,64]{0,1:T(8,128)(2,1)}) %reduce-scatter.16.cloned.1.call-update) | async-done | bytes 65552 | tf_op jit(solution)/shard_map/reduce_scatter | solution.py:231
  814.6 31.6 %reduce-scatter.14.cloned.1.call-done = bf16[512,1024]{1,0:T(8,128)(2,1)} async-done(((bf16[1024,1024]{1,0:T(8,128)(2,1)}), bf16[512,1024]{1,0:T(8,128)(2,1)}) %reduce-scatter.14.cloned.1.call-update) | async-done | bytes 1048592 | tf_op jit(solution)/shard_map/reduce_scatter | solution.py:216
  (241 shorter events, 138.0 us)
Async XLA Ops:
  7.2 38.2 %all-gather.9.cloned.1.call-start = ((), (), s32[]{:S(2)}) async-start(), calls=%async_computation.7 | async-start | bytes 3145728 | tf_op jit(solution)/shard_map/all_gather | solution.py:54
  7.9 84.9 %all-gather.11.cloned.1.call-start = ((), (), s32[]{:S(2)}) async-start(), calls=%async_computation.8 | async-start | bytes 3342336 | tf_op jit(solution)/shard_map/all_gather | solution.py:56
  8.7 125.3 %all-gather.13.cloned.1.call-start = ((), (), s32[]{:S(2)}) async-start(), calls=%async_computation.9 | async-start | bytes 1114112 | tf_op jit(solution)/shard_map/all_gather | solution.py:57
  9.4 159.7 %reduce-scatter.8.cloned.1.call-start = ((), (), s32[]{:S(2)}) async-start(), calls=%async_computation.10 | async-start | bytes 3145728 | tf_op jit(solution)/shard_map/reduce_scatter | solution.py:91
  134.0 35.1 %copy-start.7 = (bf16[512,1024]{1,0:T(8,128)(2,1)S(1)}, bf16[512,1024]{1,0:T(8,128)(2,1)}, u32[]{:S(2)}) copy-start(bf16[512,1024]{1,0:T(8,128)(2,1)} %param.19) | copy-start | bytes 3145732
  134.0 35.1 %copy-start.25 = (f32[1024]{0:T(1024)S(1)}, f32[1024]{0:T(1024)}, u32[]{:S(2)}) copy-start(f32[1024]{0:T(1024)} %param.24) | copy-start | bytes 12292
  138.3 34.4 %copy-start.26 = (f32[1024]{0:T(1024)S(1)}, f32[1024]{0:T(1024)}, u32[]{:S(2)}) copy-start(f32[1024]{0:T(1024)} %param.25) | copy-start | bytes 12292
  138.3 34.4 %copy-start.35 = (f32[1024]{0:T(1024)S(1)}, f32[1024]{0:T(1024)}, u32[]{:S(2)}) copy-start(f32[1024]{0:T(1024)} %param.26) | copy-start | bytes 12292
  138.3 83.6 %all-gather.17.cloned.1.call-start = ((), (), s32[]{:S(2)}) async-start(), calls=%async_computation.12 | async-start | bytes 4456448 | tf_op jit(solution)/shard_map/all_gather | solution.py:58
  138.9 116.8 %copy-start.45 = (f32[2048]{0:T(1024)S(1)}, f32[2048]{0:T(1024)}, u32[]{:S(2)}) copy-start(f32[2048]{0:T(1024)} %param.28) | copy-start | bytes 24580
  138.9 116.7 %all-gather.15.cloned.1.call-start = ((), (), s32[]{:S(2)}) async-start(), calls=%async_computation.11 | async-start | bytes 3145728 | tf_op jit(solution)/shard_map/all_gather | solution.py:103
  174.3 134.4 %all-gather.19.cloned.1.call-start = ((), (), s32[]{:S(2)}) async-start(), calls=%async_computation.13 | async-start | bytes 4456448 | tf_op jit(solution)/shard_map/all_gather | solution.py:59
  175.0 173.4 %reduce-scatter.10.cloned.1.call-start = ((), (), s32[]{:S(2)}) async-start(), calls=%async_computation.14 | async-start | bytes 3145728 | tf_op jit(solution)/shard_map/reduce_scatter | solution.py:109
  308.6 39.8 %copy-start.38 = (f32[1024]{0:T(1024)S(1)}, f32[1024]{0:T(1024)}, u32[]{:S(2)}) copy-start(f32[1024]{0:T(1024)} %param.30) | copy-start | bytes 12292
  318.0 33.2 %copy-start.29 = (f32[1024]{0:T(1024)S(1)}, f32[1024]{0:T(1024)}, u32[]{:S(2)}) copy-start(f32[1024]{0:T(1024)} %param.31) | copy-start | bytes 12292
  318.0 73.5 %all-gather.21.cloned.1.call-start = ((), (), s32[]{:S(2)}) async-start(), calls=%async_computation.15 | async-start | bytes 3145728 | tf_op jit(solution)/shard_map/all_gather | solution.py:130
  319.3 33.4 %copy-start.37 = (f32[1024]{0:T(1024)S(1)}, f32[1024]{0:T(1024)}, u32[]{:S(2)}) copy-start(f32[1024]{0:T(1024)} %param.32) | copy-start | bytes 12292
  358.2 86.9 %reduce-scatter.12.cloned.1.call-start = ((), (), s32[]{:S(2)}) async-start(), calls=%async_computation.16 | async-start | bytes 3145728 | tf_op jit(solution)/shard_map/reduce_scatter | solution.py:142
  391.4 15.9 %copy-start.41 = (bf16[1024,2048]{1,0:T(8,128)(2,1)S(1)}, bf16[1024,2048]{1,0:T(8,128)(2,1)}, u32[]{:S(2)}) copy-start(bf16[1024,2048]{1,0:T(8,128)(2,1)} %all-gather.17.cloned.1.call-done) | copy-start | bytes 12582916
  413.1 72.8 %all-gather.23.cloned.1.call-start = ((), (), s32[]{:S(2)}) async-start(), calls=%async_computation.17 | async-start | bytes 3145728 | tf_op jit(solution)/shard_map/all_gather | solution.py:153
  450.2 10.9 %copy-start.27 = (f32[512]{0:T(512)}, f32[512]{0:T(512)S(1)}, u32[]{:S(2)}) copy-start(f32[512]{0:T(512)S(1)} %negate_multiply_fusion.1) | copy-start | bytes 6148
  452.7 212.0 %reduce-scatter.20.cloned.1.call-start = ((), (), s32[]{:S(2)}) async-start(), calls=%async_computation.21 | async-start | bytes 4456448 | tf_op jit(solution)/shard_map/reduce_scatter | solution.py:237
  461.1 205.3 %reduce-scatter.18.cloned.1.call-start = ((), (), s32[]{:S(2)}) async-start(), calls=%async_computation.20 | async-start | bytes 4456448 | tf_op jit(solution)/shard_map/reduce_scatter | solution.py:234
  471.2 14.8 %copy-start.44 = (bf16[512,1024]{0,1:T(8,128)(2,1)S(1)}, bf16[512,1024]{0,1:T(8,128)(2,1)}, u32[]{:S(2)}) copy-start(bf16[512,1024]{0,1:T(8,128)(2,1)} %all-gather.13.cloned.1.call-done) | copy-start | bytes 3145732
  471.2 282.1 %all-reduce.5.cloned.1.call-start = ((), (), s32[]{:S(2)}) async-start(), calls=%async_computation.22 | async-start | bytes 8388608
  565.9 10.2 %copy-start.2 = (bf16[1024,8,64]{0,2,1:T(8,128)(2,1)S(1)}, bf16[1024,8,64]{0,2,1:T(8,128)(2,1)}, u32[]{:S(2)}) copy-start(bf16[1024,8,64]{0,2,1:T(8,128)(2,1)} %copy-done.1) | copy-start | bytes 3145732 | tf_op jit(solution)/shard_map/while
  565.9 10.7 %copy-start.20 = (bf16[2,512,8,64]{1,3,2,0:T(8,128)(2,1)S(1)}, bf16[2,512,8,64]{1,3,2,0:T(8,128)(2,1)}, u32[]{:S(2)}) copy-start(bf16[2,512,8,64]{1,3,2,0:T(8,128)(2,1)} %get-tuple-element.467) | copy-start | bytes 3145732 | tf_op jit(solution)/shard_map/while
  610.6 202.5 %reduce-scatter.16.cloned.1.call-start = ((), (), s32[]{:S(2)}) async-start(), calls=%async_computation.19 | async-start | bytes 1114112 | tf_op jit(solution)/shard_map/reduce_scatter | solution.py:231
  614.3 231.9 %reduce-scatter.14.cloned.1.call-start = ((), (), s32[]{:S(2)}) async-start(), calls=%async_computation.18 | async-start | bytes 3145728 | tf_op jit(solution)/shard_map/reduce_scatter | solution.py:216
  622.1 49.8 %copy-start.36 = (f32[2048]{0:T(1024)S(1)}, f32[2048]{0:T(1024)}, u32[]{:S(2)}) copy-start(f32[2048]{0:T(1024)} %get-tuple-element.267) | copy-start | bytes 24580
  622.1 224.1 %copy-start.13 = (f32[512,1024]{1,0:T(8,128)S(1)}, f32[512,1024]{1,0:T(8,128)}, u32[]{:S(2)}) copy-start(f32[512,1024]{1,0:T(8,128)} %copy-done.12) | copy-start | bytes 6291460
  622.1 224.1 %copy-start.28 = (f32[512]{0:T(512)S(1)}, f32[512]{0:T(512)}, u32[]{:S(2)}) copy-start(f32[512]{0:T(512)} %copy-done.27) | copy-start | bytes 6148
  (44 other events, 217.0 us)
Sparse Core Ops, SparseCore 0:
  9.6 35.8 all-gather.8
  47.6 45.1 all-gather.10
  95.0 36.7 all-gather.12
  138.4 30.6 reduce-scatter.7
  171.3 50.5 all-gather.16
  224.0 31.6 all-gather.14
  258.0 50.5 all-gather.18
  318.1 30.3 reduce-scatter.9
  358.3 33.0 all-gather.20
  413.3 31.8 reduce-scatter.11
  452.8 33.1 all-gather.22
  490.2 72.7 reduce-scatter.19
  566.8 71.3 reduce-scatter.17
  642.2 111.0 all-reduce.4
  756.8 56.2 reduce-scatter.15
  815.3 30.8 reduce-scatter.13
where the time goes:
time: 861 us; the launch traced here: 855 us
  waiting for transfers between devices  442 us (51%)
  matrix products  185 us (21%)
  blocking collectives  101 us (12%)
  other arithmetic  67 us (8%)
  local copies, waits for them, and re-layouts  36.7 us (4%)
  between operations  15.3 us (2%)
    psum x1, blocking collectives, on_device(): lax.psum((grad_project_bias, grad_expand_bias, grad_output_bias), 'dp')  60.2 us
    reduce_scatter x1, waiting for transfers between devices, on_device(): lax.psum_scatter(grad_output_local.astype(jnp.bfloat16), 'dp', scatter_di...  57.9 us
    all_gather x1, waiting for transfers between devices, on_device(): lax.all_gather(project_weight, 'dp', axis=1, tiled=True)  47.4 us
    all_gather x1, waiting for transfers between devices, on_device(): lax.all_gather(expand_weight, 'dp', axis=0, tiled=True)  46.9 us
    psum x1, blocking collectives, on_device(): lax.psum((grad_first_gain, grad_first_shift, grad_second_gain, grad_secon...  41.2 us
    all_gather x1, waiting for transfers between devices, on_device(): whole_tokens = lax.all_gather(tokens, 'tensor', axis=0, tiled=True)  34.1 us
    all_gather x1, waiting for transfers between devices, on_device(): whole_first = lax.all_gather(first_low, 'tensor', axis=0, tiled=True)  33.7 us
    all_gather x1, waiting for transfers between devices, on_device(): lax.all_gather(branch_grad, 'tensor', axis=0, tiled=True)  33.2 us
  transfers between devices with their start and end apart: 16, of which 13 were waited for; matrix products, arithmetic and copies ran while one was open for 27% of the time, Pallas kernels for 0%

commit v1 on v0

v1 whole, which is shorter than its diff:
```python
from functools import partial

import jax
import jax.numpy as jnp
from jax import lax
from jax.sharding import PartitionSpec as P

HEAD_DIM = 64
BLOCK = 512
EPS = 1e-05
BIG_NEGATIVE = -1e30
ALL = ("dp", "tensor")
Z, X, C, Y = range(4)
F32 = jnp.float32
BF16 = jnp.bfloat16


def digit_sizes():
    rest = lax.axis_size("dp")
    core = 2 if rest % 2 == 0 else 1
    rest //= core
    across = 2 if rest % 2 == 0 else 1
    rest //= across
    return (rest, across, core, lax.axis_size("tensor"))


def my_digits(sizes):
    dp = lax.axis_index("dp")
    return (
        dp // (sizes[X] * sizes[C]),
        dp // sizes[C] % sizes[X],
        dp % sizes[C],
        lax.axis_index("tensor"),
    )


def hop(value, sizes, digit, step=1):
    pairs = []
    nz, nx, nc, ny = sizes
    for z in range(nz):
        for x in range(nx):
            for c in range(nc):
                for y in range(ny):
                    there = [z, x, c, y]
                    there[digit] = (there[digit] + step) % sizes[digit]
                    source = ((z * nx + x) * nc + c) * ny + y
                    target = ((there[0] * nx + there[1]) * nc + there[2]) * ny + there[3]
                    pairs.append((source, target))
    return lax.ppermute(value, ALL, pairs)


def ring(value, sizes, digit):
    pieces = [value]
    for _ in range(sizes[digit] - 1):
        pieces.append(hop(pieces[-1], sizes, digit))
    return pieces


def place(pieces, index, axis):
    count = len(pieces)
    if count == 1:
        return jnp.expand_dims(pieces[0], axis)
    shape = list(pieces[0].shape)
    shape.insert(axis, count)
    out = jnp.zeros(shape, pieces[0].dtype)
    for k, piece in enumerate(pieces):
        out = lax.dynamic_update_index_in_dim(out, piece, (index - k) % count, axis)
    return out


def pick(value, index, axis):
    return lax.dynamic_index_in_dim(value, index, axis, keepdims=False)


def ring_sum(value, sizes, digit, index, axis):
    count = sizes[digit]
    if count == 1:
        return jnp.squeeze(value, axis)
    moving = pick(value, (index - 1) % count, axis)
    for k in range(1, count):
        moving = hop(moving, sizes, digit) + pick(value, (index - 1 - k) % count, axis)
    return moving


def gather_xzc(shard, sizes, at):
    rows, width = shard.shape
    both = place(ring(shard, sizes, X), at[X], 0)
    deep = place(ring(both, sizes, Z), at[Z], 0)
    full = place(ring(deep, sizes, C), at[C], 2)
    return full.reshape(-1, width)


def gather_zxyc(shard, sizes, at, widths):
    deep = place(ring(shard, sizes, Z), at[Z], 0)
    across = ring(deep, sizes, X)
    halves = list(zip(*[ring(piece, sizes, Y) for piece in across]))
    out = []
    for half in halves:
        cored = list(zip(*[ring(piece, sizes, C) for piece in half]))
        mats = []
        begin = 0
        for width in widths:
            parts = [
                place([p[..., begin : begin + width] for p in by_x], at[X], 1) for by_x in cored
            ]
            mats.append(place(parts, at[C], 2).reshape(-1, width))
            begin += width
        out.append(mats)
    return out


def gather_yzxc(shard, sizes, at):
    width = shard.shape[-1]
    halves = jnp.stack(ring(shard, sizes, Y))
    deep = place(ring(halves, sizes, Z), at[Z], 1)
    cored = [ring(piece, sizes, C) for piece in ring(deep, sizes, X)]
    out = []
    for k in range(sizes[Y]):
        parts = [place([by_c[c][k] for by_c in cored], at[X], 1) for c in range(sizes[C])]
        out.append(place(parts, at[C], 2).reshape(-1, width))
    return out


def core_sum(value, sizes, at):
    return ring_sum(value, sizes, C, at[C], 2)


def scatter_czx(full, sizes, at):
    width = full.shape[-1]
    parts = core_sum(full.reshape(sizes[Z], sizes[X], sizes[C], -1, width), sizes, at)
    return ring_sum(ring_sum(parts, sizes, Z, at[Z], 0), sizes, X, at[X], 0)


def y_sum(halves, sizes):
    count = sizes[Y]
    total = halves[0]
    for k in range(1, count):
        total = total + hop(halves[k], sizes, Y, -k)
    return total


def scatter_cyxz(halves, sizes, at):
    width = halves[0].shape[-1]
    parts = [
        core_sum(h.reshape(sizes[Z], sizes[X], sizes[C], -1, width), sizes, at) for h in halves
    ]
    mine = y_sum(parts, sizes)
    return ring_sum(ring_sum(mine, sizes, X, at[X], 1), sizes, Z, at[Z], 0)


def scatter_cxzy(halves, sizes, at):
    width = halves[0].shape[-1]
    parts = [
        core_sum(h.reshape(sizes[Z], sizes[X], sizes[C], -1, width), sizes, at) for h in halves
    ]
    parts = jnp.stack([ring_sum(p, sizes, X, at[X], 1) for p in parts], axis=1)
    parts = ring_sum(parts, sizes, Z, at[Z], 0)
    return y_sum([parts[k] for k in range(sizes[Y])], sizes)


def norm_parts(rows):
    average = jnp.mean(rows, axis=-1, keepdims=True)
    centered = rows - average
    scale = lax.rsqrt(jnp.mean(centered * centered, axis=-1, keepdims=True) + EPS)
    return centered * scale, scale


def norm_back(grad, unit, scale, gain):
    inner = grad * gain
    return scale * (
        inner
        - jnp.mean(inner, axis=-1, keepdims=True)
        - unit * jnp.mean(inner * unit, axis=-1, keepdims=True)
    )


def gelu_both(upper):
    below = 0.5 * lax.erfc(upper * -(0.5**0.5))
    density = jnp.exp(-0.5 * upper * upper) * 0.3989422804014327
    return upper * below, below + upper * density


def dot(a, b, dims):
    return lax.dot_general(a, b, (dims, ((), ())), preferred_element_type=F32)


NN = ((1,), (0,))
NT = ((1,), (1,))
TN = ((0,), (0,))


def attention(query, key, value, segment):
    rows, width = query.shape
    heads = width // HEAD_DIM
    scale = HEAD_DIM ** (-0.5)
    query, key, value = (t.reshape(rows, heads, HEAD_DIM) for t in (query, key, value))

    def attend_block(index):
        begin = index * BLOCK
        query_block = lax.dynamic_slice_in_dim(query, begin, BLOCK, 0)
        segment_block = lax.dynamic_slice_in_dim(segment, begin, BLOCK, 0)
        scores = jnp.einsum("qhd,khd->hqk", query_block, key, preferred_element_type=F32) * scale
        same = segment_block[:, None] == segment[None, :]
        masked = jnp.where(same[None], scores, BIG_NEGATIVE)
        top = jnp.max(masked, axis=-1, keepdims=True)
        weights = jnp.exp(masked - top)
        totals = jnp.sum(weights, axis=-1, keepdims=True)
        low = (weights / totals).astype(BF16)
        mixed = jnp.einsum("hqk,khd->qhd", low, value, preferred_element_type=F32)
        return mixed.astype(BF16), top + jnp.log(totals)

    mixed, logs = lax.map(attend_block, jnp.arange(rows // BLOCK, dtype=jnp.int32))
    return mixed.reshape(rows, width), logs


def attention_back(query, key, value, segment, logs, grad):
    rows, width = query.shape
    heads = width // HEAD_DIM
    scale = HEAD_DIM ** (-0.5)
    query, key, value, grad = (
        t.reshape(rows, heads, HEAD_DIM) for t in (query, key, value, grad)
    )

    def attend_back(carry, index):
        key_grad, value_grad = carry
        begin = index * BLOCK
        query_block = lax.dynamic_slice_in_dim(query, begin, BLOCK, 0)
        segment_block = lax.dynamic_slice_in_dim(segment, begin, BLOCK, 0)
        grad_block = lax.dynamic_slice_in_dim(grad, begin, BLOCK, 0)
        scores = jnp.einsum("qhd,khd->hqk", query_block, key, preferred_element_type=F32) * scale
        same = segment_block[:, None] == segment[None, :]
        masked = jnp.where(same[None], scores, BIG_NEGATIVE)
        probs = jnp.exp(masked - logs[index])
        low = probs.astype(BF16)
        value_grad = value_grad + jnp.einsum(
            "hqk,qhd->khd", low, grad_block, preferred_element_type=F32
        )
        prob_grad = jnp.einsum("qhd,khd->hqk", grad_block, value, preferred_element_type=F32)
        inner = jnp.sum(probs * prob_grad, axis=-1, keepdims=True)
        score_grad = (probs * (prob_grad - inner)).astype(BF16)
        query_grad = (
            jnp.einsum("hqk,khd->qhd", score_grad, key, preferred_element_type=F32) * scale
        )
        key_grad = (
            key_grad
            + jnp.einsum("hqk,qhd->khd", score_grad, query_block, preferred_element_type=F32)
            * scale
        )
        return ((key_grad, value_grad), query_grad.astype(BF16))

    empty = jnp.zeros((rows, heads, HEAD_DIM), F32)
    (key_grad, value_grad), query_grad = lax.scan(
        attend_back, (empty, empty), jnp.arange(rows // BLOCK, dtype=jnp.int32)
    )
    return tuple(t.reshape(rows, width).astype(BF16) for t in (query_grad, key_grad, value_grad))


def on_device(
    tokens,
    lengths,
    project_weight,
    project_bias,
    output_weight,
    output_bias,
    first_gain,
    first_shift,
    expand_weight,
    expand_bias,
    shrink_weight,
    shrink_bias,
    second_gain,
    second_shift,
    cotangent,
):
    sizes = digit_sizes()
    at = my_digits(sizes)
    n_t = sizes[Y]
    mine = at[Y]
    rows, width = tokens.shape
    all_rows = rows * n_t
    heads_width = project_weight.shape[2]
    hidden = expand_weight.shape[1]
    depth = project_weight.shape[1]

    ends = jnp.cumsum(lengths[0], dtype=jnp.int32)
    positions = lax.iota(jnp.int32, all_rows)
    segment = jnp.sum(
        (positions[:, None] >= ends[None, :]).astype(jnp.int32), axis=1, dtype=jnp.int32
    )
    valid = (mine * rows + lax.iota(jnp.int32, rows) < ends[-1])[:, None]

    whole_tokens = place(ring(tokens, sizes, Y), mine, 0).reshape(all_rows, width)
    proj = gather_xzc(
        jnp.transpose(project_weight, (1, 0, 2)).reshape(depth, 3 * heads_width), sizes, at
    )
    gathered = gather_zxyc(
        jnp.concatenate([output_weight.T, expand_weight], axis=1),
        sizes,
        at,
        (heads_width, hidden),
    )
    mix = [g[0] for g in gathered]
    expand = [g[1] for g in gathered]
    shrink = gather_yzxc(shrink_weight.T, sizes, at)
    expand_biases = ring(expand_bias, sizes, Y)

    bias = jnp.concatenate([project_bias[0], jnp.zeros_like(project_bias[0]), project_bias[1]])
    projected = (dot(whole_tokens, proj, NN) + bias).astype(BF16)
    query, key, value = (
        projected[:, c * heads_width : (c + 1) * heads_width] for c in range(3)
    )
    mixed_heads, logs = attention(query, key, value, segment)
    by_rows = mixed_heads.reshape(n_t, rows, heads_width)
    mixed = [pick(by_rows, mine, 0)]
    for k in range(1, n_t):
        mixed.append(hop(pick(by_rows, (mine + k) % n_t, 0), sizes, Y, k))

    attn = sum(dot(m, w, NT) for m, w in zip(mixed, mix)) + output_bias
    unit1, scale1 = norm_parts(tokens.astype(F32) + attn)
    normed1 = unit1 * first_gain + first_shift
    low1 = normed1.astype(BF16)
    active, slope = [], []
    for w, b in zip(expand, expand_biases):
        act, der = gelu_both(dot(low1, w, NN) + b)
        active.append(act.astype(BF16))
        slope.append(der.astype(BF16))
    branch = sum(dot(a, w, NT) for a, w in zip(active, shrink)) + shrink_bias
    unit2, scale2 = norm_parts(normed1 + branch)
    layer_output = jnp.where(valid, unit2 * second_gain + second_shift, 0.0).astype(BF16)

    grad = jnp.where(valid, cotangent.astype(F32), 0.0)
    grad_second_gain = jnp.sum(grad * unit2, axis=0)
    grad_second_shift = jnp.sum(grad, axis=0)
    grad_r2 = norm_back(grad, unit2, scale2, second_gain)
    grad_branch = grad_r2.astype(BF16)
    grad_shrink_bias = jnp.sum(grad_branch, axis=0, dtype=F32)
    grad_shrink = [dot(grad_branch, a, TN).astype(BF16) for a in active]
    grad_shrink_weight = scatter_cxzy(grad_shrink, sizes, at).astype(F32).T
    grad_upper = [
        (dot(grad_branch, w, NN) * s.astype(F32)).astype(BF16) for w, s in zip(shrink, slope)
    ]
    grad_expand_biases = [jnp.sum(g, axis=0, dtype=F32) for g in grad_upper]
    grad_expand = [dot(low1, g, TN).astype(BF16) for g in grad_upper]
    grad_normed1 = sum(dot(g, w, NT) for g, w in zip(grad_upper, expand)) + grad_r2
    grad_first_gain = jnp.sum(grad_normed1 * unit1, axis=0)
    grad_first_shift = jnp.sum(grad_normed1, axis=0)
    grad_r1 = norm_back(grad_normed1, unit1, scale1, first_gain)
    grad_attn = grad_r1.astype(BF16)
    grad_output_bias = jnp.sum(grad_attn, axis=0, dtype=F32)

    grad_by_rows = jnp.zeros((n_t, rows, heads_width), BF16)
    for k, w in enumerate(mix):
        part = dot(grad_attn, w, NN).astype(BF16)
        if k:
            part = hop(part, sizes, Y, -k)
        grad_by_rows = lax.dynamic_update_index_in_dim(grad_by_rows, part, (mine + k) % n_t, 0)
    grad_mix = [dot(grad_attn, m, TN).astype(BF16) for m in mixed]
    owned = scatter_cyxz(
        [jnp.concatenate([a, b], axis=1) for a, b in zip(grad_mix, grad_expand)], sizes, at
    ).astype(F32)
    grad_output_weight = owned[:, :heads_width].T
    grad_expand_weight = owned[:, heads_width:]

    packed = jnp.concatenate(
        [
            grad_second_gain,
            grad_second_shift,
            grad_shrink_bias,
            grad_first_gain,
            grad_first_shift,
            grad_output_bias,
            place(grad_expand_biases, mine, 0).reshape(-1),
        ]
    )
    packed = lax.psum(packed, ALL)
    (
        grad_second_gain,
        grad_second_shift,
        grad_shrink_bias,
        grad_first_gain,
        grad_first_shift,
        grad_output_bias,
    ) = (packed[i * width : (i + 1) * width] for i in range(6))
    grad_expand_bias = pick(packed[6 * width :].reshape(n_t, hidden), mine, 0)

    projected_grad = jnp.concatenate(
        attention_back(
            query, key, value, segment, logs, grad_by_rows.reshape(all_rows, heads_width)
        ),
        axis=1,
    )
    grad_project_bias = lax.psum(
        jnp.stack(
            [
                jnp.sum(projected_grad[:, :heads_width], axis=0, dtype=F32),
                jnp.sum(projected_grad[:, 2 * heads_width :], axis=0, dtype=F32),
            ]
        ),
        "dp",
    )
    grad_project = scatter_czx(dot(whole_tokens, projected_grad, TN).astype(BF16), sizes, at)
    grad_project_weight = jnp.transpose(
        grad_project.reshape(depth, 3, heads_width), (1, 0, 2)
    ).astype(F32)
    token_grad = grad_r1
    for k in range(n_t):
        begin = (mine + k) % n_t * rows
        part = dot(lax.dynamic_slice_in_dim(projected_grad, begin, rows, 0), proj, NT)
        if k:
            part = hop(part.astype(BF16), sizes, Y, k).astype(F32)
        token_grad = token_grad + part
    grad_tokens = token_grad.astype(BF16)
    return (
        layer_output,
        grad_tokens,
        grad_project_weight,
        grad_project_bias,
        grad_output_weight,
        grad_output_bias,
        grad_first_gain,
        grad_first_shift,
        grad_expand_weight,
        grad_expand_bias,
        grad_shrink_weight,
        grad_shrink_bias,
        grad_second_gain,
        grad_second_shift,
    )


def solution(mesh):
    rows = P(("dp", "tensor"), None)
    weights = (P(None, "dp", "tensor"), P("tensor", "dp"), P("dp", "tensor"), P("tensor", "dp"))
    in_specs = (
        rows,
        P("dp", None),
        weights[0],
        P(None, "tensor"),
        weights[1],
        P(),
        P(),
        P(),
        weights[2],
        P("tensor"),
        weights[3],
        P(),
        P(),
        P(),
        rows,
    )
    out_specs = (
        rows,
        rows,
        weights[0],
        P(None, "tensor"),
        weights[1],
        P(),
        P(),
        P(),
        weights[2],
        P("tensor"),
        weights[3],
        P(),
        P(),
        P(),
    )
    return jax.shard_map(
        on_device, mesh=mesh, in_specs=in_specs, out_specs=out_specs, check_vma=False
    )
```

time: 861 us -> 676 us (0.79)
  waiting for transfers between devices: 442 us -> 173 us
  local copies, waits for them, and re-layouts: 36.7 us -> 116 us
  starting transfers between devices: 0.65 us -> 34.5 us
  blocking collectives: 101 us -> 70.4 us
  matrix products: 185 us -> 201 us
  between operations: 15.3 us -> 2.88 us
    all_gather x8 -> x0, waiting for transfers between devices: 236 us -> none  [the longest x1 47.4 us: on_device(): lax.all_gather(project_weight, 'dp', axis=1, tiled=True)]
    reduce_scatter x7 -> x0, waiting for transfers between devices: 181 us -> none  [the longest x1 57.9 us: on_device(): lax.psum_scatter(grad_output_local.astype(jnp.bfloat16), 'dp', scatter_di...]
    ppermute x0 -> x47, waiting for transfers between devices: none -> 173 us  [hop(): return lax.ppermute(value, ALL, pairs)]
    dynamic_update_slice x0 -> x53, local copies, waits for them, and re-layouts: none -> 54 us  [the longest x51 35.9 us: place(): out = lax.dynamic_update_index_in_dim(out, piece, (index - k) % count, axis)]
    ppermute x0 -> x47, starting transfers between devices: none -> 34.5 us  [hop(): return lax.ppermute(value, ALL, pairs)]
    psum x2, blocking collectives: 101 us -> 70.4 us  [the longest x1 37.3 us: on_device(): packed = lax.psum(packed, ALL)]
    unnamed x17 -> x0, waiting for transfers between devices: 24.7 us -> none
    broadcast_in_dim x0 -> x24, local copies, waits for them, and re-layouts: none -> 12.5 us  [the longest x13 4.9 us: place(): out = lax.dynamic_update_index_in_dim(out, piece, (index - k) % count, axis)]
  transfers between devices with their start and end apart: 16 -> 47, of which waited for: 13 -> 16; matrix products, arithmetic and copies ran while one was open for 27% -> 45% of each run, Pallas kernels for 0% -> 0%
where the time goes in v1:
time: 676 us; the launch traced here: 668 us
  matrix products  201 us (30%)
  waiting for transfers between devices  173 us (26%)
  local copies, waits for them, and re-layouts  116 us (17%)
  blocking collectives  70.4 us (10%)
  other arithmetic  63.5 us (9%)
  starting transfers between devices  34.5 us (5%)
  loops' own time  7.06 us (1%)
    ppermute x47, waiting for transfers between devices, hop(): return lax.ppermute(value, ALL, pairs)  173 us
    dot_general x22, matrix products, dot(): return lax.dot_general(a, b, (dims, ((), ())), preferred_element_type=F32)  95.2 us
    psum x1, blocking collectives, on_device(): packed = lax.psum(packed, ALL)  37.3 us
    dynamic_update_slice x51, local copies, waits for them, and re-layouts, place(): out = lax.dynamic_update_index_in_dim(out, piece, (index - k) % count, axis)  35.9 us
    ppermute x47, starting transfers between devices, hop(): return lax.ppermute(value, ALL, pairs)  34.5 us
    psum x1, blocking collectives, on_device(): lax.psum(jnp.stack([jnp.sum(projected_grad[:, :heads_width], axis=0, dtyp...  33.2 us
    dot_general x2, matrix products, attend_back(): jnp.einsum('qhd,khd->hqk', query_block, key, preferred_element_type=F32)  32.1 us
    dot_general x2, matrix products, attend_back(): jnp.einsum('qhd,khd->hqk', grad_block, value, preferred_element_type=F32)  19.1 us
  transfers between devices with their start and end apart: 47, of which 16 were waited for; matrix products, arithmetic and copies ran while one was open for 45% of the time, Pallas kernels for 0%

profile of v1, /device:TPU:0, one launch (start us, length us, event | category | flops | bytes accessed | tf_op | source)
XLA Modules:
  0.0 668.5 jit_solution(4259040252603572100)
XLA Ops:
  27.4 6.7 %collective-permute-done.2 = bf16[2,64,1536]{2,1,0:T(8,128)(2,1)S(1)} collective-permute-done((bf16[2,64,1536]{2,1,0:T(8,128)(2,1)S(1)}, bf16[2,64,1536]{2,1,0:T(8,128)(2,1)S(1)}, u32[]{:S(2)}, u32[]{:S(2)}) %collective-permute-start.2) | collective-permute-done | bytes 393248 | tf_op jit(solution)/shard_map/ppermute | solution.py:49
  34.1 18.2 %collective-permute-done.7 = bf16[64,2560]{1,0:T(8,128)(2,1)S(1)} collective-permute-done((bf16[64,2560]{1,0:T(8,128)(2,1)}, bf16[64,2560]{1,0:T(8,128)(2,1)S(1)}, u32[]{:S(2)}, u32[]{:S(2)}) %collective-permute-start.7) | collective-permute-done | bytes 327712 | tf_op jit(solution)/shard_map/ppermute | solution.py:49
  54.6 13.2 %collective-permute-done.8 = bf16[64,2560]{1,0:T(8,128)(2,1)S(1)} collective-permute-done((bf16[64,2560]{1,0:T(8,128)(2,1)S(1)}, bf16[64,2560]{1,0:T(8,128)(2,1)S(1)}, u32[]{:S(2)}, u32[]{:S(2)}) %collective-permute-start.8) | collective-permute-done | bytes 327712 | tf_op jit(solution)/shard_map/ppermute | solution.py:49
  77.3 9.5 %collective-permute-done.4 = bf16[2,64,1536]{2,1,0:T(8,128)(2,1)S(1)} collective-permute-done((bf16[2,64,1536]{2,1,0:T(8,128)(2,1)S(1)}, bf16[2,64,1536]{2,1,0:T(8,128)(2,1)S(1)}, u32[]{:S(2)}, u32[]{:S(2)}) %collective-permute-start.4) | collective-permute-done | bytes 393248 | tf_op jit(solution)/shard_map/ppermute | solution.py:49
  87.3 11.7 %collective-permute-done.20 = bf16[2,64,2048]{2,1,0:T(8,128)(2,1)S(1)} collective-permute-done((bf16[2,64,2048]{2,1,0:T(8,128)(2,1)S(1)}, bf16[2,64,2048]{2,1,0:T(8,128)(2,1)S(1)}, u32[]{:S(2)}, u32[]{:S(2)}) %collective-permute-start.20) | collective-permute-done | bytes 524320 | tf_op jit(solution)/shard_map/ppermute | solution.py:49
  126.1 30.0 %while.27 = (s32[]{:T(128)}, bf16[2,512,8,64]{1,3,2,0:T(8,128)(2,1)S(1)}, f32[2,8,512,1]{2,1,3,0:T(8,128)S(1)}, s32[2]{0:T(128)S(1)}, s32[1024]{0:T(1024)S(1)}, ...) while((s32[]{:T(128)}, ...), condition=%wide.region_5.6_spmd, body=%wide.region_2.5_spmd.sunk | while | flops 1124855808 | bytes 55716032 | solution.py:212
  183.6 13.1 %multiply_convert_fusion.4 = (bf16[512,2048]{1,0:T(8,128)(2,1)S(1)}, f32[512,2048]{1,0:T(8,128)}, f32[512,2048]{1,0:T(8,128)}) fusion(f32[2048]{0:T(1024)S(1)} %copy-done.63, bf16[512,1024]{1,0:T(8,128)(2,1)S(1)} %fusion.57, bf16[1024,2048]{1,0:T(8,128)(2,1)S(1)} %bitcast.445), kind=kOutput, calls=%fused_computation.76 | convolution fusion | flops 2215641088 | bytes 15736832 | tf_op jit(solution)/shard_map/dot_general | solution.py:184
  200.8 13.4 %multiply_convert_fusion.3 = (bf16[512,2048]{1,0:T(8,128)(2,1)S(1)}, f32[512,2048]{1,0:T(8,128)}, f32[512,2048]{1,0:T(8,128)}) fusion(f32[2048]{0:T(1024)} %collective-permute-done.24, bf16[512,1024]{1,0:T(8,128)(2,1)S(1)} %fusion.57, bf16[1024,2048]{1,0:T(8,128)(2,1)S(1)} %bitcast.447), kind=kOutput, calls=%fused_computation.63 | convolution fusion | flops 2215641088 | bytes 15736832 | tf_op jit(solution)/shard_map/dot_general | solution.py:184
  227.8 6.7 %convert_reduce_fusion.1 = (f32[2048]{0:T(1024)S(1)}, bf16[512,2048]{1,0:T(8,128)(2,1)}) fusion(f32[512,2048]{1,0:T(8,128)S(1)} %copy-done.65, f32[512,2048]{1,0:T(8,128)} %get-tuple-element.299, f32[2048]{0:T(1024)S(1)} %copy-done.63, bf16[512,1024]{1,0:T(8,128)(2,1)S(1)} %get-tuple-element.270, bf16[1024,2048]{1,0:T(8,128)(2,1)S(1)} %bitcast.444), kind=kOutput, calls=%fused_computation.60 | convolution fusion | flops 2160064512 | bytes 15745024 | tf_op jit(solution)/shard_map/dot_general | solution.py:184
  268.7 37.3 %psum.15 = f32[10240]{0:T(1024)S(1)} all-reduce(f32[10240]{0:T(1024)S(1)} %constant_dynamic-update-slice_fusion.13), channel_id=1, replica_groups=mesh['dp'=16,'tensor'=2] {'dp','tensor'}, use_global_device_ids=true, to_apply=%region_28.29 | all-reduce | flops 10240 | bytes 81920 | tf_op jit(solution)/shard_map/psum | solution.py:375
  324.8 9.1 %dynamic_update_slice.275 = bf16[2,512,512]{1,0,2:T(2,128)(2,1)S(1)} dynamic-update-slice(bf16[2,512,512]{1,0,2:T(2,128)(2,1)S(1)} %broadcast_in_dim.330, bf16[1,512,512]{1,0,2:T(2,128)(2,1)S(1)} %copy.144, s32[]{:T(128)S(6)} %select_n.405, s32[]{:T(128)} %constant.637.clone.1, s32[]{:T(128)} %constant.637.clone.1) | dynamic-update-slice | bytes 1048580 | tf_op jit(solution)/shard_map/jit(dynamic_update_index_in_dim)/dynamic_update_slice | solution.py:356
  338.4 9.1 %dynamic_update_slice.276 = bf16[2,512,512]{1,0,2:T(2,128)(2,1)S(1)} dynamic-update-slice(bf16[2,512,512]{1,0,2:T(2,128)(2,1)S(1)} %dynamic_update_slice.275, bf16[1,512,512]{1,0,2:T(2,128)(2,1)S(1)} %copy.145, s32[]{:T(128)S(6)} %select_n.430, s32[]{:T(128)} %constant.637.clone.1, s32[]{:T(128)} %constant.637.clone.1) | dynamic-update-slice | bytes 1048580 | tf_op jit(solution)/shard_map/jit(dynamic_update_index_in_dim)/dynamic_update_slice | solution.py:356
  350.1 118.7 %while.28 = (s32[]{:T(128)}, f32[1024,8,64]{0,2,1:T(8,128)}, f32[1024,8,64]{0,2,1:T(8,128)}, bf16[2,512,8,64]{1,3,2,0:T(8,128)(2,1)}, s32[2]{0:T(128)S(1)}, /*in...) while((s32[]{:T(128)}, f32[1024,8,64]{0,2,1:T(8,128)}, ...), condition=%wide.region_16.17_spmd.clone, body=%wide.region_14.16_spmd.clone.sunk | while | flops 2725769216 | bytes 266955216 | solution.py:252
  351.5 9.5 %fusion.202 = f32[8,512,1024]{2,1,0:T(8,128)} fusion(bf16[1024,8,64]{0,2,1:T(8,128)(2,1)} %get-tuple-element.509, bf16[1024,8,64]{0,2,1:T(8,128)(2,1)} %get-tuple-element.508, s32[]{:T(128)S(6)} %select_n.490), kind=kOutput, calls=%fused_computation.29.clone.1 | convolution fusion | flops 536870912 | bytes 18350084 | tf_op jit(solution)/shard_map/while/body/eval_jaxpr/qhd,khd->hqk/dot_general | solution.py:238
  365.6 16.0 %multiply_reduce_fusion.9 = (f32[8,512]{1,0:T(8,128)}, f32[8,512,1024]{2,1,0:T(8,128)}) fusion(f32[8,512,1024]{2,1,0:T(8,128)} %fusion.202, f32[8,512]{1,0:T(8,128)} %dynamic-slice_bitcast_fusion.14, bf16[1024,8,64]{0,2,1:T(8,128)(2,1)S(1)} %get-tuple-element.506, bf16[1024,8,64]{0,2,1:T(8,128)(2,1)} %get-tuple-element.504, s32[]{:T(128)S(6)} %select_n.490, ...), kind=kOutput, calls=%fused_computation.17.clone.1 | convolution fusion | flops 557838336 | bytes 35684356 | tf_op jit(solution)/shard_map/while/body/eval_jaxpr/qhd,khd->hqk/dot_general | solution.py:230
  381.6 9.3 %multiply_convert_fusion.7 = bf16[8,512,1024]{2,1,0:T(8,128)(2,1)} fusion(f32[8,512,1024]{2,1,0:T(8,128)} %get-tuple-element.429, f32[8,512,1024]{2,1,0:T(8,128)S(1)} %bitcast.428, f32[8,512]{1,0:T(8,128)} %get-tuple-element.430), kind=kLoop, calls=%fused_computation.16.clone.1 | loop fusion | flops 12582912 | bytes 41959424 | tf_op jit(solution)/shard_map/while/body/eval_jaxpr/convert_element_type | solution.py:240
  397.6 6.9 %fusion.203 = bf16[2,512,8,64]{1,3,2,0:T(8,128)(2,1)S(1)} fusion(bf16[2,512,8,64]{1,3,2,0:T(8,128)(2,1)S(1)} %copy-done.9, s32[]{:T(128)} %get-tuple-element.483, bf16[8,512,1024]{2,1,0:T(8,128)(2,1)} %multiply_convert_fusion.7, bf16[1024,8,64]{0,2,1:T(8,128)(2,1)S(1)} %get-tuple-element.506), kind=kOutput, calls=%fused_computation.26.clone.1 | convolution fusion | flops 537395200 | bytes 9961476 | tf_op jit(solution)/shard_map/while/body/eval_jaxpr/hqk,khd->qhd/dot_general | solution.py:242
  410.1 9.5 %fusion.202 = f32[8,512,1024]{2,1,0:T(8,128)} fusion(bf16[1024,8,64]{0,2,1:T(8,128)(2,1)} %get-tuple-element.509, bf16[1024,8,64]{0,2,1:T(8,128)(2,1)} %get-tuple-element.508, s32[]{:T(128)S(6)} %select_n.490), kind=kOutput, calls=%fused_computation.29.clone.1 | convolution fusion | flops 536870912 | bytes 18350084 | tf_op jit(solution)/shard_map/while/body/eval_jaxpr/qhd,khd->hqk/dot_general | solution.py:238
  424.2 16.1 %multiply_reduce_fusion.9 = (f32[8,512]{1,0:T(8,128)}, f32[8,512,1024]{2,1,0:T(8,128)}) fusion(f32[8,512,1024]{2,1,0:T(8,128)} %fusion.202, f32[8,512]{1,0:T(8,128)} %dynamic-slice_bitcast_fusion.14, bf16[1024,8,64]{0,2,1:T(8,128)(2,1)S(1)} %get-tuple-element.506, bf16[1024,8,64]{0,2,1:T(8,128)(2,1)} %get-tuple-element.504, s32[]{:T(128)S(6)} %select_n.490, ...), kind=kOutput, calls=%fused_computation.17.clone.1 | convolution fusion | flops 557838336 | bytes 35684356 | tf_op jit(solution)/shard_map/while/body/eval_jaxpr/qhd,khd->hqk/dot_general | solution.py:230
  440.3 9.3 %multiply_convert_fusion.7 = bf16[8,512,1024]{2,1,0:T(8,128)(2,1)} fusion(f32[8,512,1024]{2,1,0:T(8,128)} %get-tuple-element.429, f32[8,512,1024]{2,1,0:T(8,128)S(1)} %bitcast.428, f32[8,512]{1,0:T(8,128)} %get-tuple-element.430), kind=kLoop, calls=%fused_computation.16.clone.1 | loop fusion | flops 12582912 | bytes 41959424 | tf_op jit(solution)/shard_map/while/body/eval_jaxpr/convert_element_type | solution.py:240
  449.6 7.2 %bitcast_add_fusion.19 = f32[1024,8,64]{0,2,1:T(8,128)} fusion(f32[1024,8,64]{0,2,1:T(8,128)} %get-tuple-element.484, bf16[8,512,1024]{2,1,0:T(8,128)(2,1)} %multiply_convert_fusion.7, pred[]{:T(512)S(6)} %compare.25, bf16[1024,8,64]{0,2,1:T(8,128)(2,1)} %get-tuple-element.504, s32[]{:T(128)S(6)} %select_n.490), kind=kOutput, calls=%fused_computation.22.clone.1 | convolution fusion | flops 538443776 | bytes 13107205 | tf_op jit(solution)/shard_map/while/body/eval_jaxpr/hqk,qhd->khd/dot_general | solution.py:246
  456.8 6.9 %fusion.203 = bf16[2,512,8,64]{1,3,2,0:T(8,128)(2,1)S(1)} fusion(bf16[2,512,8,64]{1,3,2,0:T(8,128)(2,1)S(1)} %copy-done.9, s32[]{:T(128)} %get-tuple-element.483, bf16[8,512,1024]{2,1,0:T(8,128)(2,1)} %multiply_convert_fusion.7, bf16[1024,8,64]{0,2,1:T(8,128)(2,1)S(1)} %get-tuple-element.506), kind=kOutput, calls=%fused_computation.26.clone.1 | convolution fusion | flops 537395200 | bytes 9961476 | tf_op jit(solution)/shard_map/while/body/eval_jaxpr/hqk,khd->qhd/dot_general | solution.py:242
  472.3 7.2 %convolution_convert_fusion.4 = bf16[1024,1536]{1,0:T(8,128)(2,1)S(1)} fusion(bf16[1024,1024]{1,0:T(8,128)(2,1)} %bitcast.9, bf16[1024,512]{0,1:T(8,128)(2,1)S(1)} %bitcast.454, bf16[1024,512]{0,1:T(8,128)(2,1)S(1)} %bitcast.451, bf16[1024,512]{0,1:T(8,128)(2,1)S(1)} %bitcast.456), kind=kOutput, calls=%fused_computation.95 | convolution fusion | flops 3232235520 | bytes 8388608 | tf_op jit(solution)/shard_map/dot_general | solution.py:184
  486.6 33.2 %psum.14 = f32[2,512]{1,0:T(2,128)} all-reduce(f32[2,512]{1,0:T(2,128)S(1)} %pad_maximum_fusion.6), channel_id=1, replica_groups=mesh['dp'=16,'tensor'=2] {'dp'}, use_global_device_ids=true, to_apply=%region_19.20 | all-reduce | flops 1024 | bytes 8192 | tf_op jit(solution)/shard_map/psum | solution.py:392
  541.2 7.4 %collective-permute-done.29 = bf16[2,64,1536]{2,1,0:T(8,128)(2,1)S(1)} collective-permute-done((bf16[2,64,1536]{2,1,0:T(8,128)(2,1)S(1)}, bf16[2,64,1536]{2,1,0:T(8,128)(2,1)S(1)}, u32[]{:S(2)}, u32[]{:S(2)}) %collective-permute-start.29) | collective-permute-done | bytes 393248 | tf_op jit(solution)/shard_map/ppermute | solution.py:49
  553.2 19.2 %collective-permute-done.40 = bf16[4,64,2048]{2,1,0:T(8,128)(2,1)S(1)} collective-permute-done((bf16[4,64,2048]{2,1,0:T(8,128)(2,1)S(1)}, bf16[4,64,2048]{2,1,0:T(8,128)(2,1)S(1)}, u32[]{:S(2)}, u32[]{:S(2)}) %collective-permute-start.40) | collective-permute-done | bytes 1048608 | tf_op jit(solution)/shard_map/ppermute | solution.py:49
  572.8 11.0 %collective-permute-done.43 = bf16[2,64,2048]{2,1,0:T(8,128)(2,1)S(1)} collective-permute-done((bf16[2,64,2048]{2,1,0:T(8,128)(2,1)S(1)}, bf16[2,64,2048]{2,1,0:T(8,128)(2,1)S(1)}, u32[]{:S(2)}, u32[]{:S(2)}) %collective-permute-start.43) | collective-permute-done | bytes 524320 | tf_op jit(solution)/shard_map/ppermute | solution.py:49
  583.9 18.3 %collective-permute-done.34 = bf16[4,2,64,2560]{3,2,1,0:T(8,128)(2,1)S(1)} collective-permute-done((bf16[4,2,64,2560]{3,2,1,0:T(8,128)(2,1)S(1)}, bf16[4,2,64,2560]{3,2,1,0:T(8,128)(2,1)S(1)}, u32[]{:S(2)}, u32[]{:S(2)}) %collective-permute-start.34) | collective-permute-done | bytes 2621472 | tf_op jit(solution)/shard_map/ppermute | solution.py:49
  612.7 18.4 %collective-permute-done.35 = bf16[4,64,2560]{2,1,0:T(8,128)(2,1)} collective-permute-done((bf16[4,64,2560]{2,1,0:T(8,128)(2,1)}, bf16[4,64,2560]{2,1,0:T(8,128)(2,1)}, u32[]{:S(2)}, u32[]{:S(2)}) %collective-permute-start.35) | collective-permute-done | bytes 1310752 | tf_op jit(solution)/shard_map/ppermute | solution.py:49
  637.9 10.6 %collective-permute-done.36 = bf16[64,2560]{1,0:T(8,128)(2,1)S(1)} collective-permute-done((bf16[64,2560]{1,0:T(8,128)(2,1)S(1)}, bf16[64,2560]{1,0:T(8,128)(2,1)S(1)}, u32[]{:S(2)}, u32[]{:S(2)}) %collective-permute-start.36) | collective-permute-done | bytes 327712 | tf_op jit(solution)/shard_map/ppermute | solution.py:49
  650.1 7.7 %collective-permute-done.37 = bf16[64,2560]{1,0:T(8,128)(2,1)S(1)} collective-permute-done((bf16[64,2560]{1,0:T(8,128)(2,1)S(1)}, bf16[64,2560]{1,0:T(8,128)(2,1)S(1)}, u32[]{:S(2)}, u32[]{:S(2)}) %collective-permute-start.37) | collective-permute-done | bytes 327712 | tf_op jit(solution)/shard_map/ppermute | solution.py:49
  658.7 8.0 %collective-permute-done.38 = bf16[64,2560]{1,0:T(8,128)(2,1)S(1)} collective-permute-done((bf16[64,2560]{1,0:T(8,128)(2,1)S(1)}, bf16[64,2560]{1,0:T(8,128)(2,1)S(1)}, u32[]{:S(2)}, u32[]{:S(2)}) %collective-permute-start.38) | collective-permute-done | bytes 327712 | tf_op jit(solution)/shard_map/ppermute | solution.py:49
  (482 shorter events, 278.8 us)
Async XLA Ops:
  0.7 21.3 %collective-permute-start.17 = (bf16[64,2048]{1,0:T(8,128)(2,1)}, bf16[64,2048]{1,0:T(8,128)(2,1)S(1)}, u32[]{:S(2)}, u32[]{:S(2)}) collective-permute-start(bf16[64,2048]{1,0:T(8,128)(2,1)} %bitcast.471), channel_id=1, source_target_pairs={{0,1},{1,0},{2,3},{3,2},{4,5},{5,4},{6,7},{7,6},{8,9},{9,8},{10,11... | collective-permute-start | bytes 786440 | tf_op jit(solution)/shard_map/ppermute | solution.py:49
  4.8 21.4 %collective-permute-start.6 = (bf16[64,2560]{1,0:T(8,128)(2,1)S(1)}, bf16[64,2560]{1,0:T(8,128)(2,1)}, u32[]{:S(2)}, u32[]{:S(2)}) collective-permute-start(bf16[64,2560]{1,0:T(8,128)(2,1)S(1)} %pad_maximum_fusion.4), channel_id=1, source_target_pairs={{0,8},{1,9},{2,10},{3,11},{4,12},{5,13},{6,14},{7,15},{8,16},{9,17... | collective-permute-start | bytes 983048 | tf_op jit(solution)/shard_map/ppermute | solution.py:49
  9.5 60.0 %collective-permute-start = (bf16[512,1024]{1,0:T(8,128)(2,1)}, bf16[512,1024]{1,0:T(8,128)(2,1)}, u32[]{:S(2)}, u32[]{:S(2)}) collective-permute-start(bf16[512,1024]{1,0:T(8,128)(2,1)} %param.19), channel_id=1, source_target_pairs={{0,1},{1,0},{2,3},{3,2},{4,5},{5,4},{6,7},{7,6},{8,9},{9,8},{10,11... | collective-permute-start | bytes 3145736 | tf_op jit(solution)/shard_map/ppermute | solution.py:49
  10.0 190.8 %collective-permute-start.24 = (f32[2048]{0:T(1024)}, f32[2048]{0:T(1024)}, u32[]{:S(2)}, u32[]{:S(2)}) collective-permute-start(f32[2048]{0:T(1024)} %param.28), channel_id=1, source_target_pairs={{0,1},{1,0},{2,3},{3,2},{4,5},{5,4},{6,7},{7,6},{8,9},{9,8},{10,11... | collective-permute-start | bytes 24584 | tf_op jit(solution)/shard_map/ppermute | solution.py:49
  22.1 30.3 %collective-permute-start.18 = (bf16[2,64,2048]{2,1,0:T(8,128)(2,1)S(1)}, bf16[2,64,2048]{2,1,0:T(8,128)(2,1)S(1)}, u32[]{:S(2)}, u32[]{:S(2)}) collective-permute-start(bf16[2,64,2048]{2,1,0:T(8,128)(2,1)S(1)} %pad_maximum_fusion.3), channel_id=1, source_target_pairs={{0,8},{1,9},{2,10},{3,11},{4,12},{5,13},{6,14},{7,15},{8,16},{9,17... | collective-permute-start | bytes 1572872 | tf_op jit(solution)/shard_map/ppermute | solution.py:49
  26.1 26.2 %collective-permute-start.7 = (bf16[64,2560]{1,0:T(8,128)(2,1)}, bf16[64,2560]{1,0:T(8,128)(2,1)S(1)}, u32[]{:S(2)}, u32[]{:S(2)}) collective-permute-start(bf16[64,2560]{1,0:T(8,128)(2,1)} %collective-permute-done.6), channel_id=1, source_target_pairs={{0,8},{1,9},{2,10},{3,11},{4,12},{5,13},{6,14},{7,15},{8,16},{9,17... | collective-permute-start | bytes 983048 | tf_op jit(solution)/shard_map/ppermute | solution.py:49
  34.1 34.7 %collective-permute-start.3 = (bf16[2,64,1536]{2,1,0:T(8,128)(2,1)S(1)}, bf16[2,64,1536]{2,1,0:T(8,128)(2,1)S(1)}, u32[]{:S(2)}, u32[]{:S(2)}) collective-permute-start(bf16[2,64,1536]{2,1,0:T(8,128)(2,1)S(1)} %collective-permute-done.2), channel_id=1, source_target_pairs={{0,8},{1,9},{2,10},{3,11},{4,12},{5,13},{6,14},{7,15},{8,16},{9,17... | collective-permute-start | bytes 1179656 | tf_op jit(solution)/shard_map/ppermute | solution.py:49
  52.4 24.0 %collective-permute-start.19 = (bf16[2,64,2048]{2,1,0:T(8,128)(2,1)S(1)}, bf16[2,64,2048]{2,1,0:T(8,128)(2,1)S(1)}, u32[]{:S(2)}, u32[]{:S(2)}) collective-permute-start(bf16[2,64,2048]{2,1,0:T(8,128)(2,1)S(1)} %collective-permute-done.18), channel_id=1, source_target_pairs={{0,8},{1,9},{2,10},{3,11},{4,12},{5,13},{6,14},{7,15},{8,16},{9,17... | collective-permute-start | bytes 1572872 | tf_op jit(solution)/shard_map/ppermute | solution.py:49
  67.8 35.7 %collective-permute-start.13 = (bf16[4,64,2560]{2,1,0:T(8,128)(2,1)S(1)}, bf16[4,64,2560]{2,1,0:T(8,128)(2,1)S(1)}, u32[]{:S(2)}, u32[]{:S(2)}) collective-permute-start(bf16[4,64,2560]{2,1,0:T(8,128)(2,1)S(1)} %bitcast_dynamic-update-slice_fusion.13), channel_id=1, source_target_pairs={{0,1},{1,0},{2,3},{3,2},{4,5},{5,4},{6,7},{7,6},{8,9},{9,8},{10,11... | collective-permute-start | bytes 3932168 | tf_op jit(solution)/shard_map/ppermute | solution.py:49
  68.8 35.4 %collective-permute-start.9 = (bf16[4,64,2560]{2,1,0:T(8,128)(2,1)S(1)}, bf16[4,64,2560]{2,1,0:T(8,128)(2,1)}, u32[]{:S(2)}, u32[]{:S(2)}) collective-permute-start(bf16[4,64,2560]{2,1,0:T(8,128)(2,1)S(1)} %bitcast_dynamic-update-slice_fusion.13), channel_id=1, source_target_pairs={{0,4},{1,5},{2,6},{3,7},{4,0},{5,1},{6,2},{7,3},{8,12},{9,13},{10,... | collective-permute-start | bytes 3932168 | tf_op jit(solution)/shard_map/ppermute | solution.py:49
  69.5 37.8 %collective-permute-start.10 = (bf16[4,64,2560]{2,1,0:T(8,128)(2,1)S(1)}, bf16[4,64,2560]{2,1,0:T(8,128)(2,1)S(1)}, u32[]{:S(2)}, u32[]{:S(2)}) collective-permute-start(bf16[4,64,2560]{2,1,0:T(8,128)(2,1)S(1)} %bitcast_dynamic-update-slice_fusion.13), channel_id=1, source_target_pairs={{0,2},{1,3},{2,0},{3,1},{4,6},{5,7},{6,4},{7,5},{8,10},{9,11},{10,... | collective-permute-start | bytes 3932168 | tf_op jit(solution)/shard_map/ppermute | solution.py:49
  103.6 73.3 %collective-permute-start.22 = (bf16[2,4,64,2048]{3,2,1,0:T(8,128)(2,1)}, bf16[2,4,64,2048]{3,2,1,0:T(8,128)(2,1)}, u32[]{:S(2)}, u32[]{:S(2)}) collective-permute-start(bf16[2,4,64,2048]{3,2,1,0:T(8,128)(2,1)} %bitcast_dynamic-update-slice_fusion.8), channel_id=1, source_target_pairs={{0,2},{1,3},{2,0},{3,1},{4,6},{5,7},{6,4},{7,5},{8,10},{9,11},{10,... | collective-permute-start | bytes 6291464 | tf_op jit(solution)/shard_map/ppermute | solution.py:49
  104.2 68.3 %collective-permute-start.21 = (bf16[2,4,64,2048]{3,2,1,0:T(8,128)(2,1)}, bf16[2,4,64,2048]{3,2,1,0:T(8,128)(2,1)}, u32[]{:S(2)}, u32[]{:S(2)}) collective-permute-start(bf16[2,4,64,2048]{3,2,1,0:T(8,128)(2,1)} %bitcast_dynamic-update-slice_fusion.8), channel_id=1, source_target_pairs={{0,4},{1,5},{2,6},{3,7},{4,0},{5,1},{6,2},{7,3},{8,12},{9,13},{10,... | collective-permute-start | bytes 6291464 | tf_op jit(solution)/shard_map/ppermute | solution.py:49
  107.4 48.9 %collective-permute-start.14 = (bf16[4,64,2560]{2,1,0:T(8,128)(2,1)}, bf16[4,64,2560]{2,1,0:T(8,128)(2,1)}, u32[]{:S(2)}, u32[]{:S(2)}) collective-permute-start(bf16[4,64,2560]{2,1,0:T(8,128)(2,1)} %collective-permute-done.9), channel_id=1, source_target_pairs={{0,1},{1,0},{2,3},{3,2},{4,5},{5,4},{6,7},{7,6},{8,9},{9,8},{10,11... | collective-permute-start | bytes 3932168 | tf_op jit(solution)/shard_map/ppermute | solution.py:49
  114.8 45.9 %collective-permute-start.11 = (bf16[4,64,2560]{2,1,0:T(8,128)(2,1)}, bf16[4,64,2560]{2,1,0:T(8,128)(2,1)}, u32[]{:S(2)}, u32[]{:S(2)}) collective-permute-start(bf16[4,64,2560]{2,1,0:T(8,128)(2,1)} %collective-permute-done.9), channel_id=1, source_target_pairs={{0,2},{1,3},{2,0},{3,1},{4,6},{5,7},{6,4},{7,5},{8,10},{9,11},{10,... | collective-permute-start | bytes 3932168 | tf_op jit(solution)/shard_map/ppermute | solution.py:49
  160.7 20.3 %collective-permute-start.12 = (bf16[512,512]{0,1:T(8,128)(2,1)S(1)}, bf16[512,512]{0,1:T(8,128)(2,1)S(1)}, u32[]{:S(2)}, u32[]{:S(2)}) collective-permute-start(bf16[512,512]{0,1:T(8,128)(2,1)S(1)} %dynamic-slice_bitcast_fusion.9), channel_id=1, source_target_pairs={{0,1},{1,0},{2,3},{3,2},{4,5},{5,4},{6,7},{7,6},{8,9},{9,8},{10,11... | collective-permute-start | bytes 1572872 | tf_op jit(solution)/shard_map/ppermute | solution.py:49
  176.3 20.5 %collective-permute-start.23 = (bf16[2,4,64,2048]{3,2,1,0:T(8,128)(2,1)}, bf16[2,4,64,2048]{3,2,1,0:T(8,128)(2,1)S(1)}, u32[]{:S(2)}, u32[]{:S(2)}) collective-permute-start(bf16[2,4,64,2048]{3,2,1,0:T(8,128)(2,1)} %collective-permute-done.21), channel_id=1, source_target_pairs={{0,2},{1,3},{2,0},{3,1},{4,6},{5,7},{6,4},{7,5},{8,10},{9,11},{10,... | collective-permute-start | bytes 6291464 | tf_op jit(solution)/shard_map/ppermute | solution.py:49
  266.5 257.7 %collective-permute-start.41 = (bf16[4,2,64,2048]{3,2,1,0:T(8,128)(2,1)}, bf16[4,2,64,2048]{3,2,1,0:T(8,128)(2,1)}, u32[]{:S(2)}, u32[]{:S(2)}) collective-permute-start(bf16[4,2,64,2048]{3,2,1,0:T(8,128)(2,1)} %dynamic-slice_bitcast_fusion.3), channel_id=1, source_target_pairs={{0,2},{1,3},{2,0},{3,1},{4,6},{5,7},{6,4},{7,5},{8,10},{9,11},{10,... | collective-permute-start | bytes 6291464 | tf_op jit(solution)/shard_map/ppermute | solution.py:49
  268.0 259.3 %collective-permute-start.39 = (bf16[4,2,64,2048]{3,2,1,0:T(8,128)(2,1)}, bf16[4,2,64,2048]{3,2,1,0:T(8,128)(2,1)}, u32[]{:S(2)}, u32[]{:S(2)}) collective-permute-start(bf16[4,2,64,2048]{3,2,1,0:T(8,128)(2,1)} %dynamic-slice_bitcast_fusion.4), channel_id=1, source_target_pairs={{0,2},{1,3},{2,0},{3,1},{4,6},{5,7},{6,4},{7,5},{8,10},{9,11},{10,... | collective-permute-start | bytes 6291464 | tf_op jit(solution)/shard_map/ppermute | solution.py:49
  313.1 270.9 %collective-permute-start.32 = (bf16[4,2,64,2560]{3,2,1,0:T(8,128)(2,1)}, bf16[4,2,64,2560]{3,2,1,0:T(8,128)(2,1)}, u32[]{:S(2)}, u32[]{:S(2)}) collective-permute-start(bf16[4,2,64,2560]{3,2,1,0:T(8,128)(2,1)} %dynamic-slice_bitcast_fusion.2), channel_id=1, source_target_pairs={{0,2},{1,3},{2,0},{3,1},{4,6},{5,7},{6,4},{7,5},{8,10},{9,11},{10,... | collective-permute-start | bytes 7864328 | tf_op jit(solution)/shard_map/ppermute | solution.py:49
  314.4 20.8 %collective-permute-start.25 = (bf16[512,512]{1,0:T(8,128)(2,1)}, bf16[512,512]{1,0:T(8,128)(2,1)S(1)}, u32[]{:S(2)}, u32[]{:S(2)}) collective-permute-start(bf16[512,512]{1,0:T(8,128)(2,1)} %convolution_convert_fusion.7), channel_id=1, source_target_pairs={{0,1},{1,0},{2,3},{3,2},{4,5},{5,4},{6,7},{7,6},{8,9},{9,8},{10,11... | collective-permute-start | bytes 1572872 | tf_op jit(solution)/shard_map/ppermute | solution.py:49
  323.2 215.8 %collective-permute-start.33 = (bf16[4,2,64,2560]{3,2,1,0:T(8,128)(2,1)}, bf16[4,2,64,2560]{3,2,1,0:T(8,128)(2,1)}, u32[]{:S(2)}, u32[]{:S(2)}) collective-permute-start(bf16[4,2,64,2560]{3,2,1,0:T(8,128)(2,1)} %dynamic-slice_bitcast_fusion.1), channel_id=1, source_target_pairs={{0,2},{1,3},{2,0},{3,1},{4,6},{5,7},{6,4},{7,5},{8,10},{9,11},{10,... | collective-permute-start | bytes 7864328 | tf_op jit(solution)/shard_map/ppermute | solution.py:49
  481.0 45.8 %collective-permute-start.27 = (bf16[4,2,64,1536]{3,2,1,0:T(8,128)(2,1)}, bf16[4,2,64,1536]{3,2,1,0:T(8,128)(2,1)S(1)}, u32[]{:S(2)}, u32[]{:S(2)}) collective-permute-start(bf16[4,2,64,1536]{3,2,1,0:T(8,128)(2,1)} %dynamic-slice_bitcast_fusion.5), channel_id=1, source_target_pairs={{0,2},{1,3},{2,0},{3,1},{4,6},{5,7},{6,4},{7,5},{8,10},{9,11},{10,... | collective-permute-start | bytes 4718600 | tf_op jit(solution)/shard_map/ppermute | solution.py:49
  524.1 82.5 %collective-permute-start.26 = (bf16[512,1024]{1,0:T(8,128)(2,1)S(1)}, bf16[512,1024]{1,0:T(8,128)(2,1)S(1)}, u32[]{:S(2)}, u32[]{:S(2)}) collective-permute-start(bf16[512,1024]{1,0:T(8,128)(2,1)S(1)} %fusion.62), channel_id=1, source_target_pairs={{0,1},{1,0},{2,3},{3,2},{4,5},{5,4},{6,7},{7,6},{8,9},{9,8},{10,11... | collective-permute-start | bytes 3145736 | tf_op jit(solution)/shard_map/ppermute | solution.py:49
  526.9 26.2 %collective-permute-start.42 = (bf16[4,64,2048]{2,1,0:T(8,128)(2,1)S(1)}, bf16[4,64,2048]{2,1,0:T(8,128)(2,1)S(1)}, u32[]{:S(2)}, u32[]{:S(2)}) collective-permute-start(bf16[4,64,2048]{2,1,0:T(8,128)(2,1)S(1)} %dynamic-slice_bitcast_fusion.7), channel_id=1, source_target_pairs={{0,4},{1,5},{2,6},{3,7},{4,0},{5,1},{6,2},{7,3},{8,12},{9,13},{10,... | collective-permute-start | bytes 3145736 | tf_op jit(solution)/shard_map/ppermute | solution.py:49
  536.9 35.4 %collective-permute-start.40 = (bf16[4,64,2048]{2,1,0:T(8,128)(2,1)S(1)}, bf16[4,64,2048]{2,1,0:T(8,128)(2,1)S(1)}, u32[]{:S(2)}, u32[]{:S(2)}) collective-permute-start(bf16[4,64,2048]{2,1,0:T(8,128)(2,1)S(1)} %dynamic-slice_bitcast_fusion.8), channel_id=1, source_target_pairs={{0,4},{1,5},{2,6},{3,7},{4,0},{5,1},{6,2},{7,3},{8,12},{9,13},{10,... | collective-permute-start | bytes 3145736 | tf_op jit(solution)/shard_map/ppermute | solution.py:49
  548.6 53.7 %collective-permute-start.34 = (bf16[4,2,64,2560]{3,2,1,0:T(8,128)(2,1)S(1)}, bf16[4,2,64,2560]{3,2,1,0:T(8,128)(2,1)S(1)}, u32[]{:S(2)}, u32[]{:S(2)}) collective-permute-start(bf16[4,2,64,2560]{3,2,1,0:T(8,128)(2,1)S(1)} %bitcast_add_fusion.2), channel_id=1, source_target_pairs={{0,1},{1,0},{2,3},{3,2},{4,5},{5,4},{6,7},{7,6},{8,9},{9,8},{10,11... | collective-permute-start | bytes 7864328 | tf_op jit(solution)/shard_map/ppermute | solution.py:49
  553.0 19.5 %collective-permute-start.30 = (bf16[2,64,1536]{2,1,0:T(8,128)(2,1)S(1)}, bf16[2,64,1536]{2,1,0:T(8,128)(2,1)S(1)}, u32[]{:S(2)}, u32[]{:S(2)}) collective-permute-start(bf16[2,64,1536]{2,1,0:T(8,128)(2,1)S(1)} %bitcast_add_fusion.11), channel_id=1, source_target_pairs={{0,8},{1,9},{2,10},{3,11},{4,12},{5,13},{6,14},{7,15},{8,16},{9,17... | collective-permute-start | bytes 1179656 | tf_op jit(solution)/shard_map/ppermute | solution.py:49
  572.7 36.8 %collective-permute-start.31 = (bf16[64,1536]{1,0:T(8,128)(2,1)S(1)}, bf16[64,1536]{1,0:T(8,128)(2,1)S(1)}, u32[]{:S(2)}, u32[]{:S(2)}) collective-permute-start(bf16[64,1536]{1,0:T(8,128)(2,1)S(1)} %dynamic-slice_bitcast_fusion.12), channel_id=1, source_target_pairs={{0,4},{1,5},{2,6},{3,7},{4,0},{5,1},{6,2},{7,3},{8,12},{9,13},{10,... | collective-permute-start | bytes 589832 | tf_op jit(solution)/shard_map/ppermute | solution.py:49
  583.9 26.8 %collective-permute-start.44 = (bf16[2,64,2048]{2,1,0:T(8,128)(2,1)S(1)}, bf16[2,64,2048]{2,1,0:T(8,128)(2,1)}, u32[]{:S(2)}, u32[]{:S(2)}) collective-permute-start(bf16[2,64,2048]{2,1,0:T(8,128)(2,1)S(1)} %fusion.91), channel_id=1, source_target_pairs={{0,8},{1,9},{2,10},{3,11},{4,12},{5,13},{6,14},{7,15},{8,16},{9,17... | collective-permute-start | bytes 1572872 | tf_op jit(solution)/shard_map/ppermute | solution.py:49
  606.0 25.1 %collective-permute-start.35 = (bf16[4,64,2560]{2,1,0:T(8,128)(2,1)}, bf16[4,64,2560]{2,1,0:T(8,128)(2,1)}, u32[]{:S(2)}, u32[]{:S(2)}) collective-permute-start(bf16[4,64,2560]{2,1,0:T(8,128)(2,1)} %dynamic-slice_bitcast_fusion.6), channel_id=1, source_target_pairs={{0,4},{1,5},{2,6},{3,7},{4,0},{5,1},{6,2},{7,3},{8,12},{9,13},{10,... | collective-permute-start | bytes 3932168 | tf_op jit(solution)/shard_map/ppermute | solution.py:49
  611.8 26.0 %collective-permute-start.45 = (bf16[2,64,2048]{2,1,0:T(8,128)(2,1)S(1)}, bf16[2,64,2048]{2,1,0:T(8,128)(2,1)S(1)}, u32[]{:S(2)}, u32[]{:S(2)}) collective-permute-start(bf16[2,64,2048]{2,1,0:T(8,128)(2,1)S(1)} %fusion.94), channel_id=1, source_target_pairs={{0,8},{1,9},{2,10},{3,11},{4,12},{5,13},{6,14},{7,15},{8,16},{9,17... | collective-permute-start | bytes 1572872 | tf_op jit(solution)/shard_map/ppermute | solution.py:49
  (101 other events, 962.0 us)

commit v2 on v1

v2 whole, which is shorter than its diff:
```python
import jax
import jax.numpy as jnp
from jax import lax
from jax.experimental import pallas as pl
from jax.experimental.pallas import tpu as pltpu
from jax.sharding import PartitionSpec as P

HEAD_DIM = 64
TILE = 256
PAIR = 2 * HEAD_DIM
EPS = 1e-05
BIG_NEGATIVE = -1e30
ALL = ("dp", "tensor")
Z, X, C, Y = range(4)
F32 = jnp.float32
BF16 = jnp.bfloat16


def digit_sizes():
    rest = lax.axis_size("dp")
    core = 2 if rest % 2 == 0 else 1
    rest //= core
    across = 2 if rest % 2 == 0 else 1
    rest //= across
    return (rest, across, core, lax.axis_size("tensor"))


def my_digits(sizes):
    dp = lax.axis_index("dp")
    return (
        dp // (sizes[X] * sizes[C]),
        dp // sizes[C] % sizes[X],
        dp % sizes[C],
        lax.axis_index("tensor"),
    )


def hop(value, sizes, digit, step=1):
    pairs = []
    nz, nx, nc, ny = sizes
    for z in range(nz):
        for x in range(nx):
            for c in range(nc):
                for y in range(ny):
                    there = [z, x, c, y]
                    there[digit] = (there[digit] + step) % sizes[digit]
                    source = ((z * nx + x) * nc + c) * ny + y
                    target = ((there[0] * nx + there[1]) * nc + there[2]) * ny + there[3]
                    pairs.append((source, target))
    return lax.ppermute(value, ALL, pairs)


def ring(value, sizes, digit):
    pieces = [value]
    for _ in range(sizes[digit] - 1):
        pieces.append(hop(pieces[-1], sizes, digit))
    return pieces


def place(pieces, index, axis):
    count = len(pieces)
    if count == 1:
        return jnp.expand_dims(pieces[0], axis)
    shape = list(pieces[0].shape)
    shape.insert(axis, count)
    out = jnp.zeros(shape, pieces[0].dtype)
    for k, piece in enumerate(pieces):
        out = lax.dynamic_update_index_in_dim(out, piece, (index - k) % count, axis)
    return out


def pick(value, index, axis):
    return lax.dynamic_index_in_dim(value, index, axis, keepdims=False)


def ring_sum(value, sizes, digit, index, axis):
    count = sizes[digit]
    if count == 1:
        return jnp.squeeze(value, axis)
    moving = pick(value, (index - 1) % count, axis)
    for k in range(1, count):
        moving = hop(moving, sizes, digit) + pick(value, (index - 1 - k) % count, axis)
    return moving


def after(value, *others):
    return lax.optimization_barrier((value, *others))[0]


def all_sum(value, sizes, digits):
    for digit in digits:
        value = sum(ring(value, sizes, digit))
    return value


def put(out, piece, x, c, begin):
    zero = jnp.int32(0)
    return lax.dynamic_update_slice(
        out, piece[:, None, None], (zero, x.astype(jnp.int32), c.astype(jnp.int32), zero, jnp.int32(begin))
    )


def gather_project(shard, sizes, at):
    half = shard.shape[1] // 2
    first = ring(shard[:, :half], sizes, X)
    second = place(ring(shard[:, half:], sizes, Z), at[Z], 0)
    first = place(ring(place(first, at[X], 0), sizes, Z), at[Z], 0)
    second = place(ring(second, sizes, X), at[X], 1)
    both = jnp.concatenate([first, second], axis=-1)
    full = place(ring(both, sizes, C), at[C], 2)
    return full.reshape(-1, shard.shape[1]), first


def spread(halves, sizes):
    if sizes[X] == 2 and sizes[Y] == 2:
        over_x = [hop(b, sizes, X) for b in halves]
        over_y = [hop(b, sizes, Y) for b in halves]
        corner = [hop(over_x[0], sizes, Y), hop(over_y[1], sizes, X)]
        return [[halves, over_x], [over_y, corner]]
    over_x = list(zip(*[ring(b, sizes, X) for b in halves]))
    both = [list(zip(*[ring(b, sizes, Y) for b in piece])) for piece in over_x]
    return [[both[j][k] for j in range(sizes[X])] for k in range(sizes[Y])]


def gather_halves(shard, sizes, at):
    deep = place(ring(shard, sizes, Z), at[Z], 0)
    half = shard.shape[1] // 2
    return spread([deep[..., :half], deep[..., half:]], sizes), deep


def assemble(pieces, sizes, at, widths):
    out = []
    for by_x in pieces:
        begins = [0]
        for width in widths:
            begins.append(begins[-1] + width)
        nz, depth, half = by_x[0][0].shape
        mats = [jnp.zeros((nz, sizes[X], sizes[C], depth, width), BF16) for width in widths]
        for j, halves in enumerate(by_x):
            for h, piece in enumerate(halves):
                for c, part in enumerate(ring(piece, sizes, C)):
                    x_at, c_at = (at[X] - j) % sizes[X], (at[C] - c) % sizes[C]
                    for m, width in enumerate(widths):
                        low = max(begins[m], h * half)
                        high = min(begins[m + 1], (h + 1) * half)
                        if low < high:
                            cut = part[..., low - h * half : high - h * half]
                            mats[m] = put(mats[m], cut, x_at, c_at, low - begins[m])
        out.append([m.reshape(-1, m.shape[-1]) for m in mats])
    return out


def core_part(fulls, sizes, core):
    return jnp.concatenate(
        [
            pick(f.reshape(sizes[Z], sizes[X], sizes[C], -1, f.shape[-1]), core, 2)
            for f in fulls
        ],
        axis=-1,
    )


def core_sum(fulls, sizes, at):
    if sizes[C] == 1:
        return core_part(fulls, sizes, at[C])
    sent = hop(core_part(fulls, sizes, (at[C] + 1) % sizes[C]), sizes, C)
    return sent + core_part(fulls, sizes, at[C])


def corner_step(parts, sizes, at):
    far_x = (at[X] + 1) % 2
    half = parts[0].shape[-1] // 2
    cut = lambda p, h: p[..., h * half : (h + 1) * half]
    own, over_x = pick(parts[0], at[X], 1), pick(parts[0], far_x, 1)
    over_y, corner = pick(parts[1], at[X], 1), pick(parts[1], far_x, 1)
    from_x = hop(cut(corner, 0), sizes, X)
    from_y = hop(cut(corner, 1), sizes, Y)
    first = hop(cut(over_x, 0), sizes, X)
    return (own, first, over_x, over_y, from_x, from_y)


def side_step(held, sizes, wait):
    own, first, over_x, over_y, from_x, from_y = held
    half = own.shape[-1] // 2
    cut = lambda p, h: p[..., h * half : (h + 1) * half]
    second = hop(cut(over_x, 1) + from_y, sizes, X)
    send = after(jnp.concatenate([cut(over_y, 0) + from_x, cut(over_y, 1)], axis=-1), *wait)
    side = hop(send, sizes, Y)
    return own + jnp.concatenate([first, second], axis=-1) + side


def plain_square(parts, sizes, at):
    total = parts[0]
    for k in range(1, sizes[Y]):
        total = total + hop(parts[k], sizes, Y, -k)
    return ring_sum(total, sizes, X, at[X], 1)


def z_steps(value, sizes, at):
    return pick(value, (at[Z] - 1) % sizes[Z], 0)


def z_next(value, moving, k, sizes, at):
    return hop(moving, sizes, Z) + pick(value, (at[Z] - 1 - k) % sizes[Z], 0)


def norm_parts(rows):
    average = jnp.mean(rows, axis=-1, keepdims=True)
    centered = rows - average
    scale = lax.rsqrt(jnp.mean(centered * centered, axis=-1, keepdims=True) + EPS)
    return centered * scale, scale


def norm_back(grad, unit, scale, gain):
    inner = grad * gain
    return scale * (
        inner
        - jnp.mean(inner, axis=-1, keepdims=True)
        - unit * jnp.mean(inner * unit, axis=-1, keepdims=True)
    )


def gelu_both(upper):
    below = 0.5 * lax.erfc(upper * -(0.5**0.5))
    density = jnp.exp(-0.5 * upper * upper) * 0.3989422804014327
    return upper * below, below + upper * density


def dot(a, b, dims):
    return lax.dot_general(a, b, (dims, ((), ())), preferred_element_type=F32)


NN = ((1,), (0,))
NT = ((1,), (1,))
TN = ((0,), (0,))


def mm(a, b):
    return jnp.dot(a, b, preferred_element_type=F32)


def turn(block):
    return block.astype(F32).T.astype(BF16)


def half_of(block, head, axis):
    return jnp.where(
        lax.broadcasted_iota(jnp.int32, block.shape, axis) // HEAD_DIM == head, block, 0
    ).astype(block.dtype)


def set_bias(down_ref, along_ref, bias_ref):
    @pl.when(pl.program_id(0) == 0)
    def _():
        bias_ref[...] = jnp.where(down_ref[...] == along_ref[...], 0.0, BIG_NEGATIVE)


def attend_kernel(q_ref, k_ref, v_ref, down_ref, along_ref, low_ref, full_ref, log_ref, bias_ref):
    set_bias(down_ref, along_ref, bias_ref)
    rows = q_ref.shape[0]
    tile = min(TILE, rows)
    turned = turn(q_ref[...].astype(F32) * HEAD_DIM ** (-0.5))
    keys = [half_of(k_ref[...], i, 1) for i in range(2)]
    values = [half_of(v_ref[...], i, 1) for i in range(2)]
    for begin in range(0, rows, tile):
        cols = slice(begin, begin + tile)
        mixed = jnp.zeros((tile, PAIR), F32)
        for i in range(2):
            scores = mm(keys[i], turned[:, cols]) + bias_ref[:, cols]
            top = jnp.max(scores, axis=0, keepdims=True)
            weights = jnp.exp(scores - top)
            total = jnp.sum(weights, axis=0, keepdims=True)
            log_ref[0, i : i + 1, cols] = top + jnp.log(total)
            mixed += dot((weights * (1.0 / total)).astype(BF16), values[i], TN)
        full_ref[cols, :] = mixed
        low_ref[cols, :] = mixed.astype(BF16)


def attend_back_kernel(
    q_ref, k_ref, v_ref, down_ref, along_ref, full_ref, log_ref, grad_ref, out_ref, bias_ref
):
    set_bias(down_ref, along_ref, bias_ref)
    rows = q_ref.shape[0]
    tile = min(TILE, rows)
    query = (q_ref[...].astype(F32) * HEAD_DIM ** (-0.5)).astype(BF16)
    grad = grad_ref[...]
    turned, grad_turned, key_turned = turn(query), turn(grad), turn(k_ref[...])
    inner = (grad.astype(F32) * full_ref[...]).T
    key_grad = jnp.zeros((rows, PAIR), F32)
    value_grad = jnp.zeros((rows, PAIR), F32)
    query_grad = [jnp.zeros((PAIR, tile), F32) for _ in range(rows // tile)]
    for i in range(2):
        key, value = half_of(k_ref[...], i, 1), half_of(v_ref[...], i, 1)
        kept_query, kept_grad = half_of(query, i, 1), half_of(grad, i, 1)
        kept_key = half_of(key_turned, i, 0)
        delta = jnp.sum(inner[i * HEAD_DIM : (i + 1) * HEAD_DIM], axis=0, keepdims=True)
        for j in range(rows // tile):
            cols = slice(j * tile, (j + 1) * tile)
            scores = mm(key, turned[:, cols]) + bias_ref[:, cols]
            probs = jnp.exp(scores - log_ref[0, i : i + 1, cols])
            prob_grad = mm(value, grad_turned[:, cols])
            score_grad = (probs * (prob_grad - delta[:, cols])).astype(BF16)
            value_grad += mm(probs.astype(BF16), kept_grad[cols])
            key_grad += mm(score_grad, kept_query[cols])
            query_grad[j] += mm(kept_key, score_grad)
    for j in range(rows // tile):
        out_ref[0, j * tile : (j + 1) * tile, :] = (query_grad[j].T * HEAD_DIM ** (-0.5)).astype(
            BF16
        )
    out_ref[1] = key_grad.astype(BF16)
    out_ref[2] = value_grad.astype(BF16)


def third(begin):
    return lambda h: (0, begin + h)


def attention(projected, segment):
    rows, width = projected.shape
    pairs = width // 3 // PAIR
    block = lambda f: pl.BlockSpec((rows, PAIR), f)
    return pl.pallas_call(
        attend_kernel,
        grid=(pairs,),
        in_specs=[block(third(c * pairs)) for c in range(3)]
        + [
            pl.BlockSpec((rows, 1), lambda h: (0, 0)),
            pl.BlockSpec((1, rows), lambda h: (0, 0)),
        ],
        out_specs=[
            block(third(0)),
            block(third(0)),
            pl.BlockSpec((1, 2, rows), lambda h: (h, 0, 0)),
        ],
        out_shape=[
            jax.ShapeDtypeStruct((rows, pairs * PAIR), BF16),
            jax.ShapeDtypeStruct((rows, pairs * PAIR), F32),
            jax.ShapeDtypeStruct((pairs, 2, rows), F32),
        ],
        scratch_shapes=[pltpu.VMEM((rows, rows), F32)],
        compiler_params=pltpu.CompilerParams(vmem_limit_bytes=40 * 2**20),
        cost_estimate=pl.CostEstimate(
            flops=pairs * 16 * rows * rows * PAIR,
            bytes_accessed=16 * rows * pairs * PAIR,
            transcendentals=2 * pairs * rows * rows,
        ),
    )(projected, projected, projected, segment[:, None], segment[None, :])


def attention_back(projected, segment, full, logs, grad, first, count):
    rows, width = projected.shape
    pairs = width // 3 // PAIR
    block = lambda f: pl.BlockSpec((rows, PAIR), f)
    return pl.pallas_call(
        attend_back_kernel,
        grid=(count,),
        in_specs=[block(third(c * pairs + first)) for c in range(3)]
        + [
            pl.BlockSpec((rows, 1), lambda h: (0, 0)),
            pl.BlockSpec((1, rows), lambda h: (0, 0)),
            block(third(first)),
            pl.BlockSpec((1, 2, rows), lambda h: (first + h, 0, 0)),
            block(third(first)),
        ],
        out_specs=pl.BlockSpec((3, rows, PAIR), lambda h: (0, 0, h)),
        out_shape=jax.ShapeDtypeStruct((3, rows, count * PAIR), BF16),
        scratch_shapes=[pltpu.VMEM((rows, rows), F32)],
        compiler_params=pltpu.CompilerParams(vmem_limit_bytes=48 * 2**20),
        cost_estimate=pl.CostEstimate(
            flops=count * 40 * rows * rows * PAIR,
            bytes_accessed=20 * rows * count * PAIR,
            transcendentals=2 * count * rows * rows,
        ),
    )(projected, projected, projected, segment[:, None], segment[None, :], full, logs, grad)


def on_device(
    tokens,
    lengths,
    project_weight,
    project_bias,
    output_weight,
    output_bias,
    first_gain,
    first_shift,
    expand_weight,
    expand_bias,
    shrink_weight,
    shrink_bias,
    second_gain,
    second_shift,
    cotangent,
):
    sizes = digit_sizes()
    at = my_digits(sizes)
    n_t = sizes[Y]
    mine = at[Y]
    rows, width = tokens.shape
    all_rows = rows * n_t
    heads_width = project_weight.shape[2]
    hidden = expand_weight.shape[1]
    depth = project_weight.shape[1]
    pairs = heads_width // PAIR
    square = sizes[X] == 2 and n_t == 2

    ends = jnp.cumsum(lengths[0], dtype=jnp.int32)
    positions = lax.iota(jnp.int32, all_rows)
    segment = jnp.sum(
        (positions[:, None] >= ends[None, :]).astype(jnp.int32), axis=1, dtype=jnp.int32
    )
    valid = (mine * rows + lax.iota(jnp.int32, rows) < ends[-1])[:, None]

    whole_tokens = place(ring(tokens, sizes, Y), mine, 0).reshape(all_rows, width)
    proj, early = gather_project(
        jnp.transpose(project_weight, (1, 0, 2)).reshape(depth, 3 * heads_width), sizes, at
    )
    upper_shard = jnp.concatenate([output_weight.T, expand_weight], axis=1)
    upper_pieces, deep = gather_halves(after(upper_shard, early), sizes, at)
    shrink_pieces, _ = gather_halves(after(shrink_weight.T, deep), sizes, at)
    expand_biases = ring(expand_bias, sizes, Y)

    bias = jnp.concatenate([project_bias[0], jnp.zeros_like(project_bias[0]), project_bias[1]])
    projected = (dot(whole_tokens, proj, NN) + bias).astype(BF16)
    mixed_low, mixed_full, logs = attention(projected, segment)
    by_rows = mixed_low.reshape(n_t, rows, heads_width)
    mixed = [pick(by_rows, mine, 0)]
    for k in range(1, n_t):
        mixed.append(hop(pick(by_rows, (mine + k) % n_t, 0), sizes, Y, k))

    gathered = assemble(upper_pieces, sizes, at, (heads_width, hidden))
    mix = [g[0] for g in gathered]
    expand = [g[1] for g in gathered]
    attn = sum(dot(m, w, NT) for m, w in zip(mixed, mix)) + output_bias
    unit1, scale1 = norm_parts(tokens.astype(F32) + attn)
    normed1 = unit1 * first_gain + first_shift
    low1 = normed1.astype(BF16)
    active, slope = [], []
    for w, b in zip(expand, expand_biases):
        act, der = gelu_both(dot(low1, w, NN) + b)
        active.append(act.astype(BF16))
        slope.append(der.astype(BF16))
    shrink = [g[0] for g in assemble(shrink_pieces, sizes, at, (hidden,))]
    branch = sum(dot(a, w, NT) for a, w in zip(active, shrink)) + shrink_bias
    unit2, scale2 = norm_parts(normed1 + branch)
    layer_output = jnp.where(valid, unit2 * second_gain + second_shift, 0.0).astype(BF16)

    grad = jnp.where(valid, cotangent.astype(F32), 0.0)
    grad_second_gain = jnp.sum(grad * unit2, axis=0)
    grad_second_shift = jnp.sum(grad, axis=0)
    grad_r2 = norm_back(grad, unit2, scale2, second_gain)
    grad_branch = grad_r2.astype(BF16)
    grad_shrink_bias = jnp.sum(grad_branch, axis=0, dtype=F32)
    shrink_parts = [core_sum([dot(grad_branch, a, TN).astype(BF16)], sizes, at) for a in active]
    grad_upper = [
        (dot(grad_branch, w, NN) * s.astype(F32)).astype(BF16) for w, s in zip(shrink, slope)
    ]
    grad_expand_biases = [jnp.sum(g, axis=0, dtype=F32) for g in grad_upper]
    if square:
        shrink_held = corner_step(shrink_parts, sizes, at)
    low1_later = after(low1, *shrink_parts)
    grad_expand = [dot(low1_later, g, TN).astype(BF16) for g in grad_upper]
    expand_parts = [core_sum([g], sizes, at) for g in grad_expand]
    grad_normed1 = sum(dot(g, w, NT) for g, w in zip(grad_upper, expand)) + grad_r2
    if square:
        grad_normed1 = after(grad_normed1, *shrink_held)
    grad_first_gain = jnp.sum(grad_normed1 * unit1, axis=0)
    grad_first_shift = jnp.sum(grad_normed1, axis=0)
    grad_r1 = norm_back(grad_normed1, unit1, scale1, first_gain)
    grad_attn = grad_r1.astype(BF16)
    grad_output_bias = jnp.sum(grad_attn, axis=0, dtype=F32)

    grad_pieces = []
    for k, w in enumerate(mix):
        part = dot(grad_attn, w, NN).astype(BF16)
        grad_pieces.append(hop(part, sizes, Y, -k) if k else part)
    grad_rows = place([grad_pieces[-k % n_t] for k in range(n_t)], mine, 0)
    grad_rows = grad_rows.reshape(all_rows, heads_width)
    grad_mix = [dot(grad_attn, m, TN).astype(BF16) for m in mixed]
    upper_parts = [
        jnp.concatenate([core_sum([a], sizes, at), b], axis=-1)
        for a, b in zip(grad_mix, expand_parts)
    ]
    calls = 2 if pairs % 2 == 0 else 1
    if square:
        upper_held = corner_step(upper_parts, sizes, at)
        shrink_sum = side_step(shrink_held, sizes, (grad_rows,))
        grad_rows = after(grad_rows, *upper_parts)
    else:
        shrink_sum = plain_square(shrink_parts, sizes, at)
        upper_sum = plain_square(upper_parts, sizes, at)
    done = [
        attention_back(
            projected, segment, mixed_full, logs, grad_rows, 0, pairs // calls
        )
    ]
    if square:
        upper_sum = side_step(upper_held, sizes, (done[0],))
        logs = after(logs, done[0], *upper_held)
    if calls == 2:
        done.append(
            attention_back(
                projected, segment, mixed_full, logs, grad_rows, pairs // 2, pairs // 2
            )
        )
    projected_grad = jnp.concatenate(done, axis=-1)
    moving = z_steps(shrink_sum, sizes, at)
    if sizes[Z] > 1:
        moving = z_next(shrink_sum, moving, 1, sizes, at)
        projected_grad = after(projected_grad, shrink_sum)

    project_parts = [
        dot(whole_tokens, projected_grad[c], TN).astype(BF16) for c in range(3)
    ]
    bias_sums = jnp.stack(
        [jnp.sum(projected_grad[c], axis=0, dtype=F32) for c in (0, 2)]
    )
    project_sum = core_sum(project_parts, sizes, at)
    cut = 3 * heads_width // 2
    first_half = ring_sum(project_sum[..., :cut], sizes, X, at[X], 1)
    second_half = ring_sum(project_sum[..., cut:], sizes, Z, at[Z], 0)
    first_half = ring_sum(first_half, sizes, Z, at[Z], 0)
    second_half = ring_sum(second_half, sizes, X, at[X], 0)
    grad_project = jnp.concatenate([first_half, second_half], axis=-1)
    grad_project_weight = jnp.transpose(
        grad_project.reshape(depth, 3, heads_width), (1, 0, 2)
    ).astype(F32)
    grad_project_bias = all_sum(bias_sums, sizes, (C, X, Z))

    for k in range(2, sizes[Z]):
        moving = z_next(shrink_sum, moving, k, sizes, at)
    grad_shrink_weight = moving.astype(F32).T
    owned = ring_sum(upper_sum, sizes, Z, at[Z], 0).astype(F32)
    grad_output_weight = owned[:, :heads_width].T
    grad_expand_weight = owned[:, heads_width:]

    packed = jnp.concatenate(
        [
            grad_second_gain,
            grad_second_shift,
            grad_shrink_bias,
            grad_first_gain,
            grad_first_shift,
            grad_output_bias,
            place(grad_expand_biases, mine, 0).reshape(-1),
        ]
    )
    packed = all_sum(packed, sizes, (C, X, Y, Z))
    (
        grad_second_gain,
        grad_second_shift,
        grad_shrink_bias,
        grad_first_gain,
        grad_first_shift,
        grad_output_bias,
    ) = (packed[i * width : (i + 1) * width] for i in range(6))
    grad_expand_bias = pick(packed[6 * width :].reshape(n_t, hidden), mine, 0)

    proj_cube = proj.reshape(width, 3, heads_width)
    token_grad = grad_r1
    for k in range(n_t):
        begin = (mine + k) % n_t * rows
        part = lax.dot_general(
            lax.dynamic_slice_in_dim(projected_grad, begin, rows, 1),
            proj_cube,
            (((0, 2), (1, 2)), ((), ())),
            preferred_element_type=F32,
        )
        if k:
            part = hop(part.astype(BF16), sizes, Y, k).astype(F32)
        token_grad = token_grad + part
    grad_tokens = token_grad.astype(BF16)
    return (
        layer_output,
        grad_tokens,
        grad_project_weight,
        grad_project_bias,
        grad_output_weight,
        grad_output_bias,
        grad_first_gain,
        grad_first_shift,
        grad_expand_weight,
        grad_expand_bias,
        grad_shrink_weight,
        grad_shrink_bias,
        grad_second_gain,
        grad_second_shift,
    )


def solution(mesh):
    rows = P(("dp", "tensor"), None)
    weights = (P(None, "dp", "tensor"), P("tensor", "dp"), P("dp", "tensor"), P("tensor", "dp"))
    in_specs = (
        rows,
        P("dp", None),
        weights[0],
        P(None, "tensor"),
        weights[1],
        P(),
        P(),
        P(),
        weights[2],
        P("tensor"),
        weights[3],
        P(),
        P(),
        P(),
        rows,
    )
    out_specs = (
        rows,
        rows,
        weights[0],
        P(None, "tensor"),
        weights[1],
        P(),
        P(),
        P(),
        weights[2],
        P("tensor"),
        weights[3],
        P(),
        P(),
        P(),
    )
    return jax.shard_map(
        on_device, mesh=mesh, in_specs=in_specs, out_specs=out_specs, check_vma=False
    )
```

time: 676 us -> 569 us (0.84)
  waiting for transfers between devices: 173 us -> 291 us
  matrix products: 201 us -> 84.3 us
  blocking collectives: 70.4 us -> 0 us
  local copies, waits for them, and re-layouts: 116 us -> 60.2 us
  Pallas kernels: 0 us -> 45.2 us
  other arithmetic: 63.5 us -> 24.1 us
  starting transfers between devices: 34.5 us -> 56.6 us
  loops' own time: 7.06 us -> 0 us
    ppermute x47 -> x90, waiting for transfers between devices: 173 us -> 291 us  [hop(): return lax.ppermute(value, ALL, pairs)]
    dot_general x14 -> x2, matrix products: 106 us -> 4.74 us  [on_device(): lax.dot_general(lax.dynamic_slice_in_dim(projected_grad, begin, rows, 1),...]
    psum x2 -> x0, blocking collectives: 70.4 us -> none  [the longest x1 37.3 us: on_device(): packed = lax.psum(packed, ALL)]
    pallas_call x0 -> x3, Pallas kernels: none -> 45.2 us  [the longest x2 25.4 us: attention_back(): pl.pallas_call(attend_back_kernel, grid=(count,), in_specs=[block(third(c...]
    dynamic_update_slice x51 -> x25, local copies, waits for them, and re-layouts: 35.9 us -> 5.39 us  [place(): out = lax.dynamic_update_index_in_dim(out, piece, (index - k) % count, axis)]
    ppermute x47 -> x90, starting transfers between devices: 34.5 us -> 56.6 us  [hop(): return lax.ppermute(value, ALL, pairs)]
    convert_element_type x5 -> x1, other arithmetic: 20.5 us -> 0.05 us  [on_device(): owned = ring_sum(upper_sum, sizes, Z, at[Z], 0).astype(F32)]
    dot_general x22, matrix products: 95.2 us -> 79.6 us  [dot(): return lax.dot_general(a, b, (dims, ((), ())), preferred_element_type=F32)]
  transfers between devices with their start and end apart: 47 -> 90, of which waited for: 16 -> 44; matrix products, arithmetic and copies ran while one was open for 45% -> 23% of each run, Pallas kernels for 0% -> 6%
where the time goes in v2:
time: 569 us; the launch traced here: 564 us
  waiting for transfers between devices  291 us (51%)
  matrix products  84.3 us (15%)
  local copies, waits for them, and re-layouts  60.2 us (11%)
  starting transfers between devices  56.6 us (10%)
  Pallas kernels  45.2 us (8%)
  other arithmetic  24.1 us (4%)
    ppermute x90, waiting for transfers between devices, hop(): return lax.ppermute(value, ALL, pairs)  291 us
    dot_general x22, matrix products, dot(): return lax.dot_general(a, b, (dims, ((), ())), preferred_element_type=F32)  79.6 us
    ppermute x90, starting transfers between devices, hop(): return lax.ppermute(value, ALL, pairs)  56.6 us
    pallas_call x2, Pallas kernels, attention_back(): pl.pallas_call(attend_back_kernel, grid=(count,), in_specs=[block(third(c...  25.4 us
    pallas_call x1, Pallas kernels, attention(): pl.pallas_call(attend_kernel, grid=(pairs,), in_specs=[block(third(c * pa...  19.8 us
    dynamic_update_slice x40, local copies, waits for them, and re-layouts, put(): lax.dynamic_update_slice(out, piece[:, None, None], (zero, x.astype(jnp.i...  16.2 us
  transfers between devices with their start and end apart: 90, of which 44 were waited for; matrix products, arithmetic and copies ran while one was open for 23% of the time, Pallas kernels for 6%

profile of v2, /device:TPU:0, one launch (start us, length us, event | category | flops | bytes accessed | tf_op | source)
XLA Modules:
  0.0 564.1 jit_solution(2871350049943712371)
XLA Ops:
  17.2 6.4 %collective-permute-done.6 = bf16[64,768]{1,0:T(8,128)(2,1)S(1)} collective-permute-done((bf16[64,768]{1,0:T(8,128)(2,1)S(1)}, bf16[64,768]{1,0:T(8,128)(2,1)S(1)}, u32[]{:S(2)}, u32[]{:S(2)}) %collective-permute-start.6) | collective-permute-done | bytes 98336 | tf_op jit(solution)/shard_map/ppermute | solution.py:50
  23.6 6.4 %collective-permute-done.7 = bf16[64,768]{1,0:T(8,128)(2,1)S(1)} collective-permute-done((bf16[64,768]{1,0:T(8,128)(2,1)S(1)}, bf16[64,768]{1,0:T(8,128)(2,1)S(1)}, u32[]{:S(2)}, u32[]{:S(2)}) %collective-permute-start.7) | collective-permute-done | bytes 98336 | tf_op jit(solution)/shard_map/ppermute | solution.py:50
  30.8 7.5 %collective-permute-done.3 = bf16[2,64,768]{2,1,0:T(8,128)(2,1)S(1)} collective-permute-done((bf16[2,64,768]{2,1,0:T(8,128)(2,1)S(1)}, bf16[2,64,768]{2,1,0:T(8,128)(2,1)S(1)}, u32[]{:S(2)}, u32[]{:S(2)}) %collective-permute-start.3) | collective-permute-done | bytes 196640 | tf_op jit(solution)/shard_map/ppermute | solution.py:50
  38.4 7.4 %collective-permute-done.4 = bf16[2,64,768]{2,1,0:T(8,128)(2,1)S(1)} collective-permute-done((bf16[2,64,768]{2,1,0:T(8,128)(2,1)S(1)}, bf16[2,64,768]{2,1,0:T(8,128)(2,1)S(1)}, u32[]{:S(2)}, u32[]{:S(2)}) %collective-permute-start.4) | collective-permute-done | bytes 196640 | tf_op jit(solution)/shard_map/ppermute | solution.py:50
  46.7 11.2 %collective-permute-done.10 = bf16[64,2560]{1,0:T(8,128)(2,1)S(1)} collective-permute-done((bf16[64,2560]{1,0:T(8,128)(2,1)S(1)}, bf16[64,2560]{1,0:T(8,128)(2,1)S(1)}, u32[]{:S(2)}, u32[]{:S(2)}) %collective-permute-start.10) | collective-permute-done | bytes 327712 | tf_op jit(solution)/shard_map/ppermute | solution.py:50
  60.3 8.7 %collective-permute-done.11 = bf16[64,2560]{1,0:T(8,128)(2,1)S(1)} collective-permute-done((bf16[64,2560]{1,0:T(8,128)(2,1)S(1)}, bf16[64,2560]{1,0:T(8,128)(2,1)S(1)}, u32[]{:S(2)}, u32[]{:S(2)}) %collective-permute-start.11) | collective-permute-done | bytes 327712 | tf_op jit(solution)/shard_map/ppermute | solution.py:50
  69.0 10.1 %collective-permute-done.12 = bf16[64,2560]{1,0:T(8,128)(2,1)S(1)} collective-permute-done((bf16[64,2560]{1,0:T(8,128)(2,1)S(1)}, bf16[64,2560]{1,0:T(8,128)(2,1)S(1)}, u32[]{:S(2)}, u32[]{:S(2)}) %collective-permute-start.12) | collective-permute-done | bytes 327712 | tf_op jit(solution)/shard_map/ppermute | solution.py:50
  85.0 8.0 %collective-permute-done.24 = bf16[64,2048]{1,0:T(8,128)(2,1)S(1)} collective-permute-done((bf16[64,2048]{1,0:T(8,128)(2,1)S(1)}, bf16[64,2048]{1,0:T(8,128)(2,1)S(1)}, u32[]{:S(2)}, u32[]{:S(2)}) %collective-permute-start.24) | collective-permute-done | bytes 262176 | tf_op jit(solution)/shard_map/ppermute | solution.py:50
  93.2 9.7 %collective-permute-done.25 = bf16[64,2048]{1,0:T(8,128)(2,1)S(1)} collective-permute-done((bf16[64,2048]{1,0:T(8,128)(2,1)S(1)}, bf16[64,2048]{1,0:T(8,128)(2,1)S(1)}, u32[]{:S(2)}, u32[]{:S(2)}) %collective-permute-start.25) | collective-permute-done | bytes 262176 | tf_op jit(solution)/shard_map/ppermute | solution.py:50
  103.8 6.4 %add_convert_fusion.q_ref.k_ref.v_ref = bf16[1024,1536]{1,0:T(8,128)(2,1)S(1)} fusion(bf16[1024,1024]{1,0:T(8,128)(2,1)} %bitcast.4, bf16[1024,1536]{1,0:T(8,128)(2,1)S(1)} %bitcast.464, f32[1536]{0:T(1024)S(1)} %pad_maximum_fusion.8), kind=kOutput, calls=%fused_computation.4 | convolution fusion | flops 3224371200 | bytes 8394752 | tf_op jit(solution)/shard_map/dot_general | solution.py:230
  110.2 19.8 %shard_map.254 = (bf16[1024,512]{1,0:T(8,128)(2,1)S(1)}, f32[1024,512]{1,0:T(8,128)S(1)}, f32[4,2,1024]{2,1,0:T(2,128)S(1)}) custom-call(bf16[1024,1536]{1,0:T(8,128)(2,1)S(1)} %add_convert_fusion.q_ref.k_ref.v_ref, bf16[1024,1536]{1,0:T(8,128)(2,1)S(1)} %add_convert_fusion.q_ref.k_ref.v_ref, bf16[1024,1536]{1,0:T(8,128)(2,1)S(1)} %add_convert_fusion.q_ref.k_ref.v_ref, ...), custom_call_target="tpu_custom_call" | custom-call | flops 8589934592 | bytes 8388608 | tf_op jit(solution)/shard_map/pallas_call | solution.py:322
  132.9 10.1 %reshape_reshape.3 = bf16[1024,3,512]{2,1,0:T(4,128)(2,1)} reshape(bf16[4,2,2,64,1536]{4,3,2,1,0:T(8,128)(2,1)} %copy-done.12) | data formatting | bytes 6291456 | tf_op jit(solution)/shard_map/reshape;reshape | solution.py:558
  165.2 12.9 %collective-permute-done.19 = bf16[4,64,1280]{2,1,0:T(8,128)(2,1)S(1)} collective-permute-done((bf16[4,64,1280]{2,1,0:T(8,128)(2,1)}, bf16[4,64,1280]{2,1,0:T(8,128)(2,1)S(1)}, u32[]{:S(2)}, u32[]{:S(2)}) %collective-permute-start.19) | collective-permute-done | bytes 655392 | tf_op jit(solution)/shard_map/ppermute | solution.py:50
  182.6 8.0 %collective-permute-done.29 = bf16[4,64,1024]{2,1,0:T(8,128)(2,1)S(1)} collective-permute-done((bf16[4,64,1024]{2,1,0:T(8,128)(2,1)S(1)}, bf16[4,64,1024]{2,1,0:T(8,128)(2,1)S(1)}, u32[]{:S(2)}, u32[]{:S(2)}) %collective-permute-start.29) | collective-permute-done | bytes 524320 | tf_op jit(solution)/shard_map/ppermute | solution.py:50
  192.6 8.9 %collective-permute-done.31 = bf16[4,64,1024]{2,1,0:T(8,128)(2,1)S(1)} collective-permute-done((bf16[4,64,1024]{2,1,0:T(8,128)(2,1)S(1)}, bf16[4,64,1024]{2,1,0:T(8,128)(2,1)S(1)}, u32[]{:S(2)}, u32[]{:S(2)}) %collective-permute-start.31) | collective-permute-done | bytes 524320 | tf_op jit(solution)/shard_map/ppermute | solution.py:50
  208.2 8.8 %collective-permute-done.42 = bf16[4,64,1024]{2,1,0:T(8,128)(2,1)S(1)} collective-permute-done((bf16[4,64,1024]{2,1,0:T(8,128)(2,1)S(1)}, bf16[4,64,1024]{2,1,0:T(8,128)(2,1)S(1)}, u32[]{:S(2)}, u32[]{:S(2)}) %collective-permute-start.42) | collective-permute-done | bytes 524320 | tf_op jit(solution)/shard_map/ppermute | solution.py:50
  218.9 8.5 %collective-permute-done.16 = bf16[512,512]{1,0:T(8,128)(2,1)S(1)} collective-permute-done((bf16[512,512]{1,0:T(8,128)(2,1)S(1)}, bf16[512,512]{1,0:T(8,128)(2,1)S(1)}, u32[]{:S(2)}, u32[]{:S(2)}) %collective-permute-start.16) | collective-permute-done | bytes 524320 | tf_op jit(solution)/shard_map/ppermute | solution.py:50
  231.1 12.4 %multiply_convert_fusion.3 = (bf16[512,2048]{1,0:T(8,128)(2,1)S(1)}, f32[512,2048]{1,0:T(8,128)S(1)}, f32[512,2048]{1,0:T(8,128)S(1)}) fusion(f32[2048]{0:T(1024)S(1)} %copy-done.53, bf16[512,1024]{1,0:T(8,128)(2,1)S(1)} %fusion.35, bf16[1024,2048]{1,0:T(8,128)(2,1)S(1)} %bitcast.475), kind=kOutput, calls=%fused_computation.36 | convolution fusion | flops 2215641088 | bytes 15736832 | tf_op jit(solution)/shard_map/dot_general | solution.py:230
  243.8 12.7 %multiply_convert_fusion.2 = (bf16[512,2048]{1,0:T(8,128)(2,1)S(1)}, f32[512,2048]{1,0:T(8,128)}, f32[512,2048]{1,0:T(8,128)}) fusion(f32[2048]{0:T(1024)S(1)} %collective-permute-done.37, bf16[512,1024]{1,0:T(8,128)(2,1)S(1)} %fusion.35, bf16[1024,2048]{1,0:T(8,128)(2,1)S(1)} %bitcast.477), kind=kOutput, calls=%fused_computation.23 | convolution fusion | flops 2215641088 | bytes 15736832 | tf_op jit(solution)/shard_map/dot_general | solution.py:230
  308.4 7.3 %collective-permute-done.50 = bf16[4,64,1024]{2,1,0:T(8,128)(2,1)S(1)} collective-permute-done((bf16[4,64,1024]{2,1,0:T(8,128)(2,1)S(1)}, bf16[4,64,1024]{2,1,0:T(8,128)(2,1)S(1)}, u32[]{:S(2)}, u32[]{:S(2)}) %collective-permute-start.50) | collective-permute-done | bytes 524320 | tf_op jit(solution)/shard_map/ppermute | solution.py:50
  319.0 11.7 %collective-permute-done.47 = bf16[4,64,1024]{2,1,0:T(8,128)(2,1)S(1)} collective-permute-done((bf16[4,64,1024]{2,1,0:T(8,128)(2,1)S(1)}, bf16[4,64,1024]{2,1,0:T(8,128)(2,1)S(1)}, u32[]{:S(2)}, u32[]{:S(2)}) %collective-permute-start.47) | collective-permute-done | bytes 524320 | tf_op jit(solution)/shard_map/ppermute | solution.py:50
  342.5 12.1 %collective-permute-done.83 = f32[10240]{0:T(1024)S(1)} collective-permute-done((f32[10240]{0:T(1024)S(1)}, f32[10240]{0:T(1024)S(1)}, u32[]{:S(2)}, u32[]{:S(2)}) %collective-permute-start.83) | collective-permute-done | bytes 40992 | tf_op jit(solution)/shard_map/ppermute | solution.py:50
  376.0 12.8 %shard_map.255 = bf16[3,1024,256]{2,1,0:T(8,128)(2,1)S(1)} custom-call(bf16[1024,1536]{1,0:T(8,128)(2,1)} %copy-done.4, bf16[1024,1536]{1,0:T(8,128)(2,1)} %copy-done.4, bf16[1024,1536]{1,0:T(8,128)(2,1)} %copy-done.4, s32[1024,1]{1,0:T(8,128)S(1)} %copy-done.1, s32[1,1024]{1,0:T(1,128)S(1)} %bitcast.462, f32[1024,512]{1,0:T(8,128)S(1)} %copy-done.6, ...), custom_call_target="tpu_custom_call" | custom-call | flops 10737418240 | bytes 5242880 | tf_op jit(solution)/shard_map/pallas_call | solution.py:354
  395.8 19.1 %collective-permute-done.60 = bf16[4,64,2048]{2,1,0:T(8,128)(2,1)S(1)} collective-permute-done((bf16[4,64,2048]{2,1,0:T(8,128)(2,1)S(1)}, bf16[4,64,2048]{2,1,0:T(8,128)(2,1)S(1)}, u32[]{:S(2)}, u32[]{:S(2)}) %collective-permute-start.60) | collective-permute-done | bytes 1048608 | tf_op jit(solution)/shard_map/ppermute | solution.py:50
  416.7 8.1 %collective-permute-done.87 = bf16[64,2048]{1,0:T(8,128)(2,1)S(1)} collective-permute-done((bf16[64,2048]{1,0:T(8,128)(2,1)S(1)}, bf16[64,2048]{1,0:T(8,128)(2,1)S(1)}, u32[]{:S(2)}, u32[]{:S(2)}) %collective-permute-start.87) | collective-permute-done | bytes 262176 | tf_op jit(solution)/shard_map/ppermute | solution.py:50
  425.6 7.5 %collective-permute-done.88 = bf16[64,2048]{1,0:T(8,128)(2,1)S(1)} collective-permute-done((bf16[64,2048]{1,0:T(8,128)(2,1)S(1)}, bf16[64,2048]{1,0:T(8,128)(2,1)S(1)}, u32[]{:S(2)}, u32[]{:S(2)}) %collective-permute-start.88) | collective-permute-done | bytes 262176 | tf_op jit(solution)/shard_map/ppermute | solution.py:50
  442.4 8.9 %collective-permute-done.76 = bf16[4,64,1280]{2,1,0:T(8,128)(2,1)S(1)} collective-permute-done((bf16[4,64,1280]{2,1,0:T(8,128)(2,1)S(1)}, bf16[4,64,1280]{2,1,0:T(8,128)(2,1)S(1)}, u32[]{:S(2)}, u32[]{:S(2)}) %collective-permute-start.76) | collective-permute-done | bytes 655392 | tf_op jit(solution)/shard_map/ppermute | solution.py:50
  451.2 9.2 %collective-permute-done.56 = bf16[4,64,1280]{2,1,0:T(8,128)(2,1)S(1)} collective-permute-done((bf16[4,64,1280]{2,1,0:T(8,128)(2,1)S(1)}, bf16[4,64,1280]{2,1,0:T(8,128)(2,1)S(1)}, u32[]{:S(2)}, u32[]{:S(2)}) %collective-permute-start.56) | collective-permute-done | bytes 655392 | tf_op jit(solution)/shard_map/ppermute | solution.py:50
  460.9 12.6 %shard_map.256 = bf16[3,1024,256]{2,1,0:T(8,128)(2,1)S(1)} custom-call(bf16[1024,1536]{1,0:T(8,128)(2,1)} %copy-done.4, bf16[1024,1536]{1,0:T(8,128)(2,1)} %copy-done.4, bf16[1024,1536]{1,0:T(8,128)(2,1)} %copy-done.4, s32[1024,1]{1,0:T(8,128)S(1)} %copy-done.1, s32[1,1024]{1,0:T(1,128)S(1)} %bitcast.463, f32[1024,512]{1,0:T(8,128)S(1)} %copy-done.7, ...), custom_call_target="tpu_custom_call" | custom-call | flops 10737418240 | bytes 5242880 | tf_op jit(solution)/shard_map/pallas_call | solution.py:354
  487.8 7.2 %collective-permute-done.78 = bf16[64,2560]{1,0:T(8,128)(2,1)S(1)} collective-permute-done((bf16[64,2560]{1,0:T(8,128)(2,1)S(1)}, bf16[64,2560]{1,0:T(8,128)(2,1)S(1)}, u32[]{:S(2)}, u32[]{:S(2)}) %collective-permute-start.78) | collective-permute-done | bytes 327712 | tf_op jit(solution)/shard_map/ppermute | solution.py:50
  495.9 10.4 %collective-permute-done.74 = f32[2,512]{1,0:T(2,128)S(1)} collective-permute-done((f32[2,512]{1,0:T(2,128)S(1)}, f32[2,512]{1,0:T(2,128)S(1)}, u32[]{:S(2)}, u32[]{:S(2)}) %collective-permute-start.74) | collective-permute-done | bytes 4128 | tf_op jit(solution)/shard_map/ppermute | solution.py:50
  519.6 12.8 %collective-permute-done.61 = bf16[512,1024]{1,0:T(8,128)(2,1)S(1)} collective-permute-done((bf16[512,1024]{1,0:T(8,128)(2,1)S(1)}, bf16[512,1024]{1,0:T(8,128)(2,1)S(1)}, u32[]{:S(2)}, u32[]{:S(2)}) %collective-permute-start.61) | collective-permute-done | bytes 1048608 | tf_op jit(solution)/shard_map/ppermute | solution.py:50
  (492 shorter events, 237.4 us)
Async XLA Ops:
  0.7 57.3 %collective-permute-start = (bf16[512,1024]{1,0:T(8,128)(2,1)}, bf16[512,1024]{1,0:T(8,128)(2,1)}, u32[]{:S(2)}, u32[]{:S(2)}) collective-permute-start(bf16[512,1024]{1,0:T(8,128)(2,1)} %param.15), channel_id=1, source_target_pairs={{0,1},{1,0},{2,3},{3,2},{4,5},{5,4},{6,7},{7,6},{8,9},{9,8},{10,11... | collective-permute-start | bytes 3145736 | tf_op jit(solution)/shard_map/ppermute | solution.py:50
  45.9 57.0 %collective-permute-start.9 = (bf16[4,2,64,1536]{3,2,1,0:T(8,128)(2,1)S(1)}, bf16[4,2,64,1536]{3,2,1,0:T(8,128)(2,1)S(1)}, u32[]{:S(2)}, u32[]{:S(2)}) collective-permute-start(bf16[4,2,64,1536]{3,2,1,0:T(8,128)(2,1)S(1)} %pad_maximum_fusion.3), channel_id=1, source_target_pairs={{0,2},{1,3},{2,0},{3,1},{4,6},{5,7},{6,4},{7,5},{8,10},{9,11},{10,... | collective-permute-start | bytes 4718600 | tf_op jit(solution)/shard_map/ppermute | solution.py:50
  80.4 66.1 %collective-permute-start.17 = (bf16[4,64,1280]{2,1,0:T(8,128)(2,1)}, bf16[4,64,1280]{2,1,0:T(8,128)(2,1)}, u32[]{:S(2)}, u32[]{:S(2)}) collective-permute-start(bf16[4,64,1280]{2,1,0:T(8,128)(2,1)} %get-tuple-element.105), channel_id=1, source_target_pairs={{0,1},{1,0},{2,3},{3,2},{4,5},{5,4},{6,7},{7,6},{8,9},{9,8},{10,11... | collective-permute-start | bytes 1966088 | tf_op jit(solution)/shard_map/ppermute | solution.py:50
  80.9 67.9 %collective-permute-start.14 = (bf16[4,64,1280]{2,1,0:T(8,128)(2,1)}, bf16[4,64,1280]{2,1,0:T(8,128)(2,1)}, u32[]{:S(2)}, u32[]{:S(2)}) collective-permute-start(bf16[4,64,1280]{2,1,0:T(8,128)(2,1)} %get-tuple-element.105), channel_id=1, source_target_pairs={{0,4},{1,5},{2,6},{3,7},{4,0},{5,1},{6,2},{7,3},{8,12},{9,13},{10,... | collective-permute-start | bytes 1966088 | tf_op jit(solution)/shard_map/ppermute | solution.py:50
  82.4 60.7 %collective-permute-start.13 = (bf16[4,64,1280]{2,1,0:T(8,128)(2,1)}, bf16[4,64,1280]{2,1,0:T(8,128)(2,1)}, u32[]{:S(2)}, u32[]{:S(2)}) collective-permute-start(bf16[4,64,1280]{2,1,0:T(8,128)(2,1)} %get-tuple-element.105), channel_id=1, source_target_pairs={{0,2},{1,3},{2,0},{3,1},{4,6},{5,7},{6,4},{7,5},{8,10},{9,11},{10,... | collective-permute-start | bytes 1966088 | tf_op jit(solution)/shard_map/ppermute | solution.py:50
  102.9 45.9 %collective-permute-start.21 = (bf16[4,64,1280]{2,1,0:T(8,128)(2,1)}, bf16[4,64,1280]{2,1,0:T(8,128)(2,1)}, u32[]{:S(2)}, u32[]{:S(2)}) collective-permute-start(bf16[4,64,1280]{2,1,0:T(8,128)(2,1)} %get-tuple-element.104), channel_id=1, source_target_pairs={{0,2},{1,3},{2,0},{3,1},{4,6},{5,7},{6,4},{7,5},{8,10},{9,11},{10,... | collective-permute-start | bytes 1966088 | tf_op jit(solution)/shard_map/ppermute | solution.py:50
  103.0 58.8 %collective-permute-start.22 = (bf16[4,64,1280]{2,1,0:T(8,128)(2,1)}, bf16[4,64,1280]{2,1,0:T(8,128)(2,1)}, u32[]{:S(2)}, u32[]{:S(2)}) collective-permute-start(bf16[4,64,1280]{2,1,0:T(8,128)(2,1)} %get-tuple-element.104), channel_id=1, source_target_pairs={{0,4},{1,5},{2,6},{3,7},{4,0},{5,1},{6,2},{7,3},{8,12},{9,13},{10,... | collective-permute-start | bytes 1966088 | tf_op jit(solution)/shard_map/ppermute | solution.py:50
  160.3 17.8 %collective-permute-start.19 = (bf16[4,64,1280]{2,1,0:T(8,128)(2,1)}, bf16[4,64,1280]{2,1,0:T(8,128)(2,1)S(1)}, u32[]{:S(2)}, u32[]{:S(2)}) collective-permute-start(bf16[4,64,1280]{2,1,0:T(8,128)(2,1)} %collective-permute-done.14), channel_id=1, source_target_pairs={{0,1},{1,0},{2,3},{3,2},{4,5},{5,4},{6,7},{7,6},{8,9},{9,8},{10,11... | collective-permute-start | bytes 1966088 | tf_op jit(solution)/shard_map/ppermute | solution.py:50
  161.8 44.7 %collective-permute-start.35 = (bf16[4,64,1280]{2,1,0:T(8,128)(2,1)S(1)}, bf16[4,64,1280]{2,1,0:T(8,128)(2,1)S(1)}, u32[]{:S(2)}, u32[]{:S(2)}) collective-permute-start(bf16[4,64,1280]{2,1,0:T(8,128)(2,1)S(1)} %collective-permute-done.33), channel_id=1, source_target_pairs={{0,4},{1,5},{2,6},{3,7},{4,0},{5,1},{6,2},{7,3},{8,12},{9,13},{10,... | collective-permute-start | bytes 1966088 | tf_op jit(solution)/shard_map/ppermute | solution.py:50
  163.7 26.9 %collective-permute-start.29 = (bf16[4,64,1024]{2,1,0:T(8,128)(2,1)S(1)}, bf16[4,64,1024]{2,1,0:T(8,128)(2,1)S(1)}, u32[]{:S(2)}, u32[]{:S(2)}) collective-permute-start(bf16[4,64,1024]{2,1,0:T(8,128)(2,1)S(1)} %get-tuple-element.119), channel_id=1, source_target_pairs={{0,4},{1,5},{2,6},{3,7},{4,0},{5,1},{6,2},{7,3},{8,12},{9,13},{10,... | collective-permute-start | bytes 1572872 | tf_op jit(solution)/shard_map/ppermute | solution.py:50
  164.5 26.2 %collective-permute-start.38 = (bf16[4,64,1024]{2,1,0:T(8,128)(2,1)S(1)}, bf16[4,64,1024]{2,1,0:T(8,128)(2,1)S(1)}, u32[]{:S(2)}, u32[]{:S(2)}) collective-permute-start(bf16[4,64,1024]{2,1,0:T(8,128)(2,1)S(1)} %get-tuple-element.119), channel_id=1, source_target_pairs={{0,1},{1,0},{2,3},{3,2},{4,5},{5,4},{6,7},{7,6},{8,9},{9,8},{10,11... | collective-permute-start | bytes 1572872 | tf_op jit(solution)/shard_map/ppermute | solution.py:50
  179.3 22.2 %collective-permute-start.31 = (bf16[4,64,1024]{2,1,0:T(8,128)(2,1)S(1)}, bf16[4,64,1024]{2,1,0:T(8,128)(2,1)S(1)}, u32[]{:S(2)}, u32[]{:S(2)}) collective-permute-start(bf16[4,64,1024]{2,1,0:T(8,128)(2,1)S(1)} %get-tuple-element.118), channel_id=1, source_target_pairs={{0,4},{1,5},{2,6},{3,7},{4,0},{5,1},{6,2},{7,3},{8,12},{9,13},{10,... | collective-permute-start | bytes 1572872 | tf_op jit(solution)/shard_map/ppermute | solution.py:50
  181.0 21.1 %collective-permute-start.40 = (bf16[4,64,1024]{2,1,0:T(8,128)(2,1)S(1)}, bf16[4,64,1024]{2,1,0:T(8,128)(2,1)S(1)}, u32[]{:S(2)}, u32[]{:S(2)}) collective-permute-start(bf16[4,64,1024]{2,1,0:T(8,128)(2,1)S(1)} %get-tuple-element.118), channel_id=1, source_target_pairs={{0,1},{1,0},{2,3},{3,2},{4,5},{5,4},{6,7},{7,6},{8,9},{9,8},{10,11... | collective-permute-start | bytes 1572872 | tf_op jit(solution)/shard_map/ppermute | solution.py:50
  205.9 21.4 %collective-permute-start.16 = (bf16[512,512]{1,0:T(8,128)(2,1)S(1)}, bf16[512,512]{1,0:T(8,128)(2,1)S(1)}, u32[]{:S(2)}, u32[]{:S(2)}) collective-permute-start(bf16[512,512]{1,0:T(8,128)(2,1)S(1)} %dynamic-slice_bitcast_fusion.16), channel_id=1, source_target_pairs={{0,1},{1,0},{2,3},{3,2},{4,5},{5,4},{6,7},{7,6},{8,9},{9,8},{10,11... | collective-permute-start | bytes 1572872 | tf_op jit(solution)/shard_map/ppermute | solution.py:50
  206.6 37.2 %collective-permute-start.37 = (f32[2048]{0:T(1024)S(1)}, f32[2048]{0:T(1024)S(1)}, u32[]{:S(2)}, u32[]{:S(2)}) collective-permute-start(f32[2048]{0:T(1024)S(1)} %copy-done.53), channel_id=1, source_target_pairs={{0,1},{1,0},{2,3},{3,2},{4,5},{5,4},{6,7},{7,6},{8,9},{9,8},{10,11... | collective-permute-start | bytes 24584 | tf_op jit(solution)/shard_map/ppermute | solution.py:50
  217.0 26.7 %collective-permute-start.36 = (bf16[4,64,1280]{2,1,0:T(8,128)(2,1)S(1)}, bf16[4,64,1280]{2,1,0:T(8,128)(2,1)S(1)}, u32[]{:S(2)}, u32[]{:S(2)}) collective-permute-start(bf16[4,64,1280]{2,1,0:T(8,128)(2,1)S(1)} %collective-permute-done.35), channel_id=1, source_target_pairs={{0,2},{1,3},{2,0},{3,1},{4,6},{5,7},{6,4},{7,5},{8,10},{9,11},{10,... | collective-permute-start | bytes 1966088 | tf_op jit(solution)/shard_map/ppermute | solution.py:50
  218.3 40.6 %collective-permute-start.43 = (bf16[4,64,1024]{2,1,0:T(8,128)(2,1)S(1)}, bf16[4,64,1024]{2,1,0:T(8,128)(2,1)S(1)}, u32[]{:S(2)}, u32[]{:S(2)}) collective-permute-start(bf16[4,64,1024]{2,1,0:T(8,128)(2,1)S(1)} %collective-permute-done.42), channel_id=1, source_target_pairs={{0,2},{1,3},{2,0},{3,1},{4,6},{5,7},{6,4},{7,5},{8,10},{9,11},{10,... | collective-permute-start | bytes 1572872 | tf_op jit(solution)/shard_map/ppermute | solution.py:50
  218.3 40.7 %collective-permute-start.45 = (bf16[4,64,1024]{2,1,0:T(8,128)(2,1)S(1)}, bf16[4,64,1024]{2,1,0:T(8,128)(2,1)S(1)}, u32[]{:S(2)}, u32[]{:S(2)}) collective-permute-start(bf16[4,64,1024]{2,1,0:T(8,128)(2,1)S(1)} %collective-permute-done.44), channel_id=1, source_target_pairs={{0,2},{1,3},{2,0},{3,1},{4,6},{5,7},{6,4},{7,5},{8,10},{9,11},{10,... | collective-permute-start | bytes 1572872 | tf_op jit(solution)/shard_map/ppermute | solution.py:50
  272.4 19.5 %collective-permute-start.46 = (bf16[4,2,64,2048]{3,2,1,0:T(8,128)(2,1)}, bf16[4,2,64,2048]{3,2,1,0:T(8,128)(2,1)}, u32[]{:S(2)}, u32[]{:S(2)}) collective-permute-start(bf16[4,2,64,2048]{3,2,1,0:T(8,128)(2,1)} %dynamic-slice_bitcast_fusion.3), channel_id=1, source_target_pairs={{0,2},{1,3},{2,0},{3,1},{4,6},{5,7},{6,4},{7,5},{8,10},{9,11},{10,... | collective-permute-start | bytes 6291464 | tf_op jit(solution)/shard_map/ppermute | solution.py:50
  274.1 19.9 %collective-permute-start.48 = (bf16[4,2,64,2048]{3,2,1,0:T(8,128)(2,1)}, bf16[4,2,64,2048]{3,2,1,0:T(8,128)(2,1)}, u32[]{:S(2)}, u32[]{:S(2)}) collective-permute-start(bf16[4,2,64,2048]{3,2,1,0:T(8,128)(2,1)} %dynamic-slice_bitcast_fusion.2), channel_id=1, source_target_pairs={{0,2},{1,3},{2,0},{3,1},{4,6},{5,7},{6,4},{7,5},{8,10},{9,11},{10,... | collective-permute-start | bytes 6291464 | tf_op jit(solution)/shard_map/ppermute | solution.py:50
  305.2 84.3 %collective-permute-start.55 = (bf16[4,2,64,2048]{3,2,1,0:T(8,128)(2,1)}, bf16[4,2,64,2048]{3,2,1,0:T(8,128)(2,1)}, u32[]{:S(2)}, u32[]{:S(2)}) collective-permute-start(bf16[4,2,64,2048]{3,2,1,0:T(8,128)(2,1)} %dynamic-slice_bitcast_fusion), channel_id=1, source_target_pairs={{0,2},{1,3},{2,0},{3,1},{4,6},{5,7},{6,4},{7,5},{8,10},{9,11},{10,... | collective-permute-start | bytes 6291464 | tf_op jit(solution)/shard_map/ppermute | solution.py:50
  306.7 87.1 %collective-permute-start.53 = (bf16[4,2,64,2048]{3,2,1,0:T(8,128)(2,1)}, bf16[4,2,64,2048]{3,2,1,0:T(8,128)(2,1)}, u32[]{:S(2)}, u32[]{:S(2)}) collective-permute-start(bf16[4,2,64,2048]{3,2,1,0:T(8,128)(2,1)} %dynamic-slice_bitcast_fusion.1), channel_id=1, source_target_pairs={{0,2},{1,3},{2,0},{3,1},{4,6},{5,7},{6,4},{7,5},{8,10},{9,11},{10,... | collective-permute-start | bytes 6291464 | tf_op jit(solution)/shard_map/ppermute | solution.py:50
  317.4 78.4 %collective-permute-start.59 = (bf16[4,64,1024]{2,1,0:T(8,128)(2,1)S(1)}, bf16[4,64,1024]{2,1,0:T(8,128)(2,1)}, u32[]{:S(2)}, u32[]{:S(2)}) collective-permute-start(bf16[4,64,1024]{2,1,0:T(8,128)(2,1)S(1)} %get-tuple-element.112), channel_id=1, source_target_pairs={{0,4},{1,5},{2,6},{3,7},{4,0},{5,1},{6,2},{7,3},{8,12},{9,13},{10,... | collective-permute-start | bytes 1572872 | tf_op jit(solution)/shard_map/ppermute | solution.py:50
  339.4 33.3 %collective-permute-start.51 = (bf16[512,512]{1,0:T(8,128)(2,1)}, bf16[512,512]{1,0:T(8,128)(2,1)}, u32[]{:S(2)}, u32[]{:S(2)}) collective-permute-start(bf16[512,512]{1,0:T(8,128)(2,1)} %convolution_convert_fusion.9), channel_id=1, source_target_pairs={{0,1},{1,0},{2,3},{3,2},{4,5},{5,4},{6,7},{7,6},{8,9},{9,8},{10,11... | collective-permute-start | bytes 1572872 | tf_op jit(solution)/shard_map/ppermute | solution.py:50
  388.8 26.1 %collective-permute-start.60 = (bf16[4,64,2048]{2,1,0:T(8,128)(2,1)S(1)}, bf16[4,64,2048]{2,1,0:T(8,128)(2,1)S(1)}, u32[]{:S(2)}, u32[]{:S(2)}) collective-permute-start(bf16[4,64,2048]{2,1,0:T(8,128)(2,1)S(1)} %copy-done.36), channel_id=1, source_target_pairs={{0,1},{1,0},{2,3},{3,2},{4,5},{5,4},{6,7},{7,6},{8,9},{9,8},{10,11... | collective-permute-start | bytes 3145736 | tf_op jit(solution)/shard_map/ppermute | solution.py:50
  391.7 24.9 %collective-permute-start.57 = (bf16[4,64,1280]{2,1,0:T(8,128)(2,1)S(1)}, bf16[4,64,1280]{2,1,0:T(8,128)(2,1)S(1)}, u32[]{:S(2)}, u32[]{:S(2)}) collective-permute-start(bf16[4,64,1280]{2,1,0:T(8,128)(2,1)S(1)} %get-tuple-element.101), channel_id=1, source_target_pairs={{0,4},{1,5},{2,6},{3,7},{4,0},{5,1},{6,2},{7,3},{8,12},{9,13},{10,... | collective-permute-start | bytes 1966088 | tf_op jit(solution)/shard_map/ppermute | solution.py:50
  392.4 41.0 %collective-permute-start.58 = (bf16[4,64,1280]{2,1,0:T(8,128)(2,1)S(1)}, bf16[4,64,1280]{2,1,0:T(8,128)(2,1)S(1)}, u32[]{:S(2)}, u32[]{:S(2)}) collective-permute-start(bf16[4,64,1280]{2,1,0:T(8,128)(2,1)S(1)} %get-tuple-element.100), channel_id=1, source_target_pairs={{0,1},{1,0},{2,3},{3,2},{4,5},{5,4},{6,7},{7,6},{8,9},{9,8},{10,11... | collective-permute-start | bytes 1966088 | tf_op jit(solution)/shard_map/ppermute | solution.py:50
  425.0 35.4 %collective-permute-start.77 = (bf16[4,64,2560]{2,1,0:T(8,128)(2,1)S(1)}, bf16[4,64,2560]{2,1,0:T(8,128)(2,1)S(1)}, u32[]{:S(2)}, u32[]{:S(2)}) collective-permute-start(bf16[4,64,2560]{2,1,0:T(8,128)(2,1)S(1)} %pad_maximum_fusion.5), channel_id=1, source_target_pairs={{0,1},{1,0},{2,3},{3,2},{4,5},{5,4},{6,7},{7,6},{8,9},{9,8},{10,11... | collective-permute-start | bytes 3932168 | tf_op jit(solution)/shard_map/ppermute | solution.py:50
  433.5 17.7 %collective-permute-start.76 = (bf16[4,64,1280]{2,1,0:T(8,128)(2,1)S(1)}, bf16[4,64,1280]{2,1,0:T(8,128)(2,1)S(1)}, u32[]{:S(2)}, u32[]{:S(2)}) collective-permute-start(bf16[4,64,1280]{2,1,0:T(8,128)(2,1)S(1)} %get-tuple-element.99), channel_id=1, source_target_pairs={{0,4},{1,5},{2,6},{3,7},{4,0},{5,1},{6,2},{7,3},{8,12},{9,13},{10,... | collective-permute-start | bytes 1966088 | tf_op jit(solution)/shard_map/ppermute | solution.py:50
  434.1 26.3 %collective-permute-start.56 = (bf16[4,64,1280]{2,1,0:T(8,128)(2,1)S(1)}, bf16[4,64,1280]{2,1,0:T(8,128)(2,1)S(1)}, u32[]{:S(2)}, u32[]{:S(2)}) collective-permute-start(bf16[4,64,1280]{2,1,0:T(8,128)(2,1)S(1)} %get-tuple-element.98), channel_id=1, source_target_pairs={{0,4},{1,5},{2,6},{3,7},{4,0},{5,1},{6,2},{7,3},{8,12},{9,13},{10,... | collective-permute-start | bytes 1966088 | tf_op jit(solution)/shard_map/ppermute | solution.py:50
  495.8 22.6 %collective-permute-start.62 = (bf16[4,2,64,1536]{3,2,1,0:T(8,128)(2,1)S(1)}, bf16[4,2,64,1536]{3,2,1,0:T(8,128)(2,1)S(1)}, u32[]{:S(2)}, u32[]{:S(2)}) collective-permute-start(bf16[4,2,64,1536]{3,2,1,0:T(8,128)(2,1)S(1)} %pad_maximum_fusion.4), channel_id=1, source_target_pairs={{0,2},{1,3},{2,0},{3,1},{4,6},{5,7},{6,4},{7,5},{8,10},{9,11},{10,... | collective-permute-start | bytes 4718600 | tf_op jit(solution)/shard_map/ppermute | solution.py:50
  508.5 23.9 %collective-permute-start.61 = (bf16[512,1024]{1,0:T(8,128)(2,1)S(1)}, bf16[512,1024]{1,0:T(8,128)(2,1)S(1)}, u32[]{:S(2)}, u32[]{:S(2)}) collective-permute-start(bf16[512,1024]{1,0:T(8,128)(2,1)S(1)} %bitcast_convert_fusion), channel_id=1, source_target_pairs={{0,1},{1,0},{2,3},{3,2},{4,5},{5,4},{6,7},{7,6},{8,9},{9,8},{10,11... | collective-permute-start | bytes 3145736 | tf_op jit(solution)/shard_map/ppermute | solution.py:50
  (121 other events, 1349.0 us)

commit v3 on v2

--- a/solution.py
+++ b/solution.py
@@ -73,98 +73,121 @@
     return lax.dynamic_index_in_dim(value, index, axis, keepdims=False)
 
 
-def ring_sum(value, sizes, digit, index, axis):
+def spread_sum(value, sizes, digit, index, axis):
     count = sizes[digit]
-    if count == 1:
-        return jnp.squeeze(value, axis)
-    moving = pick(value, (index - 1) % count, axis)
+    terms = [pick(value, index, axis)]
     for k in range(1, count):
-        moving = hop(moving, sizes, digit) + pick(value, (index - 1 - k) % count, axis)
-    return moving
-
-
-def after(value, *others):
-    return lax.optimization_barrier((value, *others))[0]
-
-
-def all_sum(value, sizes, digits):
-    for digit in digits:
-        value = sum(ring(value, sizes, digit))
-    return value
-
-
-def put(out, piece, x, c, begin):
-    zero = jnp.int32(0)
-    return lax.dynamic_update_slice(
-        out, piece[:, None, None], (zero, x.astype(jnp.int32), c.astype(jnp.int32), zero, jnp.int32(begin))
-    )
-
-
-def gather_project(shard, sizes, at):
+        terms.append(hop(pick(value, (index + k) % count, axis), sizes, digit, k))
+    return terms
+
+
+def sum_over(value, sizes, digit, index, axis):
+    return sum(spread_sum(value, sizes, digit, index, axis))
+
+
+def sync(*values):
+    return lax.optimization_barrier(values)
+
+
+def all_sum(value, sizes, digit):
+    return value + sum(hop(value, sizes, digit, k) for k in range(1, sizes[digit]))
+
+
+def fan(value, sizes, digit):
+    return [value] + [hop(value, sizes, digit, k) for k in range(1, sizes[digit])]
+
+
+def arrange(pieces, shapes, moves, places):
+    out = [jnp.zeros(shape, BF16) for shape in shapes]
+    for source, low, width, target, begin, lead in moves:
+        piece = pieces[source][..., low : low + width]
+        start = [jnp.int32(0) if w is None else places[w].astype(jnp.int32) for w in lead]
+        fixed = [n for n, w in enumerate(lead) if w is not None]
+        piece = jnp.expand_dims(piece, fixed)
+        start += [jnp.int32(0), jnp.int32(begin)]
+        out[target] = lax.dynamic_update_slice(out[target], piece, start)
+    return out
+
+
+def gather_project(shard, sizes, at, later):
     half = shard.shape[1] // 2
-    first = ring(shard[:, :half], sizes, X)
-    second = place(ring(shard[:, half:], sizes, Z), at[Z], 0)
-    first = place(ring(place(first, at[X], 0), sizes, Z), at[Z], 0)
-    second = place(ring(second, sizes, X), at[X], 1)
+    over_x = hop(shard[:, :half], sizes, X) if sizes[X] == 2 else None
+    second = place(fan(shard[:, half:], sizes, Z), at[Z], 0)
+    first = [shard[:, :half]] + ([over_x] if sizes[X] == 2 else [])
+    first = fan(place(first, at[X], 0), sizes, Z)
+    first, later = sync(first, later)
+    first = place(first, at[Z], 0)
+    second = place(fan(second, sizes, X), at[X], 1)
     both = jnp.concatenate([first, second], axis=-1)
-    full = place(ring(both, sizes, C), at[C], 2)
-    return full.reshape(-1, shard.shape[1]), first
-
-
-def spread(halves, sizes):
+    full = place(fan(both, sizes, C), at[C], 2)
+    return full.reshape(-1, shard.shape[1]), later
+
+
+def stack_z(pieces, sizes, at):
+    depth, width = pieces[0].shape
+    cut = (width // 2 + 127) // 128 * 128
+    shapes = [(sizes[Z], depth, cut), (sizes[Z], depth, width - cut)]
+    moves = []
+    for k in range(sizes[Z]):
+        moves.append((k, 0, cut, 0, 0, (k,)))
+        moves.append((k, cut, width - cut, 1, 0, (k,)))
+    return arrange(pieces, shapes, moves, [(at[Z] - k) % sizes[Z] for k in range(sizes[Z])])
+
+
+def spread_sides(halves, sizes):
+    over_x = list(zip(*[fan(b, sizes, X) for b in halves]))
     if sizes[X] == 2 and sizes[Y] == 2:
-        over_x = [hop(b, sizes, X) for b in halves]
-        over_y = [hop(b, sizes, Y) for b in halves]
-        corner = [hop(over_x[0], sizes, Y), hop(over_y[1], sizes, X)]
-        return [[halves, over_x], [over_y, corner]]
-    over_x = list(zip(*[ring(b, sizes, X) for b in halves]))
-    both = [list(zip(*[ring(b, sizes, Y) for b in piece])) for piece in over_x]
+        return over_x, [hop(b, sizes, Y) for b in halves]
+    return over_x, []
+
+
+def spread_corner(over_x, over_y, sizes):
+    if sizes[X] == 2 and sizes[Y] == 2:
+        corner = [hop(over_x[1][0], sizes, Y), hop(over_y[1], sizes, X)]
+        return [list(over_x), [over_y, corner]]
+    both = [list(zip(*[fan(b, sizes, Y) for b in piece])) for piece in over_x]
     return [[both[j][k] for j in range(sizes[X])] for k in range(sizes[Y])]
 
 
-def gather_halves(shard, sizes, at):
-    deep = place(ring(shard, sizes, Z), at[Z], 0)
-    half = shard.shape[1] // 2
-    return spread([deep[..., :half], deep[..., half:]], sizes), deep
-
-
-def assemble(pieces, sizes, at, widths):
-    out = []
-    for by_x in pieces:
-        begins = [0]
-        for width in widths:
-            begins.append(begins[-1] + width)
-        nz, depth, half = by_x[0][0].shape
-        mats = [jnp.zeros((nz, sizes[X], sizes[C], depth, width), BF16) for width in widths]
+def assemble(spreads, sizes, at, widths):
+    begins = [sum(widths[:m]) for m in range(len(widths))]
+    nz, depth, _ = spreads[0][0][0].shape
+    pieces, moves, shapes = [], [], []
+    for k, by_x in enumerate(spreads):
+        shapes += [(nz, sizes[X], sizes[C], depth, width) for width in widths]
         for j, halves in enumerate(by_x):
-            for h, piece in enumerate(halves):
-                for c, part in enumerate(ring(piece, sizes, C)):
-                    x_at, c_at = (at[X] - j) % sizes[X], (at[C] - c) % sizes[C]
+            base = 0
+            for half in halves:
+                size = half.shape[-1]
+                for c, part in enumerate(fan(half, sizes, C)):
                     for m, width in enumerate(widths):
-                        low = max(begins[m], h * half)
-                        high = min(begins[m + 1], (h + 1) * half)
+                        low = max(begins[m], base)
+                        high = min(begins[m] + width, base + size)
                         if low < high:
-                            cut = part[..., low - h * half : high - h * half]
-                            mats[m] = put(mats[m], cut, x_at, c_at, low - begins[m])
-        out.append([m.reshape(-1, m.shape[-1]) for m in mats])
-    return out
-
-
-def core_part(fulls, sizes, core):
-    return jnp.concatenate(
-        [
-            pick(f.reshape(sizes[Z], sizes[X], sizes[C], -1, f.shape[-1]), core, 2)
-            for f in fulls
-        ],
-        axis=-1,
-    )
-
-
-def core_sum(fulls, sizes, at):
+                            lead = (None, j, sizes[X] + c)
+                            target = k * len(widths) + m
+                            moves.append(
+                                (len(pieces), low - base, high - low, target, low - begins[m], lead)
+                            )
+                    pieces.append(part)
+                base += size
+    places = [(at[X] - j) % sizes[X] for j in range(sizes[X])]
+    places += [(at[C] - c) % sizes[C] for c in range(sizes[C])]
+    mats = arrange(pieces, shapes, moves, places)
+    mats = [m.reshape(-1, m.shape[-1]) for m in mats]
+    count = len(widths)
+    return [mats[k * count : (k + 1) * count] for k in range(len(spreads))]
+
+
+def core_part(full, sizes, core):
+    return pick(full.reshape(sizes[Z], sizes[X], sizes[C], -1, full.shape[-1]), core, 2)
+
+
+def core_send(full, sizes, at):
+    own = core_part(full, sizes, at[C])
     if sizes[C] == 1:
-        return core_part(fulls, sizes, at[C])
-    sent = hop(core_part(fulls, sizes, (at[C] + 1) % sizes[C]), sizes, C)
-    return sent + core_part(fulls, sizes, at[C])
+        return (own,)
+    return (hop(core_part(full, sizes, (at[C] + 1) % sizes[C]), sizes, C), own)
 
 
 def corner_step(parts, sizes, at):
@@ -175,33 +198,23 @@
     over_y, corner = pick(parts[1], at[X], 1), pick(parts[1], far_x, 1)
     from_x = hop(cut(corner, 0), sizes, X)
     from_y = hop(cut(corner, 1), sizes, Y)
-    first = hop(cut(over_x, 0), sizes, X)
-    return (own, first, over_x, over_y, from_x, from_y)
-
-
-def side_step(held, sizes, wait):
-    own, first, over_x, over_y, from_x, from_y = held
+    return (own, over_x, over_y, from_x, from_y)
+
+
+def side_step(held, sizes):
+    own, over_x, over_y, from_x, from_y = held
     half = own.shape[-1] // 2
     cut = lambda p, h: p[..., h * half : (h + 1) * half]
-    second = hop(cut(over_x, 1) + from_y, sizes, X)
-    send = after(jnp.concatenate([cut(over_y, 0) + from_x, cut(over_y, 1)], axis=-1), *wait)
-    side = hop(send, sizes, Y)
-    return own + jnp.concatenate([first, second], axis=-1) + side
+    to_x = jnp.concatenate([cut(over_x, 0), cut(over_x, 1) + from_y], axis=-1)
+    to_y = jnp.concatenate([cut(over_y, 0) + from_x, cut(over_y, 1)], axis=-1)
+    return (own, hop(to_x, sizes, X), hop(to_y, sizes, Y))
 
 
 def plain_square(parts, sizes, at):
     total = parts[0]
     for k in range(1, sizes[Y]):
         total = total + hop(parts[k], sizes, Y, -k)
-    return ring_sum(total, sizes, X, at[X], 1)
-
-
-def z_steps(value, sizes, at):
-    return pick(value, (at[Z] - 1) % sizes[Z], 0)
-
-
-def z_next(value, moving, k, sizes, at):
-    return hop(moving, sizes, Z) + pick(value, (at[Z] - 1 - k) % sizes[Z], 0)
+    return (sum_over(total, sizes, X, at[X], 1),)
 
 
 def norm_parts(rows):
@@ -315,14 +328,14 @@
     return lambda h: (0, begin + h)
 
 
-def attention(projected, segment):
+def attention(projected, segment, first, count):
     rows, width = projected.shape
     pairs = width // 3 // PAIR
     block = lambda f: pl.BlockSpec((rows, PAIR), f)
     return pl.pallas_call(
         attend_kernel,
-        grid=(pairs,),
-        in_specs=[block(third(c * pairs)) for c in range(3)]
+        grid=(count,),
+        in_specs=[block(third(c * pairs + first)) for c in range(3)]
         + [
             pl.BlockSpec((rows, 1), lambda h: (0, 0)),
             pl.BlockSpec((1, rows), lambda h: (0, 0)),
@@ -333,16 +346,16 @@
             pl.BlockSpec((1, 2, rows), lambda h: (h, 0, 0)),
         ],
         out_shape=[
-            jax.ShapeDtypeStruct((rows, pairs * PAIR), BF16),
-            jax.ShapeDtypeStruct((rows, pairs * PAIR), F32),
-            jax.ShapeDtypeStruct((pairs, 2, rows), F32),
+            jax.ShapeDtypeStruct((rows, count * PAIR), BF16),
+            jax.ShapeDtypeStruct((rows, count * PAIR), F32),
+            jax.ShapeDtypeStruct((count, 2, rows), F32),
         ],
         scratch_shapes=[pltpu.VMEM((rows, rows), F32)],
         compiler_params=pltpu.CompilerParams(vmem_limit_bytes=40 * 2**20),
         cost_estimate=pl.CostEstimate(
-            flops=pairs * 16 * rows * rows * PAIR,
-            bytes_accessed=16 * rows * pairs * PAIR,
-            transcendentals=2 * pairs * rows * rows,
+            flops=count * 16 * rows * rows * PAIR,
+            bytes_accessed=16 * rows * count * PAIR,
+            transcendentals=2 * count * rows * rows,
         ),
     )(projected, projected, projected, segment[:, None], segment[None, :])
 
@@ -358,8 +371,8 @@
         + [
             pl.BlockSpec((rows, 1), lambda h: (0, 0)),
             pl.BlockSpec((1, rows), lambda h: (0, 0)),
-            block(third(first)),
-            pl.BlockSpec((1, 2, rows), lambda h: (first + h, 0, 0)),
+            block(third(0)),
+            pl.BlockSpec((1, 2, rows), lambda h: (h, 0, 0)),
             block(third(first)),
         ],
         out_specs=pl.BlockSpec((3, rows, PAIR), lambda h: (0, 0, h)),
@@ -410,23 +423,41 @@
     )
     valid = (mine * rows + lax.iota(jnp.int32, rows) < ends[-1])[:, None]
 
-    whole_tokens = place(ring(tokens, sizes, Y), mine, 0).reshape(all_rows, width)
-    proj, early = gather_project(
-        jnp.transpose(project_weight, (1, 0, 2)).reshape(depth, 3 * heads_width), sizes, at
-    )
+    calls = 2 if pairs % 2 == 0 else 1
+    group = pairs // calls
+    span = group * PAIR
+
+    token_pieces = fan(tokens, sizes, Y)
     upper_shard = jnp.concatenate([output_weight.T, expand_weight], axis=1)
-    upper_pieces, deep = gather_halves(after(upper_shard, early), sizes, at)
-    shrink_pieces, _ = gather_halves(after(shrink_weight.T, deep), sizes, at)
-    expand_biases = ring(expand_bias, sizes, Y)
+    proj, (upper_shard, token_pieces) = gather_project(
+        jnp.transpose(project_weight, (1, 0, 2)).reshape(depth, 3 * heads_width),
+        sizes,
+        at,
+        (upper_shard, token_pieces),
+    )
+    whole_tokens = place(token_pieces, mine, 0).reshape(all_rows, width)
+    upper_z = fan(upper_shard, sizes, Z)
+    expand_biases = fan(expand_bias, sizes, Y)
 
     bias = jnp.concatenate([project_bias[0], jnp.zeros_like(project_bias[0]), project_bias[1]])
     projected = (dot(whole_tokens, proj, NN) + bias).astype(BF16)
-    mixed_low, mixed_full, logs = attention(projected, segment)
-    by_rows = mixed_low.reshape(n_t, rows, heads_width)
+    projected, shrink_shard = sync(projected, shrink_weight.T)
+    shrink_z = fan(shrink_shard, sizes, Z)
+    fwd = [attention(projected, segment, 0, group)]
+    fwd[0], upper_z, projected = sync(fwd[0], upper_z, projected)
+    upper_x, upper_y = spread_sides(stack_z(upper_z, sizes, at), sizes)
+    if calls == 2:
+        fwd.append(attention(projected, segment, group, group))
+    if square:
+        fwd[-1], upper_x[1], upper_y = sync(fwd[-1], upper_x[1], upper_y)
+    by_rows = jnp.concatenate([f[0] for f in fwd], axis=1).reshape(n_t, rows, heads_width)
     mixed = [pick(by_rows, mine, 0)]
     for k in range(1, n_t):
         mixed.append(hop(pick(by_rows, (mine + k) % n_t, 0), sizes, Y, k))
 
+    upper_pieces = spread_corner(upper_x, upper_y, sizes)
+    mixed, shrink_z = sync(mixed, shrink_z)
+    shrink_x, shrink_y = spread_sides(stack_z(shrink_z, sizes, at), sizes)
     gathered = assemble(upper_pieces, sizes, at, (heads_width, hidden))
     mix = [g[0] for g in gathered]
     expand = [g[1] for g in gathered]
@@ -435,10 +466,14 @@
     normed1 = unit1 * first_gain + first_shift
     low1 = normed1.astype(BF16)
     active, slope = [], []
+    low1_now = low1
     for w, b in zip(expand, expand_biases):
-        act, der = gelu_both(dot(low1, w, NN) + b)
+        act, der = gelu_both(dot(low1_now, w, NN) + b)
         active.append(act.astype(BF16))
         slope.append(der.astype(BF16))
+        if len(active) == 1:
+            active[0], low1_now, shrink_x, shrink_y = sync(active[0], low1, shrink_x, shrink_y)
+    shrink_pieces = spread_corner(shrink_x, shrink_y, sizes)
     shrink = [g[0] for g in assemble(shrink_pieces, sizes, at, (hidden,))]
     branch = sum(dot(a, w, NT) for a, w in zip(active, shrink)) + shrink_bias
     unit2, scale2 = norm_parts(normed1 + branch)
@@ -450,19 +485,16 @@
     grad_r2 = norm_back(grad, unit2, scale2, second_gain)
     grad_branch = grad_r2.astype(BF16)
     grad_shrink_bias = jnp.sum(grad_branch, axis=0, dtype=F32)
-    shrink_parts = [core_sum([dot(grad_branch, a, TN).astype(BF16)], sizes, at) for a in active]
+    shrink_core = [core_send(dot(grad_branch, a, TN).astype(BF16), sizes, at) for a in active]
     grad_upper = [
         (dot(grad_branch, w, NN) * s.astype(F32)).astype(BF16) for w, s in zip(shrink, slope)
     ]
     grad_expand_biases = [jnp.sum(g, axis=0, dtype=F32) for g in grad_upper]
+    grad_normed1 = sum(dot(g, w, NT) for g, w in zip(grad_upper, expand)) + grad_r2
+    shrink_core, grad_normed1 = sync(shrink_core, grad_normed1)
+    shrink_parts = [sum(parts) for parts in shrink_core]
     if square:
         shrink_held = corner_step(shrink_parts, sizes, at)
-    low1_later = after(low1, *shrink_parts)
-    grad_expand = [dot(low1_later, g, TN).astype(BF16) for g in grad_upper]
-    expand_parts = [core_sum([g], sizes, at) for g in grad_expand]
-    grad_normed1 = sum(dot(g, w, NT) for g, w in zip(grad_upper, expand)) + grad_r2
-    if square:
-        grad_normed1 = after(grad_normed1, *shrink_held)
     grad_first_gain = jnp.sum(grad_normed1 * unit1, axis=0)
     grad_first_shift = jnp.sum(grad_normed1, axis=0)
     grad_r1 = norm_back(grad_normed1, unit1, scale1, first_gain)
@@ -473,66 +505,18 @@
     for k, w in enumerate(mix):
         part = dot(grad_attn, w, NN).astype(BF16)
         grad_pieces.append(hop(part, sizes, Y, -k) if k else part)
+    low1, grad_attn = sync(low1, grad_attn)
+    grad_expand = [dot(low1, g, TN).astype(BF16) for g in grad_upper]
+    if square:
+        grad_expand, shrink_held = sync(grad_expand, shrink_held)
+        shrink_sides = side_step(shrink_held, sizes)
+    else:
+        shrink_sides = plain_square(shrink_parts, sizes, at)
+    expand_core = [core_send(g, sizes, at) for g in grad_expand]
+    grad_mix = [dot(grad_attn, m, TN).astype(BF16) for m in mixed]
+    mix_core = [core_send(g, sizes, at) for g in grad_mix]
     grad_rows = place([grad_pieces[-k % n_t] for k in range(n_t)], mine, 0)
     grad_rows = grad_rows.reshape(all_rows, heads_width)
-    grad_mix = [dot(grad_attn, m, TN).astype(BF16) for m in mixed]
-    upper_parts = [
-        jnp.concatenate([core_sum([a], sizes, at), b], axis=-1)
-        for a, b in zip(grad_mix, expand_parts)
-    ]
-    calls = 2 if pairs % 2 == 0 else 1
-    if square:
-        upper_held = corner_step(upper_parts, sizes, at)
-        shrink_sum = side_step(shrink_held, sizes, (grad_rows,))
-        grad_rows = after(grad_rows, *upper_parts)
-    else:
-        shrink_sum = plain_square(shrink_parts, sizes, at)
-        upper_sum = plain_square(upper_parts, sizes, at)
-    done = [
-        attention_back(
-            projected, segment, mixed_full, logs, grad_rows, 0, pairs // calls
-        )
-    ]
-    if square:
-        upper_sum = side_step(upper_held, sizes, (done[0],))
-        logs = after(logs, done[0], *upper_held)
-    if calls == 2:
-        done.append(
-            attention_back(
-                projected, segment, mixed_full, logs, grad_rows, pairs // 2, pairs // 2
-            )
-        )
-    projected_grad = jnp.concatenate(done, axis=-1)
-    moving = z_steps(shrink_sum, sizes, at)
-    if sizes[Z] > 1:
-        moving = z_next(shrink_sum, moving, 1, sizes, at)
-        projected_grad = after(projected_grad, shrink_sum)
-
-    project_parts = [
-        dot(whole_tokens, projected_grad[c], TN).astype(BF16) for c in range(3)
-    ]
-    bias_sums = jnp.stack(
-        [jnp.sum(projected_grad[c], axis=0, dtype=F32) for c in (0, 2)]
-    )
-    project_sum = core_sum(project_parts, sizes, at)
-    cut = 3 * heads_width // 2
-    first_half = ring_sum(project_sum[..., :cut], sizes, X, at[X], 1)
-    second_half = ring_sum(project_sum[..., cut:], sizes, Z, at[Z], 0)
-    first_half = ring_sum(first_half, sizes, Z, at[Z], 0)
-    second_half = ring_sum(second_half, sizes, X, at[X], 0)
-    grad_project = jnp.concatenate([first_half, second_half], axis=-1)
-    grad_project_weight = jnp.transpose(
-        grad_project.reshape(depth, 3, heads_width), (1, 0, 2)
-    ).astype(F32)
-    grad_project_bias = all_sum(bias_sums, sizes, (C, X, Z))
-
-    for k in range(2, sizes[Z]):
-        moving = z_next(shrink_sum, moving, k, sizes, at)
-    grad_shrink_weight = moving.astype(F32).T
-    owned = ring_sum(upper_sum, sizes, Z, at[Z], 0).astype(F32)
-    grad_output_weight = owned[:, :heads_width].T
-    grad_expand_weight = owned[:, heads_width:]
-
     packed = jnp.concatenate(
         [
             grad_second_gain,
@@ -544,7 +528,72 @@
             place(grad_expand_biases, mine, 0).reshape(-1),
         ]
     )
-    packed = all_sum(packed, sizes, (C, X, Y, Z))
+    grad_rows, mix_core, expand_core, packed = sync(grad_rows, mix_core, expand_core, packed)
+    upper_parts = [
+        jnp.concatenate([sum(a), sum(b)], axis=-1) for a, b in zip(mix_core, expand_core)
+    ]
+    if square:
+        upper_held = corner_step(upper_parts, sizes, at)
+    else:
+        upper_sides = plain_square(upper_parts, sizes, at)
+    packed = all_sum(packed, sizes, C)
+
+    back = []
+    project_sums = []
+    bias_sums = []
+    for n in range(calls):
+        low, full, logs = fwd[n]
+        part = attention_back(projected, segment, full, logs, grad_rows, n * group, group)
+        if n == 0:
+            if square:
+                part, shrink_sides, upper_held, packed, grad_rows = sync(
+                    part, shrink_sides, upper_held, packed, grad_rows
+                )
+                upper_sides = side_step(upper_held, sizes)
+            shrink_z = spread_sum(sum(shrink_sides), sizes, Z, at[Z], 0)
+            packed = all_sum(packed, sizes, X)
+        back.append(part)
+        columns = jnp.concatenate([part[c] for c in range(3)], axis=-1)
+        bias_sums.append(jnp.sum(columns, axis=0, dtype=F32))
+        project_sums.append(core_send(dot(whole_tokens, columns, TN).astype(BF16), sizes, at))
+        if n == 0:
+            project_sums[0], grad_rows = sync(project_sums[0], grad_rows)
+            project_x = [spread_sum(sum(project_sums[0]), sizes, X, at[X], 1)]
+    projected_grad = jnp.concatenate([b[c] for c in range(3) for b in back], axis=-1)
+    bias_sum = jnp.concatenate([b.reshape(3, span) for b in bias_sums], axis=-1)
+    bias_sum = jnp.stack([bias_sum[0], bias_sum[2]]).reshape(-1)
+    bias_sum = all_sum(bias_sum, sizes, C)
+    token_parts = []
+    for k in range(n_t):
+        begin = (mine + k) % n_t * rows
+        part = dot(lax.dynamic_slice_in_dim(projected_grad, begin, rows, 0), proj, NT)
+        token_parts.append(part.astype(BF16) if k else part)
+    project_sums, project_x, upper_sides, shrink_z, token_parts, packed, bias_sum = sync(
+        project_sums, project_x, upper_sides, shrink_z, token_parts, packed, bias_sum
+    )
+    token_parts = [hop(p, sizes, Y, k).astype(F32) if k else p for k, p in enumerate(token_parts)]
+    packed = all_sum(packed, sizes, Y)
+    bias_sum = all_sum(bias_sum, sizes, X)
+    grad_shrink_weight = sum(shrink_z).astype(F32).T
+    owned_upper = spread_sum(sum(upper_sides), sizes, Z, at[Z], 0)
+    owned = [spread_sum(sum(project_x[0]), sizes, Z, at[Z], 0)]
+    for parts in project_sums[1:]:
+        total = sum_over(sum(parts), sizes, X, at[X], 1)
+        total, owned_upper, owned[0], packed, bias_sum = sync(
+            total, owned_upper, owned[0], packed, bias_sum
+        )
+        owned.append(spread_sum(total, sizes, Z, at[Z], 0))
+    owned = [sum(o).reshape(depth, 3, span) for o in owned]
+    grad_project_weight = jnp.transpose(
+        jnp.concatenate(owned, axis=-1), (1, 0, 2)
+    ).astype(F32)
+    owned = sum(owned_upper).astype(F32)
+    grad_output_weight = owned[:, :heads_width].T
+    grad_expand_weight = owned[:, heads_width:]
+
+    packed = all_sum(jnp.concatenate([packed, bias_sum]), sizes, Z)
+    grad_project_bias = packed[-bias_sum.shape[0] :].reshape(2, heads_width)
+    packed = packed[: -bias_sum.shape[0]]
     (
         grad_second_gain,
         grad_second_shift,
@@ -554,21 +603,7 @@
         grad_output_bias,
     ) = (packed[i * width : (i + 1) * width] for i in range(6))
     grad_expand_bias = pick(packed[6 * width :].reshape(n_t, hidden), mine, 0)
-
-    proj_cube = proj.reshape(width, 3, heads_width)
-    token_grad = grad_r1
-    for k in range(n_t):
-        begin = (mine + k) % n_t * rows
-        part = lax.dot_general(
-            lax.dynamic_slice_in_dim(projected_grad, begin, rows, 1),
-            proj_cube,
-            (((0, 2), (1, 2)), ((), ())),
-            preferred_element_type=F32,
-        )
-        if k:
-            part = hop(part.astype(BF16), sizes, Y, k).astype(F32)
-        token_grad = token_grad + part
-    grad_tokens = token_grad.astype(BF16)
+    grad_tokens = (grad_r1 + sum(token_parts)).astype(BF16)
     return (
         layer_output,
         grad_tokens,

time: 569 us -> 451 us (0.79)
  waiting for transfers between devices: 291 us -> 128 us
  starting transfers between devices: 56.6 us -> 96.7 us
  other arithmetic: 24.1 us -> 41.4 us
  local copies, waits for them, and re-layouts: 60.2 us -> 48.4 us
  matrix products: 84.3 us -> 78.3 us
    ppermute x90 -> x86, waiting for transfers between devices: 291 us -> 128 us  [hop(): return lax.ppermute(value, ALL, pairs)]
    ppermute x90 -> x86, starting transfers between devices: 56.6 us -> 96.7 us  [hop(): return lax.ppermute(value, ALL, pairs)]
    dynamic_update_slice x40 -> x48, local copies, waits for them, and re-layouts: 16.2 us -> 2.21 us  [arrange(): out[target] = lax.dynamic_update_slice(out[target], piece, start)]
    another operation x9 -> x12, local copies, waits for them, and re-layouts: 13.4 us -> 2.55 us  [the longest x1 10.1 us: on_device(): proj_cube = proj.reshape(width, 3, heads_width)]
    unnamed x134 -> x140, local copies, waits for them, and re-layouts: 6.89 us -> 16.8 us
    add x31 -> x22, other arithmetic: 11.2 us -> 15.3 us  [the longest x2 4.73 us: on_device(): shrink_parts = [sum(parts) for parts in shrink_core]]
    dot_general x22 -> x23, matrix products: 79.6 us -> 78.3 us  [dot(): return lax.dot_general(a, b, (dims, ((), ())), preferred_element_type=F32)]
    pallas_call x1 -> x2, Pallas kernels: 19.8 us -> 20.3 us  [attention(): pl.pallas_call(attend_kernel, grid=(count,), in_specs=[block(third(c * pa...]
  transfers between devices with their start and end apart: 90 -> 86, of which waited for: 44 -> 30; matrix products, arithmetic and copies ran while one was open for 23% -> 29% of each run, Pallas kernels for 6% -> 10%
where the time goes in v3:
time: 451 us; the launch traced here: 442 us
  waiting for transfers between devices  128 us (28%)
  starting transfers between devices  96.7 us (21%)
  matrix products  78.3 us (17%)
  local copies, waits for them, and re-layouts  48.4 us (11%)
  Pallas kernels  45.7 us (10%)
  other arithmetic  41.4 us (9%)
    ppermute x86, waiting for transfers between devices, hop(): return lax.ppermute(value, ALL, pairs)  128 us
    ppermute x86, starting transfers between devices, hop(): return lax.ppermute(value, ALL, pairs)  96.7 us
    dot_general x23, matrix products, dot(): return lax.dot_general(a, b, (dims, ((), ())), preferred_element_type=F32)  78.3 us
    pallas_call x2, Pallas kernels, attention_back(): pl.pallas_call(attend_back_kernel, grid=(count,), in_specs=[block(third(c...  25.4 us
    pallas_call x2, Pallas kernels, attention(): pl.pallas_call(attend_kernel, grid=(count,), in_specs=[block(third(c * pa...  20.3 us
    unnamed x140, local copies, waits for them, and re-layouts  16.8 us
    squeeze x17, local copies, waits for them, and re-layouts, pick(): return lax.dynamic_index_in_dim(value, index, axis, keepdims=False)  10.1 us
  transfers between devices with their start and end apart: 86, of which 30 were waited for; matrix products, arithmetic and copies ran while one was open for 29% of the time, Pallas kernels for 10%

profile of v3, /device:TPU:0, one launch (start us, length us, event | category | flops | bytes accessed | tf_op | source)
XLA Modules:
  0.0 442.0 jit_solution(16211379443420417250)
XLA Ops:
  20.6 4.3 collective-permute-done.8
  25.3 7.0 %collective-permute-done.2 = bf16[2,64,768]{2,1,0:T(8,128)(2,1)S(1)} collective-permute-done((bf16[2,64,768]{2,1,0:T(8,128)(2,1)S(1)}, bf16[2,64,768]{2,1,0:T(8,128)(2,1)S(1)}, u32[]{:S(2)}, u32[]{:S(2)}) %collective-permute-start.2) | collective-permute-done | bytes 196640 | tf_op jit(solution)/shard_map/ppermute | solution.py:50
  48.3 3.6 add_convert_fusion.q_ref.k_ref.v_ref
  52.0 10.0 %shard_map.254 = (bf16[1024,256]{1,0:T(8,128)(2,1)S(1)}, f32[1024,256]{1,0:T(8,128)S(1)}, f32[2,2,1024]{2,1,0:T(2,128)S(1)}) custom-call(bf16[1024,1536]{1,0:T(8,128)(2,1)S(1)} %add_convert_fusion.q_ref.k_ref.v_ref, bf16[1024,1536]{1,0:T(8,128)(2,1)S(1)} %add_convert_fusion.q_ref.k_ref.v_ref, bf16[1024,1536]{1,0:T(8,128)(2,1)S(1)} %add_convert_fusion.q_ref.k_ref.v_ref, ...), custom_call_target="tpu_custom_call" | custom-call | flops 4294967296 | bytes 4194304 | tf_op jit(solution)/shard_map/pallas_call | solution.py:335
  69.1 10.3 %shard_map.255 = (bf16[1024,256]{1,0:T(8,128)(2,1)S(1)}, f32[1024,256]{1,0:T(8,128)S(1)}, f32[2,2,1024]{2,1,0:T(2,128)S(1)}) custom-call(bf16[1024,1536]{1,0:T(8,128)(2,1)S(1)} %add_convert_fusion.q_ref.k_ref.v_ref, bf16[1024,1536]{1,0:T(8,128)(2,1)S(1)} %add_convert_fusion.q_ref.k_ref.v_ref, bf16[1024,1536]{1,0:T(8,128)(2,1)S(1)} %add_convert_fusion.q_ref.k_ref.v_ref, ...), custom_call_target="tpu_custom_call" | custom-call | flops 4294967296 | bytes 4194304 | tf_op jit(solution)/shard_map/pallas_call | solution.py:335
  81.9 7.5 %collective-permute-start.18 = (bf16[64,2048]{1,0:T(8,128)(2,1)S(1)}, bf16[64,2048]{1,0:T(8,128)(2,1)S(1)}, u32[]{:S(2)}, u32[]{:S(2)}) collective-permute-start(bf16[64,2048]{1,0:T(8,128)(2,1)S(1)} %bitcast.496), channel_id=1, source_target_pairs={{0,8},{1,9},{2,10},{3,11},{4,12},{5,13},{6,14},{7,15},{8,16},{9,17... | collective-permute-start | bytes 786440 | tf_op jit(solution)/shard_map/ppermute | solution.py:50
  89.4 5.5 %collective-permute-done.14 = bf16[4,64,1280]{2,1,0:T(8,128)(2,1)S(1)} collective-permute-done((bf16[4,64,1280]{2,1,0:T(8,128)(2,1)S(1)}, bf16[4,64,1280]{2,1,0:T(8,128)(2,1)S(1)}, u32[]{:S(2)}, u32[]{:S(2)}) %collective-permute-start.14) | collective-permute-done | bytes 655392 | tf_op jit(solution)/shard_map/ppermute | solution.py:50
  95.0 6.6 %collective-permute-start.19 = (bf16[64,2048]{1,0:T(8,128)(2,1)S(1)}, bf16[64,2048]{1,0:T(8,128)(2,1)S(1)}, u32[]{:S(2)}, u32[]{:S(2)}) collective-permute-start(bf16[64,2048]{1,0:T(8,128)(2,1)S(1)} %bitcast.497), channel_id=1, source_target_pairs={{0,16},{1,17},{2,18},{3,19},{4,20},{5,21},{6,22},{7,23},{8,24},{9,... | collective-permute-start | bytes 786440 | tf_op jit(solution)/shard_map/ppermute | solution.py:50
  101.6 3.4 collective-permute-start.20
  108.5 5.9 %collective-permute-done.19 = bf16[64,2048]{1,0:T(8,128)(2,1)S(1)} collective-permute-done((bf16[64,2048]{1,0:T(8,128)(2,1)S(1)}, bf16[64,2048]{1,0:T(8,128)(2,1)S(1)}, u32[]{:S(2)}, u32[]{:S(2)}) %collective-permute-start.19) | collective-permute-done | bytes 262176 | tf_op jit(solution)/shard_map/ppermute | solution.py:50
  115.9 4.0 collective-permute-done.17
  122.6 10.9 %collective-permute-done.24 = bf16[4,64,1280]{2,1,0:T(8,128)(2,1)S(1)} collective-permute-done((bf16[4,64,1280]{2,1,0:T(8,128)(2,1)S(1)}, bf16[4,64,1280]{2,1,0:T(8,128)(2,1)S(1)}, u32[]{:S(2)}, u32[]{:S(2)}) %collective-permute-start.24) | collective-permute-done | bytes 655392 | tf_op jit(solution)/shard_map/ppermute | solution.py:50
  140.3 12.6 %multiply_convert_fusion.3 = (bf16[512,2048]{1,0:T(8,128)(2,1)S(1)}, f32[512,2048]{1,0:T(8,128)S(1)}, f32[512,2048]{1,0:T(8,128)}) fusion(f32[2048]{0:T(1024)S(1)} %copy-done.51, bf16[512,1024]{1,0:T(8,128)(2,1)S(1)} %fusion.29, bf16[1024,2048]{1,0:T(8,128)(2,1)S(1)} %bitcast.475), kind=kOutput, calls=%fused_computation.36 | convolution fusion | flops 2215641088 | bytes 15736832 | tf_op jit(solution)/shard_map/dot_general | solution.py:243
  154.5 3.8 collective-permute-done.29
  161.4 13.2 %multiply_convert_fusion.2 = (bf16[512,2048]{1,0:T(8,128)(2,1)S(1)}, f32[512,2048]{1,0:T(8,128)}, f32[512,2048]{1,0:T(8,128)}) fusion(f32[2048]{0:T(1024)S(1)} %collective-permute-done.39, bf16[512,1024]{1,0:T(8,128)(2,1)S(1)} %fusion.29, bf16[1024,2048]{1,0:T(8,128)(2,1)S(1)} %bitcast.473), kind=kOutput, calls=%fused_computation.23 | convolution fusion | flops 2215641088 | bytes 15736832 | tf_op jit(solution)/shard_map/dot_general | solution.py:243
  178.5 3.8 fusion.80
  182.6 8.0 %collective-permute-done.44 = bf16[4,64,1024]{2,1,0:T(8,128)(2,1)S(1)} collective-permute-done((bf16[4,64,1024]{2,1,0:T(8,128)(2,1)S(1)}, bf16[4,64,1024]{2,1,0:T(8,128)(2,1)S(1)}, u32[]{:S(2)}, u32[]{:S(2)}) %collective-permute-start.44) | collective-permute-done | bytes 524320 | tf_op jit(solution)/shard_map/ppermute | solution.py:50
  210.2 4.5 %convert_reduce_fusion.1 = (f32[2048]{0:T(1024)S(1)}, bf16[512,2048]{1,0:T(8,128)(2,1)}) fusion(f32[512,2048]{1,0:T(8,128)S(1)} %get-tuple-element.276, f32[512,2048]{1,0:T(8,128)S(1)} %copy-done.54, f32[2048]{0:T(1024)S(1)} %copy-done.51, bf16[512,1024]{1,0:T(8,128)(2,1)S(1)} %get-tuple-element.270, bf16[1024,2048]{1,0:T(8,128)(2,1)S(1)} %bitcast.480), kind=kOutput, calls=%fused_computation.20 | convolution fusion | flops 2160064512 | bytes 15745024 | tf_op jit(solution)/shard_map/dot_general | solution.py:243
  214.7 4.4 %convert_reduce_fusion = (f32[2048]{0:T(1024)S(1)}, bf16[512,2048]{1,0:T(8,128)(2,1)}) fusion(f32[512,2048]{1,0:T(8,128)S(1)} %copy-done.55, f32[512,2048]{1,0:T(8,128)S(1)} %copy-done.56, f32[2048]{0:T(1024)S(1)} %collective-permute-done.39, bf16[512,1024]{1,0:T(8,128)(2,1)S(1)} %get-tuple-element.270, bf16[1024,2048]{1,0:T(8,128)(2,1)S(1)} %bitcast.478), kind=kOutput, calls=%fused_computation.19 | convolution fusion | flops 2160064512 | bytes 15745024 | tf_op jit(solution)/shard_map/dot_general | solution.py:243
  219.8 5.3 %fusion.81 = f32[512,1024]{1,0:T(8,128)S(1)} fusion(bf16[512,2048]{1,0:T(8,128)(2,1)} %get-tuple-element.371, bf16[1024,2048]{1,0:T(8,128)(2,1)} %bitcast.476), kind=kOutput, calls=%fused_computation.314 | convolution fusion | flops 2147483648 | bytes 8388608 | tf_op jit(solution)/shard_map/dot_general | solution.py:243
  246.9 3.8 collective-permute-done.51
  256.5 10.6 %collective-permute-done.48 = bf16[512,512]{1,0:T(8,128)(2,1)S(1)} collective-permute-done((bf16[512,512]{1,0:T(8,128)(2,1)S(1)}, bf16[512,512]{1,0:T(8,128)(2,1)S(1)}, u32[]{:S(2)}, u32[]{:S(2)}) %collective-permute-start.48) | collective-permute-done | bytes 524320 | tf_op jit(solution)/shard_map/ppermute | solution.py:50
  273.3 12.6 %shard_map.256 = bf16[3,1024,256]{2,1,0:T(8,128)(2,1)S(1)} custom-call(bf16[1024,1536]{1,0:T(8,128)(2,1)} %copy-done.7, bf16[1024,1536]{1,0:T(8,128)(2,1)} %copy-done.7, bf16[1024,1536]{1,0:T(8,128)(2,1)} %copy-done.7, s32[1024,1]{1,0:T(8,128)S(1)} %copy-done.3, s32[1,1024]{1,0:T(1,128)S(1)} %bitcast.465, f32[1024,256]{1,0:T(8,128)S(1)} %get-tuple-element.163.full_ref, ...), custom_call_target="tpu_custom_call" | custom-call | flops 10737418240 | bytes 5242880 | tf_op jit(solution)/shard_map/pallas_call | solution.py:367
  288.2 5.3 %collective-permute-done.56 = bf16[4,64,2048]{2,1,0:T(8,128)(2,1)} collective-permute-done((bf16[4,64,2048]{2,1,0:T(8,128)(2,1)}, bf16[4,64,2048]{2,1,0:T(8,128)(2,1)}, u32[]{:S(2)}, u32[]{:S(2)}) %collective-permute-start.56) | collective-permute-done | bytes 1048608 | tf_op jit(solution)/shard_map/ppermute | solution.py:50
  294.2 12.3 %collective-permute-done.57 = bf16[4,64,1280]{2,1,0:T(8,128)(2,1)S(1)} collective-permute-done((bf16[4,64,1280]{2,1,0:T(8,128)(2,1)S(1)}, bf16[4,64,1280]{2,1,0:T(8,128)(2,1)S(1)}, u32[]{:S(2)}, u32[]{:S(2)}) %collective-permute-start.57) | collective-permute-done | bytes 655392 | tf_op jit(solution)/shard_map/ppermute | solution.py:50
  315.8 3.4 collective-permute-start.66
  330.6 12.8 %shard_map.257 = bf16[3,1024,256]{2,1,0:T(8,128)(2,1)S(1)} custom-call(bf16[1024,1536]{1,0:T(8,128)(2,1)} %copy-done.7, bf16[1024,1536]{1,0:T(8,128)(2,1)} %copy-done.7, bf16[1024,1536]{1,0:T(8,128)(2,1)} %copy-done.7, s32[1024,1]{1,0:T(8,128)S(1)} %copy-done.4, s32[1,1024]{1,0:T(1,128)S(1)} %bitcast.466, f32[1024,256]{1,0:T(8,128)S(1)} %copy-done.9, ...), custom_call_target="tpu_custom_call" | custom-call | flops 10737418240 | bytes 5242880 | tf_op jit(solution)/shard_map/pallas_call | solution.py:367
  345.0 3.2 convolution_convert_fusion.4
  367.7 3.5 collective-permute-done.62
  377.1 3.3 collective-permute-start.73
  385.7 4.5 %collective-permute-done.71 = bf16[4,64,768]{2,1,0:T(8,128)(2,1)S(1)} collective-permute-done((bf16[4,64,768]{2,1,0:T(8,128)(2,1)S(1)}, bf16[4,64,768]{2,1,0:T(8,128)(2,1)S(1)}, u32[]{:S(2)}, u32[]{:S(2)}) %collective-permute-start.71) | collective-permute-done | bytes 393248 | tf_op jit(solution)/shard_map/ppermute | solution.py:50
  391.2 21.4 %collective-permute-done.76 = bf16[64,768]{1,0:T(8,128)(2,1)S(1)} collective-permute-done((bf16[64,768]{1,0:T(8,128)(2,1)S(1)}, bf16[64,768]{1,0:T(8,128)(2,1)S(1)}, u32[]{:S(2)}, u32[]{:S(2)}) %collective-permute-start.76) | collective-permute-done | bytes 98336 | tf_op jit(solution)/shard_map/ppermute | solution.py:50
  (493 shorter events, 207.2 us)
Async XLA Ops:
  10.1 24.1 %collective-permute-start.4 = (bf16[512,1024]{1,0:T(8,128)(2,1)}, bf16[512,1024]{1,0:T(8,128)(2,1)}, u32[]{:S(2)}, u32[]{:S(2)}) collective-permute-start(bf16[512,1024]{1,0:T(8,128)(2,1)} %param.15), channel_id=1, source_target_pairs={{0,1},{1,0},{2,3},{3,2},{4,5},{5,4},{6,7},{7,6},{8,9},{9,8},{10,11... | collective-permute-start | bytes 3145736 | tf_op jit(solution)/shard_map/ppermute | solution.py:50
  37.6 24.4 %collective-permute-start.10 = (bf16[64,2560]{1,0:T(8,128)(2,1)S(1)}, bf16[64,2560]{1,0:T(8,128)(2,1)S(1)}, u32[]{:S(2)}, u32[]{:S(2)}) collective-permute-start(bf16[64,2560]{1,0:T(8,128)(2,1)S(1)} %pad_maximum_fusion.10), channel_id=1, source_target_pairs={{0,8},{1,9},{2,10},{3,11},{4,12},{5,13},{6,14},{7,15},{8,16},{9,17... | collective-permute-start | bytes 983048 | tf_op jit(solution)/shard_map/ppermute | solution.py:50
  40.5 23.5 %collective-permute-start.11 = (bf16[64,2560]{1,0:T(8,128)(2,1)S(1)}, bf16[64,2560]{1,0:T(8,128)(2,1)S(1)}, u32[]{:S(2)}, u32[]{:S(2)}) collective-permute-start(bf16[64,2560]{1,0:T(8,128)(2,1)S(1)} %pad_maximum_fusion.10), channel_id=1, source_target_pairs={{0,16},{1,17},{2,18},{3,19},{4,20},{5,21},{6,22},{7,23},{8,24},{9,... | collective-permute-start | bytes 983048 | tf_op jit(solution)/shard_map/ppermute | solution.py:50
  42.0 22.0 %collective-permute-start.12 = (bf16[64,2560]{1,0:T(8,128)(2,1)S(1)}, bf16[64,2560]{1,0:T(8,128)(2,1)S(1)}, u32[]{:S(2)}, u32[]{:S(2)}) collective-permute-start(bf16[64,2560]{1,0:T(8,128)(2,1)S(1)} %pad_maximum_fusion.10), channel_id=1, source_target_pairs={{0,24},{1,25},{2,26},{3,27},{4,28},{5,29},{6,30},{7,31},{8,0},{9,1... | collective-permute-start | bytes 983048 | tf_op jit(solution)/shard_map/ppermute | solution.py:50
  64.9 36.7 %collective-permute-start.15 = (bf16[4,64,1280]{2,1,0:T(8,128)(2,1)S(1)}, bf16[4,64,1280]{2,1,0:T(8,128)(2,1)S(1)}, u32[]{:S(2)}, u32[]{:S(2)}) collective-permute-start(bf16[4,64,1280]{2,1,0:T(8,128)(2,1)S(1)} %get-tuple-element.340), channel_id=1, source_target_pairs={{0,1},{1,0},{2,3},{3,2},{4,5},{5,4},{6,7},{7,6},{8,9},{9,8},{10,11... | collective-permute-start | bytes 1966088 | tf_op jit(solution)/shard_map/ppermute | solution.py:50
  66.4 28.6 %collective-permute-start.14 = (bf16[4,64,1280]{2,1,0:T(8,128)(2,1)S(1)}, bf16[4,64,1280]{2,1,0:T(8,128)(2,1)S(1)}, u32[]{:S(2)}, u32[]{:S(2)}) collective-permute-start(bf16[4,64,1280]{2,1,0:T(8,128)(2,1)S(1)} %get-tuple-element.339), channel_id=1, source_target_pairs={{0,4},{1,5},{2,6},{3,7},{4,0},{5,1},{6,2},{7,3},{8,12},{9,13},{10,... | collective-permute-start | bytes 1966088 | tf_op jit(solution)/shard_map/ppermute | solution.py:50
  67.9 37.1 %collective-permute-start.16 = (bf16[4,64,1280]{2,1,0:T(8,128)(2,1)S(1)}, bf16[4,64,1280]{2,1,0:T(8,128)(2,1)S(1)}, u32[]{:S(2)}, u32[]{:S(2)}) collective-permute-start(bf16[4,64,1280]{2,1,0:T(8,128)(2,1)S(1)} %get-tuple-element.339), channel_id=1, source_target_pairs={{0,1},{1,0},{2,3},{3,2},{4,5},{5,4},{6,7},{7,6},{8,9},{9,8},{10,11... | collective-permute-start | bytes 1966088 | tf_op jit(solution)/shard_map/ppermute | solution.py:50
  68.4 36.7 %collective-permute-start.21 = (bf16[4,64,1280]{2,1,0:T(8,128)(2,1)S(1)}, bf16[4,64,1280]{2,1,0:T(8,128)(2,1)S(1)}, u32[]{:S(2)}, u32[]{:S(2)}) collective-permute-start(bf16[4,64,1280]{2,1,0:T(8,128)(2,1)S(1)} %get-tuple-element.340), channel_id=1, source_target_pairs={{0,2},{1,3},{2,0},{3,1},{4,6},{5,7},{6,4},{7,5},{8,10},{9,11},{10,... | collective-permute-start | bytes 1966088 | tf_op jit(solution)/shard_map/ppermute | solution.py:50
  81.9 26.1 %collective-permute-start.18 = (bf16[64,2048]{1,0:T(8,128)(2,1)S(1)}, bf16[64,2048]{1,0:T(8,128)(2,1)S(1)}, u32[]{:S(2)}, u32[]{:S(2)}) collective-permute-start(bf16[64,2048]{1,0:T(8,128)(2,1)S(1)} %bitcast.496), channel_id=1, source_target_pairs={{0,8},{1,9},{2,10},{3,11},{4,12},{5,13},{6,14},{7,15},{8,16},{9,17... | collective-permute-start | bytes 786440 | tf_op jit(solution)/shard_map/ppermute | solution.py:50
  119.9 33.0 %collective-permute-start.37 = (bf16[4,64,1280]{2,1,0:T(8,128)(2,1)S(1)}, bf16[4,64,1280]{2,1,0:T(8,128)(2,1)S(1)}, u32[]{:S(2)}, u32[]{:S(2)}) collective-permute-start(bf16[4,64,1280]{2,1,0:T(8,128)(2,1)S(1)} %collective-permute-done.16), channel_id=1, source_target_pairs={{0,4},{1,5},{2,6},{3,7},{4,0},{5,1},{6,2},{7,3},{8,12},{9,13},{10,... | collective-permute-start | bytes 1966088 | tf_op jit(solution)/shard_map/ppermute | solution.py:50
  120.9 33.6 %collective-permute-start.28 = (bf16[4,64,1024]{2,1,0:T(8,128)(2,1)S(1)}, bf16[4,64,1024]{2,1,0:T(8,128)(2,1)S(1)}, u32[]{:S(2)}, u32[]{:S(2)}) collective-permute-start(bf16[4,64,1024]{2,1,0:T(8,128)(2,1)S(1)} %get-tuple-element.154), channel_id=1, source_target_pairs={{0,4},{1,5},{2,6},{3,7},{4,0},{5,1},{6,2},{7,3},{8,12},{9,13},{10,... | collective-permute-start | bytes 1572872 | tf_op jit(solution)/shard_map/ppermute | solution.py:50
  133.6 24.8 %collective-permute-start.30 = (bf16[4,64,1024]{2,1,0:T(8,128)(2,1)S(1)}, bf16[4,64,1024]{2,1,0:T(8,128)(2,1)S(1)}, u32[]{:S(2)}, u32[]{:S(2)}) collective-permute-start(bf16[4,64,1024]{2,1,0:T(8,128)(2,1)S(1)} %get-tuple-element.154), channel_id=1, source_target_pairs={{0,1},{1,0},{2,3},{3,2},{4,5},{5,4},{6,7},{7,6},{8,9},{9,8},{10,11... | collective-permute-start | bytes 1572872 | tf_op jit(solution)/shard_map/ppermute | solution.py:50
  135.4 23.0 %collective-permute-start.29 = (bf16[4,64,1024]{2,1,0:T(8,128)(2,1)S(1)}, bf16[4,64,1024]{2,1,0:T(8,128)(2,1)S(1)}, u32[]{:S(2)}, u32[]{:S(2)}) collective-permute-start(bf16[4,64,1024]{2,1,0:T(8,128)(2,1)S(1)} %get-tuple-element.155), channel_id=1, source_target_pairs={{0,4},{1,5},{2,6},{3,7},{4,0},{5,1},{6,2},{7,3},{8,12},{9,13},{10,... | collective-permute-start | bytes 1572872 | tf_op jit(solution)/shard_map/ppermute | solution.py:50
  137.2 21.3 %collective-permute-start.31 = (bf16[4,64,1024]{2,1,0:T(8,128)(2,1)S(1)}, bf16[4,64,1024]{2,1,0:T(8,128)(2,1)S(1)}, u32[]{:S(2)}, u32[]{:S(2)}) collective-permute-start(bf16[4,64,1024]{2,1,0:T(8,128)(2,1)S(1)} %get-tuple-element.155), channel_id=1, source_target_pairs={{0,1},{1,0},{2,3},{3,2},{4,5},{5,4},{6,7},{7,6},{8,9},{9,8},{10,11... | collective-permute-start | bytes 1572872 | tf_op jit(solution)/shard_map/ppermute | solution.py:50
  158.5 23.8 %collective-permute-start.42 = (bf16[4,64,1024]{2,1,0:T(8,128)(2,1)S(1)}, bf16[4,64,1024]{2,1,0:T(8,128)(2,1)S(1)}, u32[]{:S(2)}, u32[]{:S(2)}) collective-permute-start(bf16[4,64,1024]{2,1,0:T(8,128)(2,1)S(1)} %collective-permute-done.28), channel_id=1, source_target_pairs={{0,1},{1,0},{2,3},{3,2},{4,5},{5,4},{6,7},{7,6},{8,9},{9,8},{10,11... | collective-permute-start | bytes 1572872 | tf_op jit(solution)/shard_map/ppermute | solution.py:50
  160.0 22.5 %collective-permute-start.40 = (bf16[4,64,1024]{2,1,0:T(8,128)(2,1)S(1)}, bf16[4,64,1024]{2,1,0:T(8,128)(2,1)S(1)}, u32[]{:S(2)}, u32[]{:S(2)}) collective-permute-start(bf16[4,64,1024]{2,1,0:T(8,128)(2,1)S(1)} %collective-permute-done.30), channel_id=1, source_target_pairs={{0,2},{1,3},{2,0},{3,1},{4,6},{5,7},{6,4},{7,5},{8,10},{9,11},{10,... | collective-permute-start | bytes 1572872 | tf_op jit(solution)/shard_map/ppermute | solution.py:50
  206.4 21.7 %collective-permute-start.47 = (bf16[4,2,64,2048]{3,2,1,0:T(8,128)(2,1)}, bf16[4,2,64,2048]{3,2,1,0:T(8,128)(2,1)}, u32[]{:S(2)}, u32[]{:S(2)}) collective-permute-start(bf16[4,2,64,2048]{3,2,1,0:T(8,128)(2,1)} %get-tuple-element.282), channel_id=1, source_target_pairs={{0,2},{1,3},{2,0},{3,1},{4,6},{5,7},{6,4},{7,5},{8,10},{9,11},{10,... | collective-permute-start | bytes 6291464 | tf_op jit(solution)/shard_map/ppermute | solution.py:50
  243.9 23.8 %collective-permute-start.50 = (bf16[4,2,64,512]{3,2,1,0:T(8,128)(2,1)S(1)}, bf16[4,2,64,512]{3,2,1,0:T(8,128)(2,1)S(1)}, u32[]{:S(2)}, u32[]{:S(2)}) collective-permute-start(bf16[4,2,64,512]{3,2,1,0:T(8,128)(2,1)S(1)} %get-tuple-element.325), channel_id=1, source_target_pairs={{0,2},{1,3},{2,0},{3,1},{4,6},{5,7},{6,4},{7,5},{8,10},{9,11},{10,... | collective-permute-start | bytes 1572872 | tf_op jit(solution)/shard_map/ppermute | solution.py:50
  267.1 26.4 %collective-permute-start.56 = (bf16[4,64,2048]{2,1,0:T(8,128)(2,1)}, bf16[4,64,2048]{2,1,0:T(8,128)(2,1)}, u32[]{:S(2)}, u32[]{:S(2)}) collective-permute-start(bf16[4,64,2048]{2,1,0:T(8,128)(2,1)} %pad_maximum_fusion.7), channel_id=1, source_target_pairs={{0,1},{1,0},{2,3},{3,2},{4,5},{5,4},{6,7},{7,6},{8,9},{9,8},{10,11... | collective-permute-start | bytes 3145736 | tf_op jit(solution)/shard_map/ppermute | solution.py:50
  267.7 26.5 %collective-permute-start.55 = (bf16[4,64,2048]{2,1,0:T(8,128)(2,1)}, bf16[4,64,2048]{2,1,0:T(8,128)(2,1)}, u32[]{:S(2)}, u32[]{:S(2)}) collective-permute-start(bf16[4,64,2048]{2,1,0:T(8,128)(2,1)} %pad_maximum_fusion.6), channel_id=1, source_target_pairs={{0,4},{1,5},{2,6},{3,7},{4,0},{5,1},{6,2},{7,3},{8,12},{9,13},{10,... | collective-permute-start | bytes 3145736 | tf_op jit(solution)/shard_map/ppermute | solution.py:50
  271.2 35.3 %collective-permute-start.57 = (bf16[4,64,1280]{2,1,0:T(8,128)(2,1)S(1)}, bf16[4,64,1280]{2,1,0:T(8,128)(2,1)S(1)}, u32[]{:S(2)}, u32[]{:S(2)}) collective-permute-start(bf16[4,64,1280]{2,1,0:T(8,128)(2,1)S(1)} %get-tuple-element.313), channel_id=1, source_target_pairs={{0,4},{1,5},{2,6},{3,7},{4,0},{5,1},{6,2},{7,3},{8,12},{9,13},{10,... | collective-permute-start | bytes 1966088 | tf_op jit(solution)/shard_map/ppermute | solution.py:50
  271.8 34.7 %collective-permute-start.58 = (bf16[4,64,1280]{2,1,0:T(8,128)(2,1)S(1)}, bf16[4,64,1280]{2,1,0:T(8,128)(2,1)S(1)}, u32[]{:S(2)}, u32[]{:S(2)}) collective-permute-start(bf16[4,64,1280]{2,1,0:T(8,128)(2,1)S(1)} %get-tuple-element.312), channel_id=1, source_target_pairs={{0,1},{1,0},{2,3},{3,2},{4,5},{5,4},{6,7},{7,6},{8,9},{9,8},{10,11... | collective-permute-start | bytes 1966088 | tf_op jit(solution)/shard_map/ppermute | solution.py:50
  313.9 44.9 %collective-permute-start.65 = (bf16[64,2048]{1,0:T(8,128)(2,1)}, bf16[64,2048]{1,0:T(8,128)(2,1)}, u32[]{:S(2)}, u32[]{:S(2)}) collective-permute-start(bf16[64,2048]{1,0:T(8,128)(2,1)} %get-tuple-element.316), channel_id=1, source_target_pairs={{0,8},{1,9},{2,10},{3,11},{4,12},{5,13},{6,14},{7,15},{8,16},{9,17... | collective-permute-start | bytes 786440 | tf_op jit(solution)/shard_map/ppermute | solution.py:50
  315.8 43.1 %collective-permute-start.66 = (bf16[64,2048]{1,0:T(8,128)(2,1)}, bf16[64,2048]{1,0:T(8,128)(2,1)}, u32[]{:S(2)}, u32[]{:S(2)}) collective-permute-start(bf16[64,2048]{1,0:T(8,128)(2,1)} %get-tuple-element.315), channel_id=1, source_target_pairs={{0,16},{1,17},{2,18},{3,19},{4,20},{5,21},{6,22},{7,23},{8,24},{9,... | collective-permute-start | bytes 786440 | tf_op jit(solution)/shard_map/ppermute | solution.py:50
  320.5 50.7 %collective-permute-start.64 = (bf16[4,64,2560]{2,1,0:T(8,128)(2,1)}, bf16[4,64,2560]{2,1,0:T(8,128)(2,1)}, u32[]{:S(2)}, u32[]{:S(2)}) collective-permute-start(bf16[4,64,2560]{2,1,0:T(8,128)(2,1)} %pad_maximum_fusion.4), channel_id=1, source_target_pairs={{0,1},{1,0},{2,3},{3,2},{4,5},{5,4},{6,7},{7,6},{8,9},{9,8},{10,11... | collective-permute-start | bytes 3932168 | tf_op jit(solution)/shard_map/ppermute | solution.py:50
  326.6 44.6 %collective-permute-start.63 = (bf16[4,64,2560]{2,1,0:T(8,128)(2,1)}, bf16[4,64,2560]{2,1,0:T(8,128)(2,1)}, u32[]{:S(2)}, u32[]{:S(2)}) collective-permute-start(bf16[4,64,2560]{2,1,0:T(8,128)(2,1)} %pad_maximum_fusion.3), channel_id=1, source_target_pairs={{0,4},{1,5},{2,6},{3,7},{4,0},{5,1},{6,2},{7,3},{8,12},{9,13},{10,... | collective-permute-start | bytes 3932168 | tf_op jit(solution)/shard_map/ppermute | solution.py:50
  376.7 37.2 %collective-permute-start.72 = (bf16[64,2560]{1,0:T(8,128)(2,1)S(1)}, bf16[64,2560]{1,0:T(8,128)(2,1)S(1)}, u32[]{:S(2)}, u32[]{:S(2)}) collective-permute-start(bf16[64,2560]{1,0:T(8,128)(2,1)S(1)} %get-tuple-element.306), channel_id=1, source_target_pairs={{0,8},{1,9},{2,10},{3,11},{4,12},{5,13},{6,14},{7,15},{8,16},{9,17... | collective-permute-start | bytes 983048 | tf_op jit(solution)/shard_map/ppermute | solution.py:50
  377.1 36.8 %collective-permute-start.73 = (bf16[64,2560]{1,0:T(8,128)(2,1)S(1)}, bf16[64,2560]{1,0:T(8,128)(2,1)S(1)}, u32[]{:S(2)}, u32[]{:S(2)}) collective-permute-start(bf16[64,2560]{1,0:T(8,128)(2,1)S(1)} %get-tuple-element.305), channel_id=1, source_target_pairs={{0,16},{1,17},{2,18},{3,19},{4,20},{5,21},{6,22},{7,23},{8,24},{9,... | collective-permute-start | bytes 983048 | tf_op jit(solution)/shard_map/ppermute | solution.py:50
  380.6 33.3 %collective-permute-start.74 = (bf16[64,2560]{1,0:T(8,128)(2,1)S(1)}, bf16[64,2560]{1,0:T(8,128)(2,1)S(1)}, u32[]{:S(2)}, u32[]{:S(2)}) collective-permute-start(bf16[64,2560]{1,0:T(8,128)(2,1)S(1)} %get-tuple-element.304), channel_id=1, source_target_pairs={{0,24},{1,25},{2,26},{3,27},{4,28},{5,29},{6,30},{7,31},{8,0},{9,1... | collective-permute-start | bytes 983048 | tf_op jit(solution)/shard_map/ppermute | solution.py:50
  383.6 28.9 %collective-permute-start.76 = (bf16[64,768]{1,0:T(8,128)(2,1)S(1)}, bf16[64,768]{1,0:T(8,128)(2,1)S(1)}, u32[]{:S(2)}, u32[]{:S(2)}) collective-permute-start(bf16[64,768]{1,0:T(8,128)(2,1)S(1)} %get-tuple-element.336), channel_id=1, source_target_pairs={{0,16},{1,17},{2,18},{3,19},{4,20},{5,21},{6,22},{7,23},{8,24},{9,... | collective-permute-start | bytes 294920 | tf_op jit(solution)/shard_map/ppermute | solution.py:50
  390.2 23.7 %collective-permute-start.77 = (bf16[64,768]{1,0:T(8,128)(2,1)S(1)}, bf16[64,768]{1,0:T(8,128)(2,1)S(1)}, u32[]{:S(2)}, u32[]{:S(2)}) collective-permute-start(bf16[64,768]{1,0:T(8,128)(2,1)S(1)} %get-tuple-element.335), channel_id=1, source_target_pairs={{0,24},{1,25},{2,26},{3,27},{4,28},{5,29},{6,30},{7,31},{8,0},{9,1... | collective-permute-start | bytes 294920 | tf_op jit(solution)/shard_map/ppermute | solution.py:50
  412.6 25.9 %collective-permute-start.70 = (bf16[512,1024]{1,0:T(8,128)(2,1)}, bf16[512,1024]{1,0:T(8,128)(2,1)S(1)}, u32[]{:S(2)}, u32[]{:S(2)}) collective-permute-start(bf16[512,1024]{1,0:T(8,128)(2,1)} %fusion.34), channel_id=1, source_target_pairs={{0,1},{1,0},{2,3},{3,2},{4,5},{5,4},{6,7},{7,6},{8,9},{9,8},{10,11... | collective-permute-start | bytes 3145736 | tf_op jit(solution)/shard_map/ppermute | solution.py:50
  (116 other events, 1192.9 us)

commit v4 on v3

--- a/solution.py
+++ b/solution.py
@@ -135,7 +135,7 @@
 
 
 def spread_sides(halves, sizes):
-    over_x = list(zip(*[fan(b, sizes, X) for b in halves]))
+    over_x = [list(p) for p in zip(*[fan(b, sizes, X) for b in halves])]
     if sizes[X] == 2 and sizes[Y] == 2:
         return over_x, [hop(b, sizes, Y) for b in halves]
     return over_x, []
@@ -144,7 +144,7 @@
 def spread_corner(over_x, over_y, sizes):
     if sizes[X] == 2 and sizes[Y] == 2:
         corner = [hop(over_x[1][0], sizes, Y), hop(over_y[1], sizes, X)]
-        return [list(over_x), [over_y, corner]]
+        return [over_x, [over_y, corner]]
     both = [list(zip(*[fan(b, sizes, Y) for b in piece])) for piece in over_x]
     return [[both[j][k] for j in range(sizes[X])] for k in range(sizes[Y])]
 
@@ -234,7 +234,7 @@
 
 
 def gelu_both(upper):
-    below = 0.5 * lax.erfc(upper * -(0.5**0.5))
+    below = 0.5 + 0.5 * lax.erf(upper * 0.5**0.5)
     density = jnp.exp(-0.5 * upper * upper) * 0.3989422804014327
     return upper * below, below + upper * density
 
@@ -449,15 +449,16 @@
     if calls == 2:
         fwd.append(attention(projected, segment, group, group))
     if square:
-        fwd[-1], upper_x[1], upper_y = sync(fwd[-1], upper_x[1], upper_y)
+        fwd[-1], upper_x[1], upper_y, shrink_z = sync(fwd[-1], upper_x[1], upper_y, shrink_z)
     by_rows = jnp.concatenate([f[0] for f in fwd], axis=1).reshape(n_t, rows, heads_width)
     mixed = [pick(by_rows, mine, 0)]
     for k in range(1, n_t):
         mixed.append(hop(pick(by_rows, (mine + k) % n_t, 0), sizes, Y, k))
 
     upper_pieces = spread_corner(upper_x, upper_y, sizes)
-    mixed, shrink_z = sync(mixed, shrink_z)
     shrink_x, shrink_y = spread_sides(stack_z(shrink_z, sizes, at), sizes)
+    if square:
+        mixed, shrink_x[1][0], shrink_y[1] = sync(mixed, shrink_x[1][0], shrink_y[1])
     gathered = assemble(upper_pieces, sizes, at, (heads_width, hidden))
     mix = [g[0] for g in gathered]
     expand = [g[1] for g in gathered]
@@ -466,13 +467,10 @@
     normed1 = unit1 * first_gain + first_shift
     low1 = normed1.astype(BF16)
     active, slope = [], []
-    low1_now = low1
     for w, b in zip(expand, expand_biases):
-        act, der = gelu_both(dot(low1_now, w, NN) + b)
+        act, der = gelu_both(dot(low1, w, NN) + b)
         active.append(act.astype(BF16))
         slope.append(der.astype(BF16))
-        if len(active) == 1:
-            active[0], low1_now, shrink_x, shrink_y = sync(active[0], low1, shrink_x, shrink_y)
     shrink_pieces = spread_corner(shrink_x, shrink_y, sizes)
     shrink = [g[0] for g in assemble(shrink_pieces, sizes, at, (hidden,))]
     branch = sum(dot(a, w, NT) for a, w in zip(active, shrink)) + shrink_bias
@@ -571,7 +569,7 @@
     project_sums, project_x, upper_sides, shrink_z, token_parts, packed, bias_sum = sync(
         project_sums, project_x, upper_sides, shrink_z, token_parts, packed, bias_sum
     )
-    token_parts = [hop(p, sizes, Y, k).astype(F32) if k else p for k, p in enumerate(token_parts)]
+    token_parts = [hop(p, sizes, Y, k) if k else p for k, p in enumerate(token_parts)]
     packed = all_sum(packed, sizes, Y)
     bias_sum = all_sum(bias_sum, sizes, X)
     grad_shrink_weight = sum(shrink_z).astype(F32).T
@@ -579,8 +577,8 @@
     owned = [spread_sum(sum(project_x[0]), sizes, Z, at[Z], 0)]
     for parts in project_sums[1:]:
         total = sum_over(sum(parts), sizes, X, at[X], 1)
-        total, owned_upper, owned[0], packed, bias_sum = sync(
-            total, owned_upper, owned[0], packed, bias_sum
+        total, owned_upper, owned[0], token_parts, packed, bias_sum = sync(
+            total, owned_upper, owned[0], token_parts, packed, bias_sum
         )
         owned.append(spread_sum(total, sizes, Z, at[Z], 0))
     owned = [sum(o).reshape(depth, 3, span) for o in owned]
@@ -603,7 +601,7 @@
         grad_output_bias,
     ) = (packed[i * width : (i + 1) * width] for i in range(6))
     grad_expand_bias = pick(packed[6 * width :].reshape(n_t, hidden), mine, 0)
-    grad_tokens = (grad_r1 + sum(token_parts)).astype(BF16)
+    grad_tokens = (grad_r1 + sum(p.astype(F32) for p in token_parts)).astype(BF16)
     return (
         layer_output,
         grad_tokens,

time: 451 us -> 429 us (0.951)
  matrix products: 78.3 us -> 57.3 us
  waiting for transfers between devices: 128 us -> 147 us
  starting transfers between devices: 96.7 us -> 90 us
  local copies, waits for them, and re-layouts: 48.4 us -> 41.7 us
  other arithmetic: 41.4 us -> 36.1 us
    dot_general x23, matrix products: 78.3 us -> 57.3 us  [dot(): return lax.dot_general(a, b, (dims, ((), ())), preferred_element_type=F32)]
    ppermute x86, waiting for transfers between devices: 128 us -> 147 us  [hop(): return lax.ppermute(value, ALL, pairs)]
    ppermute x86, starting transfers between devices: 96.7 us -> 90 us  [hop(): return lax.ppermute(value, ALL, pairs)]
    unnamed x140 -> x132, local copies, waits for them, and re-layouts: 16.8 us -> 14.9 us
  transfers between devices with their start and end apart: 86 -> 86, of which waited for: 30 -> 33; matrix products, arithmetic and copies ran while one was open for 29% -> 21% of each run, Pallas kernels for 10% -> 11%
where the time goes in v4:
time: 429 us; the launch traced here: 421 us
  waiting for transfers between devices  147 us (34%)
  starting transfers between devices  90 us (21%)
  matrix products  57.3 us (13%)
  Pallas kernels  45.5 us (11%)
  local copies, waits for them, and re-layouts  41.7 us (10%)
  other arithmetic  36.1 us (8%)
    ppermute x86, waiting for transfers between devices, hop(): return lax.ppermute(value, ALL, pairs)  147 us
    ppermute x86, starting transfers between devices, hop(): return lax.ppermute(value, ALL, pairs)  90 us
    dot_general x23, matrix products, dot(): return lax.dot_general(a, b, (dims, ((), ())), preferred_element_type=F32)  57.3 us
    pallas_call x2, Pallas kernels, attention_back(): pl.pallas_call(attend_back_kernel, grid=(count,), in_specs=[block(third(c...  25.4 us
    pallas_call x2, Pallas kernels, attention(): pl.pallas_call(attend_kernel, grid=(count,), in_specs=[block(third(c * pa...  20.1 us
    unnamed x132, local copies, waits for them, and re-layouts  14.9 us
    squeeze x17, local copies, waits for them, and re-layouts, pick(): return lax.dynamic_index_in_dim(value, index, axis, keepdims=False)  9.25 us
  transfers between devices with their start and end apart: 86, of which 33 were waited for; matrix products, arithmetic and copies ran while one was open for 21% of the time, Pallas kernels for 11%

profile of v4, /device:TPU:0, one launch (start us, length us, event | category | flops | bytes accessed | tf_op | source)
XLA Modules:
  0.0 421.3 jit_solution(1550064974114947823)
XLA Ops:
  1.6 3.1 collective-permute-start.5
  20.6 4.3 %collective-permute-done.8 = bf16[4,64,768]{2,1,0:T(8,128)(2,1)S(1)} collective-permute-done((bf16[4,64,768]{2,1,0:T(8,128)(2,1)S(1)}, bf16[4,64,768]{2,1,0:T(8,128)(2,1)S(1)}, u32[]{:S(2)}, u32[]{:S(2)}) %collective-permute-start.8) | collective-permute-done | bytes 393248 | tf_op jit(solution)/shard_map/ppermute | solution.py:50
  25.3 7.0 %collective-permute-done.2 = bf16[2,64,768]{2,1,0:T(8,128)(2,1)S(1)} collective-permute-done((bf16[2,64,768]{2,1,0:T(8,128)(2,1)S(1)}, bf16[2,64,768]{2,1,0:T(8,128)(2,1)S(1)}, u32[]{:S(2)}, u32[]{:S(2)}) %collective-permute-start.2) | collective-permute-done | bytes 196640 | tf_op jit(solution)/shard_map/ppermute | solution.py:50
  48.3 3.6 add_convert_fusion.q_ref.k_ref.v_ref
  52.0 10.0 %shard_map.254 = (bf16[1024,256]{1,0:T(8,128)(2,1)S(1)}, f32[1024,256]{1,0:T(8,128)S(1)}, f32[2,2,1024]{2,1,0:T(2,128)S(1)}) custom-call(bf16[1024,1536]{1,0:T(8,128)(2,1)S(1)} %add_convert_fusion.q_ref.k_ref.v_ref, bf16[1024,1536]{1,0:T(8,128)(2,1)S(1)} %add_convert_fusion.q_ref.k_ref.v_ref, bf16[1024,1536]{1,0:T(8,128)(2,1)S(1)} %add_convert_fusion.q_ref.k_ref.v_ref, ...), custom_call_target="tpu_custom_call" | custom-call | flops 4294967296 | bytes 4194304 | tf_op jit(solution)/shard_map/pallas_call | solution.py:335
  64.2 7.8 %collective-permute-start.17 = (bf16[64,2048]{1,0:T(8,128)(2,1)S(1)}, bf16[64,2048]{1,0:T(8,128)(2,1)S(1)}, u32[]{:S(2)}, u32[]{:S(2)}) collective-permute-start(bf16[64,2048]{1,0:T(8,128)(2,1)S(1)} %bitcast.496), channel_id=1, source_target_pairs={{0,8},{1,9},{2,10},{3,11},{4,12},{5,13},{6,14},{7,15},{8,16},{9,17... | collective-permute-start | bytes 786440 | tf_op jit(solution)/shard_map/ppermute | solution.py:50
  76.2 3.0 collective-permute-done.17
  79.9 10.0 %shard_map.255 = (bf16[1024,256]{1,0:T(8,128)(2,1)S(1)}, f32[1024,256]{1,0:T(8,128)S(1)}, f32[2,2,1024]{2,1,0:T(2,128)S(1)}) custom-call(bf16[1024,1536]{1,0:T(8,128)(2,1)S(1)} %add_convert_fusion.q_ref.k_ref.v_ref, bf16[1024,1536]{1,0:T(8,128)(2,1)S(1)} %add_convert_fusion.q_ref.k_ref.v_ref, bf16[1024,1536]{1,0:T(8,128)(2,1)S(1)} %add_convert_fusion.q_ref.k_ref.v_ref, ...), custom_call_target="tpu_custom_call" | custom-call | flops 4294967296 | bytes 4194304 | tf_op jit(solution)/shard_map/pallas_call | solution.py:335
  90.0 3.2 collective-permute-done.18
  95.6 5.7 %collective-permute-done.19 = bf16[64,2048]{1,0:T(8,128)(2,1)S(1)} collective-permute-done((bf16[64,2048]{1,0:T(8,128)(2,1)S(1)}, bf16[64,2048]{1,0:T(8,128)(2,1)S(1)}, u32[]{:S(2)}, u32[]{:S(2)}) %collective-permute-start.19) | collective-permute-done | bytes 262176 | tf_op jit(solution)/shard_map/ppermute | solution.py:50
  110.5 6.9 %collective-permute-done.21 = bf16[4,64,1024]{2,1,0:T(8,128)(2,1)S(1)} collective-permute-done((bf16[4,64,1024]{2,1,0:T(8,128)(2,1)S(1)}, bf16[4,64,1024]{2,1,0:T(8,128)(2,1)S(1)}, u32[]{:S(2)}, u32[]{:S(2)}) %collective-permute-start.21) | collective-permute-done | bytes 524320 | tf_op jit(solution)/shard_map/ppermute | solution.py:50
  120.3 11.2 %collective-permute-done.20 = bf16[512,512]{1,0:T(8,128)(2,1)S(1)} collective-permute-done((bf16[512,512]{1,0:T(8,128)(2,1)S(1)}, bf16[512,512]{1,0:T(8,128)(2,1)S(1)}, u32[]{:S(2)}, u32[]{:S(2)}) %collective-permute-start.20) | collective-permute-done | bytes 524320 | tf_op jit(solution)/shard_map/ppermute | solution.py:50
  133.2 9.5 %collective-permute-done.39 = bf16[4,64,1024]{2,1,0:T(8,128)(2,1)S(1)} collective-permute-done((bf16[4,64,1024]{2,1,0:T(8,128)(2,1)S(1)}, bf16[4,64,1024]{2,1,0:T(8,128)(2,1)S(1)}, u32[]{:S(2)}, u32[]{:S(2)}) %collective-permute-start.39) | collective-permute-done | bytes 524320 | tf_op jit(solution)/shard_map/ppermute | solution.py:50
  146.1 10.1 %collective-permute-done.26 = bf16[4,64,1280]{2,1,0:T(8,128)(2,1)S(1)} collective-permute-done((bf16[4,64,1280]{2,1,0:T(8,128)(2,1)S(1)}, bf16[4,64,1280]{2,1,0:T(8,128)(2,1)S(1)}, u32[]{:S(2)}, u32[]{:S(2)}) %collective-permute-start.26) | collective-permute-done | bytes 655392 | tf_op jit(solution)/shard_map/ppermute | solution.py:50
  162.8 6.8 %collective-permute-done.42 = bf16[4,64,1024]{2,1,0:T(8,128)(2,1)S(1)} collective-permute-done((bf16[4,64,1024]{2,1,0:T(8,128)(2,1)S(1)}, bf16[4,64,1024]{2,1,0:T(8,128)(2,1)S(1)}, u32[]{:S(2)}, u32[]{:S(2)}) %collective-permute-start.42) | collective-permute-done | bytes 524320 | tf_op jit(solution)/shard_map/ppermute | solution.py:50
  175.6 3.4 multiply_convert_fusion.3
  179.2 2.9 multiply_convert_fusion.2
  197.6 4.8 %convert_reduce_fusion.1 = (f32[2048]{0:T(1024)S(1)}, bf16[512,2048]{1,0:T(8,128)(2,1)}) fusion(f32[512,2048]{1,0:T(8,128)S(1)} %get-tuple-element.357, f32[2048]{0:T(1024)S(1)} %copy-done.51, bf16[512,1024]{1,0:T(8,128)(2,1)S(1)} %get-tuple-element.262, bf16[1024,2048]{1,0:T(8,128)(2,1)S(1)} %bitcast.478), kind=kOutput, calls=%fused_computation.14 | convolution fusion | flops 2163210240 | bytes 11550720 | tf_op jit(solution)/shard_map/dot_general | solution.py:243
  207.9 4.7 %convert_reduce_fusion = (f32[2048]{0:T(1024)S(1)}, bf16[512,2048]{1,0:T(8,128)(2,1)}) fusion(f32[512,2048]{1,0:T(8,128)S(1)} %get-tuple-element.355, f32[2048]{0:T(1024)S(1)} %collective-permute-done.38, bf16[512,1024]{1,0:T(8,128)(2,1)S(1)} %get-tuple-element.262, bf16[1024,2048]{1,0:T(8,128)(2,1)S(1)} %bitcast.480), kind=kOutput, calls=%fused_computation.13 | convolution fusion | flops 2163210240 | bytes 11550720 | tf_op jit(solution)/shard_map/dot_general | solution.py:243
  213.3 5.3 %fusion.63 = f32[512,1024]{1,0:T(8,128)S(1)} fusion(bf16[512,2048]{1,0:T(8,128)(2,1)} %get-tuple-element.361, bf16[1024,2048]{1,0:T(8,128)(2,1)} %bitcast.476), kind=kOutput, calls=%fused_computation.284 | convolution fusion | flops 2147483648 | bytes 8388608 | tf_op jit(solution)/shard_map/dot_general | solution.py:243
  251.6 10.0 %collective-permute-done.48 = bf16[512,512]{1,0:T(8,128)(2,1)S(1)} collective-permute-done((bf16[512,512]{1,0:T(8,128)(2,1)S(1)}, bf16[512,512]{1,0:T(8,128)(2,1)S(1)}, u32[]{:S(2)}, u32[]{:S(2)}) %collective-permute-start.48) | collective-permute-done | bytes 524320 | tf_op jit(solution)/shard_map/ppermute | solution.py:50
  268.2 12.6 %shard_map.256 = bf16[3,1024,256]{2,1,0:T(8,128)(2,1)S(1)} custom-call(bf16[1024,1536]{1,0:T(8,128)(2,1)} %copy-done.4, bf16[1024,1536]{1,0:T(8,128)(2,1)} %copy-done.4, bf16[1024,1536]{1,0:T(8,128)(2,1)} %copy-done.4, s32[1024,1]{1,0:T(8,128)S(1)} %copy.79.down_ref, s32[1,1024]{1,0:T(1,128)S(1)} %bitcast.465, f32[1024,256]{1,0:T(8,128)S(1)} %get-tuple-element.153.full_ref, ...), custom_call_target="tpu_custom_call" | custom-call | flops 10737418240 | bytes 5242880 | tf_op jit(solution)/shard_map/pallas_call | solution.py:367
  283.1 4.9 %collective-permute-done.56 = bf16[4,64,2048]{2,1,0:T(8,128)(2,1)} collective-permute-done((bf16[4,64,2048]{2,1,0:T(8,128)(2,1)}, bf16[4,64,2048]{2,1,0:T(8,128)(2,1)}, u32[]{:S(2)}, u32[]{:S(2)}) %collective-permute-start.56) | collective-permute-done | bytes 1048608 | tf_op jit(solution)/shard_map/ppermute | solution.py:50
  289.2 12.3 %collective-permute-done.57 = bf16[4,64,1280]{2,1,0:T(8,128)(2,1)S(1)} collective-permute-done((bf16[4,64,1280]{2,1,0:T(8,128)(2,1)}, bf16[4,64,1280]{2,1,0:T(8,128)(2,1)S(1)}, u32[]{:S(2)}, u32[]{:S(2)}) %collective-permute-start.57) | collective-permute-done | bytes 655392 | tf_op jit(solution)/shard_map/ppermute | solution.py:50
  320.5 12.8 %shard_map.257 = bf16[3,1024,256]{2,1,0:T(8,128)(2,1)S(1)} custom-call(bf16[1024,1536]{1,0:T(8,128)(2,1)} %copy-done.4, bf16[1024,1536]{1,0:T(8,128)(2,1)} %copy-done.4, bf16[1024,1536]{1,0:T(8,128)(2,1)} %copy-done.4, s32[1024,1]{1,0:T(8,128)S(1)} %copy-done.3, s32[1,1024]{1,0:T(1,128)S(1)} %bitcast.466, f32[1024,256]{1,0:T(8,128)S(1)} %copy-done.6, ...), custom_call_target="tpu_custom_call" | custom-call | flops 10737418240 | bytes 5242880 | tf_op jit(solution)/shard_map/pallas_call | solution.py:367
  335.0 3.2 convolution_convert_fusion.4
  343.8 3.3 fusion.18
  353.7 3.9 collective-permute-done.67
  357.6 4.0 collective-permute-done.62
  375.0 12.6 %collective-permute-done.75 = bf16[64,768]{1,0:T(8,128)(2,1)S(1)} collective-permute-done((bf16[64,768]{1,0:T(8,128)(2,1)S(1)}, bf16[64,768]{1,0:T(8,128)(2,1)S(1)}, u32[]{:S(2)}, u32[]{:S(2)}) %collective-permute-start.75) | collective-permute-done | bytes 98336 | tf_op jit(solution)/shard_map/ppermute | solution.py:50
  390.1 8.2 %collective-permute-done.70 = bf16[4,64,768]{2,1,0:T(8,128)(2,1)S(1)} collective-permute-done((bf16[4,64,768]{2,1,0:T(8,128)(2,1)S(1)}, bf16[4,64,768]{2,1,0:T(8,128)(2,1)S(1)}, u32[]{:S(2)}, u32[]{:S(2)}) %collective-permute-start.70) | collective-permute-done | bytes 393248 | tf_op jit(solution)/shard_map/ppermute | solution.py:50
  398.4 4.6 %collective-permute-done.76 = bf16[64,768]{1,0:T(8,128)(2,1)S(1)} collective-permute-done((bf16[64,768]{1,0:T(8,128)(2,1)S(1)}, bf16[64,768]{1,0:T(8,128)(2,1)S(1)}, u32[]{:S(2)}, u32[]{:S(2)}) %collective-permute-start.76) | collective-permute-done | bytes 98336 | tf_op jit(solution)/shard_map/ppermute | solution.py:50
  (485 shorter events, 201.8 us)
Async XLA Ops:
  10.1 24.1 %collective-permute-start.4 = (bf16[512,1024]{1,0:T(8,128)(2,1)}, bf16[512,1024]{1,0:T(8,128)(2,1)}, u32[]{:S(2)}, u32[]{:S(2)}) collective-permute-start(bf16[512,1024]{1,0:T(8,128)(2,1)} %param.15), channel_id=1, source_target_pairs={{0,1},{1,0},{2,3},{3,2},{4,5},{5,4},{6,7},{7,6},{8,9},{9,8},{10,11... | collective-permute-start | bytes 3145736 | tf_op jit(solution)/shard_map/ppermute | solution.py:50
  37.6 24.4 %collective-permute-start.10 = (bf16[64,2560]{1,0:T(8,128)(2,1)S(1)}, bf16[64,2560]{1,0:T(8,128)(2,1)S(1)}, u32[]{:S(2)}, u32[]{:S(2)}) collective-permute-start(bf16[64,2560]{1,0:T(8,128)(2,1)S(1)} %pad_maximum_fusion.10), channel_id=1, source_target_pairs={{0,8},{1,9},{2,10},{3,11},{4,12},{5,13},{6,14},{7,15},{8,16},{9,17... | collective-permute-start | bytes 983048 | tf_op jit(solution)/shard_map/ppermute | solution.py:50
  40.5 23.5 %collective-permute-start.11 = (bf16[64,2560]{1,0:T(8,128)(2,1)S(1)}, bf16[64,2560]{1,0:T(8,128)(2,1)S(1)}, u32[]{:S(2)}, u32[]{:S(2)}) collective-permute-start(bf16[64,2560]{1,0:T(8,128)(2,1)S(1)} %pad_maximum_fusion.10), channel_id=1, source_target_pairs={{0,16},{1,17},{2,18},{3,19},{4,20},{5,21},{6,22},{7,23},{8,24},{9,... | collective-permute-start | bytes 983048 | tf_op jit(solution)/shard_map/ppermute | solution.py:50
  42.0 22.0 %collective-permute-start.12 = (bf16[64,2560]{1,0:T(8,128)(2,1)S(1)}, bf16[64,2560]{1,0:T(8,128)(2,1)S(1)}, u32[]{:S(2)}, u32[]{:S(2)}) collective-permute-start(bf16[64,2560]{1,0:T(8,128)(2,1)S(1)} %pad_maximum_fusion.10), channel_id=1, source_target_pairs={{0,24},{1,25},{2,26},{3,27},{4,28},{5,29},{6,30},{7,31},{8,0},{9,1... | collective-permute-start | bytes 983048 | tf_op jit(solution)/shard_map/ppermute | solution.py:50
  72.0 29.2 %collective-permute-start.13 = (bf16[4,64,1280]{2,1,0:T(8,128)(2,1)S(1)}, bf16[4,64,1280]{2,1,0:T(8,128)(2,1)S(1)}, u32[]{:S(2)}, u32[]{:S(2)}) collective-permute-start(bf16[4,64,1280]{2,1,0:T(8,128)(2,1)S(1)} %get-tuple-element.326), channel_id=1, source_target_pairs={{0,4},{1,5},{2,6},{3,7},{4,0},{5,1},{6,2},{7,3},{8,12},{9,13},{10,... | collective-permute-start | bytes 1966088 | tf_op jit(solution)/shard_map/ppermute | solution.py:50
  72.6 29.9 %collective-permute-start.15 = (bf16[4,64,1280]{2,1,0:T(8,128)(2,1)S(1)}, bf16[4,64,1280]{2,1,0:T(8,128)(2,1)S(1)}, u32[]{:S(2)}, u32[]{:S(2)}) collective-permute-start(bf16[4,64,1280]{2,1,0:T(8,128)(2,1)S(1)} %get-tuple-element.326), channel_id=1, source_target_pairs={{0,1},{1,0},{2,3},{3,2},{4,5},{5,4},{6,7},{7,6},{8,9},{9,8},{10,11... | collective-permute-start | bytes 1966088 | tf_op jit(solution)/shard_map/ppermute | solution.py:50
  74.2 28.4 %collective-permute-start.14 = (bf16[4,64,1280]{2,1,0:T(8,128)(2,1)S(1)}, bf16[4,64,1280]{2,1,0:T(8,128)(2,1)S(1)}, u32[]{:S(2)}, u32[]{:S(2)}) collective-permute-start(bf16[4,64,1280]{2,1,0:T(8,128)(2,1)S(1)} %get-tuple-element.325), channel_id=1, source_target_pairs={{0,4},{1,5},{2,6},{3,7},{4,0},{5,1},{6,2},{7,3},{8,12},{9,13},{10,... | collective-permute-start | bytes 1966088 | tf_op jit(solution)/shard_map/ppermute | solution.py:50
  75.6 27.2 %collective-permute-start.16 = (bf16[4,64,1280]{2,1,0:T(8,128)(2,1)S(1)}, bf16[4,64,1280]{2,1,0:T(8,128)(2,1)S(1)}, u32[]{:S(2)}, u32[]{:S(2)}) collective-permute-start(bf16[4,64,1280]{2,1,0:T(8,128)(2,1)S(1)} %get-tuple-element.325), channel_id=1, source_target_pairs={{0,1},{1,0},{2,3},{3,2},{4,5},{5,4},{6,7},{7,6},{8,9},{9,8},{10,11... | collective-permute-start | bytes 1966088 | tf_op jit(solution)/shard_map/ppermute | solution.py:50
  104.7 26.8 %collective-permute-start.31 = (bf16[4,64,1024]{2,1,0:T(8,128)(2,1)S(1)}, bf16[4,64,1024]{2,1,0:T(8,128)(2,1)S(1)}, u32[]{:S(2)}, u32[]{:S(2)}) collective-permute-start(bf16[4,64,1024]{2,1,0:T(8,128)(2,1)S(1)} %get-tuple-element.331), channel_id=1, source_target_pairs={{0,2},{1,3},{2,0},{3,1},{4,6},{5,7},{6,4},{7,5},{8,10},{9,11},{10,... | collective-permute-start | bytes 1572872 | tf_op jit(solution)/shard_map/ppermute | solution.py:50
  107.4 24.1 %collective-permute-start.20 = (bf16[512,512]{1,0:T(8,128)(2,1)S(1)}, bf16[512,512]{1,0:T(8,128)(2,1)S(1)}, u32[]{:S(2)}, u32[]{:S(2)}) collective-permute-start(bf16[512,512]{1,0:T(8,128)(2,1)S(1)} %get-tuple-element.314), channel_id=1, source_target_pairs={{0,1},{1,0},{2,3},{3,2},{4,5},{5,4},{6,7},{7,6},{8,9},{9,8},{10,11... | collective-permute-start | bytes 1572872 | tf_op jit(solution)/shard_map/ppermute | solution.py:50
  108.8 33.9 %collective-permute-start.39 = (bf16[4,64,1024]{2,1,0:T(8,128)(2,1)S(1)}, bf16[4,64,1024]{2,1,0:T(8,128)(2,1)S(1)}, u32[]{:S(2)}, u32[]{:S(2)}) collective-permute-start(bf16[4,64,1024]{2,1,0:T(8,128)(2,1)S(1)} %get-tuple-element.332), channel_id=1, source_target_pairs={{0,1},{1,0},{2,3},{3,2},{4,5},{5,4},{6,7},{7,6},{8,9},{9,8},{10,11... | collective-permute-start | bytes 1572872 | tf_op jit(solution)/shard_map/ppermute | solution.py:50
  117.5 40.5 %collective-permute-start.33 = (bf16[4,64,1024]{2,1,0:T(8,128)(2,1)S(1)}, bf16[4,64,1024]{2,1,0:T(8,128)(2,1)S(1)}, u32[]{:S(2)}, u32[]{:S(2)}) collective-permute-start(bf16[4,64,1024]{2,1,0:T(8,128)(2,1)S(1)} %get-tuple-element.331), channel_id=1, source_target_pairs={{0,4},{1,5},{2,6},{3,7},{4,0},{5,1},{6,2},{7,3},{8,12},{9,13},{10,... | collective-permute-start | bytes 1572872 | tf_op jit(solution)/shard_map/ppermute | solution.py:50
  120.3 23.1 %collective-permute-start.24 = (bf16[4,64,1280]{2,1,0:T(8,128)(2,1)S(1)}, bf16[4,64,1280]{2,1,0:T(8,128)(2,1)S(1)}, u32[]{:S(2)}, u32[]{:S(2)}) collective-permute-start(bf16[4,64,1280]{2,1,0:T(8,128)(2,1)S(1)} %collective-permute-done.13), channel_id=1, source_target_pairs={{0,2},{1,3},{2,0},{3,1},{4,6},{5,7},{6,4},{7,5},{8,10},{9,11},{10,... | collective-permute-start | bytes 1966088 | tf_op jit(solution)/shard_map/ppermute | solution.py:50
  131.5 24.7 %collective-permute-start.26 = (bf16[4,64,1280]{2,1,0:T(8,128)(2,1)S(1)}, bf16[4,64,1280]{2,1,0:T(8,128)(2,1)S(1)}, u32[]{:S(2)}, u32[]{:S(2)}) collective-permute-start(bf16[4,64,1280]{2,1,0:T(8,128)(2,1)S(1)} %collective-permute-done.13), channel_id=1, source_target_pairs={{0,1},{1,0},{2,3},{3,2},{4,5},{5,4},{6,7},{7,6},{8,9},{9,8},{10,11... | collective-permute-start | bytes 1966088 | tf_op jit(solution)/shard_map/ppermute | solution.py:50
  160.8 18.4 %collective-permute-start.38 = (f32[2048]{0:T(1024)S(1)}, f32[2048]{0:T(1024)S(1)}, u32[]{:S(2)}, u32[]{:S(2)}) collective-permute-start(f32[2048]{0:T(1024)S(1)} %copy-done.51), channel_id=1, source_target_pairs={{0,1},{1,0},{2,3},{3,2},{4,5},{5,4},{6,7},{7,6},{8,9},{9,8},{10,11... | collective-permute-start | bytes 24584 | tf_op jit(solution)/shard_map/ppermute | solution.py:50
  238.6 24.2 %collective-permute-start.50 = (bf16[4,2,64,512]{3,2,1,0:T(8,128)(2,1)S(1)}, bf16[4,2,64,512]{3,2,1,0:T(8,128)(2,1)S(1)}, u32[]{:S(2)}, u32[]{:S(2)}) collective-permute-start(bf16[4,2,64,512]{3,2,1,0:T(8,128)(2,1)S(1)} %get-tuple-element.311), channel_id=1, source_target_pairs={{0,2},{1,3},{2,0},{3,1},{4,6},{5,7},{6,4},{7,5},{8,10},{9,11},{10,... | collective-permute-start | bytes 1572872 | tf_op jit(solution)/shard_map/ppermute | solution.py:50
  245.9 18.4 %collective-permute-start.54 = (bf16[4,2,64,2048]{3,2,1,0:T(8,128)(2,1)S(1)}, bf16[4,2,64,2048]{3,2,1,0:T(8,128)(2,1)S(1)}, u32[]{:S(2)}, u32[]{:S(2)}) collective-permute-start(bf16[4,2,64,2048]{3,2,1,0:T(8,128)(2,1)S(1)} %get-tuple-element.264), channel_id=1, source_target_pairs={{0,2},{1,3},{2,0},{3,1},{4,6},{5,7},{6,4},{7,5},{8,10},{9,11},{10,... | collective-permute-start | bytes 6291464 | tf_op jit(solution)/shard_map/ppermute | solution.py:50
  261.6 26.4 %collective-permute-start.56 = (bf16[4,64,2048]{2,1,0:T(8,128)(2,1)}, bf16[4,64,2048]{2,1,0:T(8,128)(2,1)}, u32[]{:S(2)}, u32[]{:S(2)}) collective-permute-start(bf16[4,64,2048]{2,1,0:T(8,128)(2,1)} %pad_maximum_fusion.7), channel_id=1, source_target_pairs={{0,1},{1,0},{2,3},{3,2},{4,5},{5,4},{6,7},{7,6},{8,9},{9,8},{10,11... | collective-permute-start | bytes 3145736 | tf_op jit(solution)/shard_map/ppermute | solution.py:50
  262.8 26.5 %collective-permute-start.55 = (bf16[4,64,2048]{2,1,0:T(8,128)(2,1)}, bf16[4,64,2048]{2,1,0:T(8,128)(2,1)}, u32[]{:S(2)}, u32[]{:S(2)}) collective-permute-start(bf16[4,64,2048]{2,1,0:T(8,128)(2,1)} %pad_maximum_fusion.6), channel_id=1, source_target_pairs={{0,4},{1,5},{2,6},{3,7},{4,0},{5,1},{6,2},{7,3},{8,12},{9,13},{10,... | collective-permute-start | bytes 3145736 | tf_op jit(solution)/shard_map/ppermute | solution.py:50
  264.3 18.7 %collective-permute-start.59 = (f32[10240]{0:T(1024)S(1)}, f32[10240]{0:T(1024)S(1)}, u32[]{:S(2)}, u32[]{:S(2)}) collective-permute-start(f32[10240]{0:T(1024)S(1)} %constant_dynamic-update-slice_fusion.11), channel_id=1, source_target_pairs={{0,2},{1,3},{2,0},{3,1},{4,6},{5,7},{6,4},{7,5},{8,10},{9,11},{10,... | collective-permute-start | bytes 122888 | tf_op jit(solution)/shard_map/ppermute | solution.py:50
  266.7 34.8 %collective-permute-start.57 = (bf16[4,64,1280]{2,1,0:T(8,128)(2,1)}, bf16[4,64,1280]{2,1,0:T(8,128)(2,1)S(1)}, u32[]{:S(2)}, u32[]{:S(2)}) collective-permute-start(bf16[4,64,1280]{2,1,0:T(8,128)(2,1)} %get-tuple-element.299), channel_id=1, source_target_pairs={{0,4},{1,5},{2,6},{3,7},{4,0},{5,1},{6,2},{7,3},{8,12},{9,13},{10,... | collective-permute-start | bytes 1966088 | tf_op jit(solution)/shard_map/ppermute | solution.py:50
  267.3 34.2 %collective-permute-start.58 = (bf16[4,64,1280]{2,1,0:T(8,128)(2,1)}, bf16[4,64,1280]{2,1,0:T(8,128)(2,1)S(1)}, u32[]{:S(2)}, u32[]{:S(2)}) collective-permute-start(bf16[4,64,1280]{2,1,0:T(8,128)(2,1)} %get-tuple-element.298), channel_id=1, source_target_pairs={{0,1},{1,0},{2,3},{3,2},{4,5},{5,4},{6,7},{7,6},{8,9},{9,8},{10,11... | collective-permute-start | bytes 1966088 | tf_op jit(solution)/shard_map/ppermute | solution.py:50
  310.0 38.7 %collective-permute-start.65 = (bf16[64,2048]{1,0:T(8,128)(2,1)}, bf16[64,2048]{1,0:T(8,128)(2,1)}, u32[]{:S(2)}, u32[]{:S(2)}) collective-permute-start(bf16[64,2048]{1,0:T(8,128)(2,1)} %get-tuple-element.302), channel_id=1, source_target_pairs={{0,8},{1,9},{2,10},{3,11},{4,12},{5,13},{6,14},{7,15},{8,16},{9,17... | collective-permute-start | bytes 786440 | tf_op jit(solution)/shard_map/ppermute | solution.py:50
  310.3 38.5 %collective-permute-start.66 = (bf16[64,2048]{1,0:T(8,128)(2,1)}, bf16[64,2048]{1,0:T(8,128)(2,1)}, u32[]{:S(2)}, u32[]{:S(2)}) collective-permute-start(bf16[64,2048]{1,0:T(8,128)(2,1)} %get-tuple-element.301), channel_id=1, source_target_pairs={{0,16},{1,17},{2,18},{3,19},{4,20},{5,21},{6,22},{7,23},{8,24},{9,... | collective-permute-start | bytes 786440 | tf_op jit(solution)/shard_map/ppermute | solution.py:50
  313.0 48.5 %collective-permute-start.64 = (bf16[4,64,2560]{2,1,0:T(8,128)(2,1)}, bf16[4,64,2560]{2,1,0:T(8,128)(2,1)}, u32[]{:S(2)}, u32[]{:S(2)}) collective-permute-start(bf16[4,64,2560]{2,1,0:T(8,128)(2,1)} %pad_maximum_fusion.4), channel_id=1, source_target_pairs={{0,1},{1,0},{2,3},{3,2},{4,5},{5,4},{6,7},{7,6},{8,9},{9,8},{10,11... | collective-permute-start | bytes 3932168 | tf_op jit(solution)/shard_map/ppermute | solution.py:50
  319.0 42.6 %collective-permute-start.63 = (bf16[4,64,2560]{2,1,0:T(8,128)(2,1)}, bf16[4,64,2560]{2,1,0:T(8,128)(2,1)}, u32[]{:S(2)}, u32[]{:S(2)}) collective-permute-start(bf16[4,64,2560]{2,1,0:T(8,128)(2,1)} %pad_maximum_fusion.3), channel_id=1, source_target_pairs={{0,4},{1,5},{2,6},{3,7},{4,0},{5,1},{6,2},{7,3},{8,12},{9,13},{10,... | collective-permute-start | bytes 3932168 | tf_op jit(solution)/shard_map/ppermute | solution.py:50
  342.7 18.9 %collective-permute-start.61 = (bf16[4,2,64,768]{3,2,1,0:T(8,128)(2,1)S(1)}, bf16[4,2,64,768]{3,2,1,0:T(8,128)(2,1)S(1)}, u32[]{:S(2)}, u32[]{:S(2)}) collective-permute-start(bf16[4,2,64,768]{3,2,1,0:T(8,128)(2,1)S(1)} %get-tuple-element.281), channel_id=1, source_target_pairs={{0,2},{1,3},{2,0},{3,1},{4,6},{5,7},{6,4},{7,5},{8,10},{9,11},{10,... | collective-permute-start | bytes 2359304 | tf_op jit(solution)/shard_map/ppermute | solution.py:50
  365.9 21.7 %collective-permute-start.75 = (bf16[64,768]{1,0:T(8,128)(2,1)S(1)}, bf16[64,768]{1,0:T(8,128)(2,1)S(1)}, u32[]{:S(2)}, u32[]{:S(2)}) collective-permute-start(bf16[64,768]{1,0:T(8,128)(2,1)S(1)} %get-tuple-element.322), channel_id=1, source_target_pairs={{0,16},{1,17},{2,18},{3,19},{4,20},{5,21},{6,22},{7,23},{8,24},{9,... | collective-permute-start | bytes 294920 | tf_op jit(solution)/shard_map/ppermute | solution.py:50
  366.5 36.5 %collective-permute-start.77 = (bf16[512,1024]{1,0:T(8,128)(2,1)S(1)}, bf16[512,1024]{1,0:T(8,128)(2,1)S(1)}, u32[]{:S(2)}, u32[]{:S(2)}) collective-permute-start(bf16[512,1024]{1,0:T(8,128)(2,1)S(1)} %fusion.18), channel_id=1, source_target_pairs={{0,1},{1,0},{2,3},{3,2},{4,5},{5,4},{6,7},{7,6},{8,9},{9,8},{10,11... | collective-permute-start | bytes 3145736 | tf_op jit(solution)/shard_map/ppermute | solution.py:50
  369.7 33.3 %collective-permute-start.71 = (bf16[64,2560]{1,0:T(8,128)(2,1)S(1)}, bf16[64,2560]{1,0:T(8,128)(2,1)S(1)}, u32[]{:S(2)}, u32[]{:S(2)}) collective-permute-start(bf16[64,2560]{1,0:T(8,128)(2,1)S(1)} %get-tuple-element.292), channel_id=1, source_target_pairs={{0,8},{1,9},{2,10},{3,11},{4,12},{5,13},{6,14},{7,15},{8,16},{9,17... | collective-permute-start | bytes 983048 | tf_op jit(solution)/shard_map/ppermute | solution.py:50
  372.3 30.6 %collective-permute-start.72 = (bf16[64,2560]{1,0:T(8,128)(2,1)S(1)}, bf16[64,2560]{1,0:T(8,128)(2,1)S(1)}, u32[]{:S(2)}, u32[]{:S(2)}) collective-permute-start(bf16[64,2560]{1,0:T(8,128)(2,1)S(1)} %get-tuple-element.291), channel_id=1, source_target_pairs={{0,16},{1,17},{2,18},{3,19},{4,20},{5,21},{6,22},{7,23},{8,24},{9,... | collective-permute-start | bytes 983048 | tf_op jit(solution)/shard_map/ppermute | solution.py:50
  373.1 29.8 %collective-permute-start.73 = (bf16[64,2560]{1,0:T(8,128)(2,1)S(1)}, bf16[64,2560]{1,0:T(8,128)(2,1)S(1)}, u32[]{:S(2)}, u32[]{:S(2)}) collective-permute-start(bf16[64,2560]{1,0:T(8,128)(2,1)S(1)} %get-tuple-element.290), channel_id=1, source_target_pairs={{0,24},{1,25},{2,26},{3,27},{4,28},{5,29},{6,30},{7,31},{8,0},{9,1... | collective-permute-start | bytes 983048 | tf_op jit(solution)/shard_map/ppermute | solution.py:50
  (112 other events, 1194.8 us)

commit v5 on v4

--- a/solution.py
+++ b/solution.py
@@ -149,17 +149,23 @@
     return [[both[j][k] for j in range(sizes[X])] for k in range(sizes[Y])]
 
 
+def last_digit(stacked, sizes, digit):
+    count = stacked.shape[1]
+    cored = [fan(piece, sizes, C) for piece in fan(stacked, sizes, digit)]
+    return [[[part[:, n] for part in by_core] for n in range(count)] for by_core in cored]
+
+
 def assemble(spreads, sizes, at, widths):
     begins = [sum(widths[:m]) for m in range(len(widths))]
-    nz, depth, _ = spreads[0][0][0].shape
+    nz, depth, _ = spreads[0][0][0][0].shape
     pieces, moves, shapes = [], [], []
     for k, by_x in enumerate(spreads):
         shapes += [(nz, sizes[X], sizes[C], depth, width) for width in widths]
         for j, halves in enumerate(by_x):
             base = 0
             for half in halves:
-                size = half.shape[-1]
-                for c, part in enumerate(fan(half, sizes, C)):
+                size = half[0].shape[-1]
+                for c, part in enumerate(half):
                     for m, width in enumerate(widths):
                         low = max(begins[m], base)
                         high = min(begins[m] + width, base + size)
@@ -429,36 +435,41 @@
 
     token_pieces = fan(tokens, sizes, Y)
     upper_shard = jnp.concatenate([output_weight.T, expand_weight], axis=1)
-    proj, (upper_shard, token_pieces) = gather_project(
+    proj, (upper_shard, token_pieces, shrink_shard) = gather_project(
         jnp.transpose(project_weight, (1, 0, 2)).reshape(depth, 3 * heads_width),
         sizes,
         at,
-        (upper_shard, token_pieces),
+        (upper_shard, token_pieces, shrink_weight.T),
     )
     whole_tokens = place(token_pieces, mine, 0).reshape(all_rows, width)
     upper_z = fan(upper_shard, sizes, Z)
+    cut = hidden // 2
+    shrink_y = jnp.stack(fan(shrink_shard[:, :cut], sizes, Y))
+    shrink_x = jnp.stack(fan(shrink_shard[:, cut:], sizes, X))
     expand_biases = fan(expand_bias, sizes, Y)
 
     bias = jnp.concatenate([project_bias[0], jnp.zeros_like(project_bias[0]), project_bias[1]])
     projected = (dot(whole_tokens, proj, NN) + bias).astype(BF16)
-    projected, shrink_shard = sync(projected, shrink_weight.T)
-    shrink_z = fan(shrink_shard, sizes, Z)
+    projected, shrink_y, shrink_x = sync(projected, shrink_y, shrink_x)
+    shrink_y = fan(shrink_y, sizes, Z)
     fwd = [attention(projected, segment, 0, group)]
     fwd[0], upper_z, projected = sync(fwd[0], upper_z, projected)
     upper_x, upper_y = spread_sides(stack_z(upper_z, sizes, at), sizes)
     if calls == 2:
         fwd.append(attention(projected, segment, group, group))
     if square:
-        fwd[-1], upper_x[1], upper_y, shrink_z = sync(fwd[-1], upper_x[1], upper_y, shrink_z)
+        fwd[-1], upper_x[1], upper_y, shrink_y = sync(fwd[-1], upper_x[1], upper_y, shrink_y)
     by_rows = jnp.concatenate([f[0] for f in fwd], axis=1).reshape(n_t, rows, heads_width)
     mixed = [pick(by_rows, mine, 0)]
     for k in range(1, n_t):
         mixed.append(hop(pick(by_rows, (mine + k) % n_t, 0), sizes, Y, k))
 
     upper_pieces = spread_corner(upper_x, upper_y, sizes)
-    shrink_x, shrink_y = spread_sides(stack_z(shrink_z, sizes, at), sizes)
-    if square:
-        mixed, shrink_x[1][0], shrink_y[1] = sync(mixed, shrink_x[1][0], shrink_y[1])
+    shrink_x = fan(shrink_x, sizes, Z)
+    mixed, shrink_x = sync(mixed, shrink_x)
+    over_x = last_digit(place(shrink_y, at[Z], 0), sizes, X)
+    over_y = last_digit(place(shrink_x, at[Z], 0), sizes, Y)
+    upper_pieces = [[[fan(h, sizes, C) for h in by_h] for by_h in by_x] for by_x in upper_pieces]
     gathered = assemble(upper_pieces, sizes, at, (heads_width, hidden))
     mix = [g[0] for g in gathered]
     expand = [g[1] for g in gathered]
@@ -471,7 +482,9 @@
         act, der = gelu_both(dot(low1, w, NN) + b)
         active.append(act.astype(BF16))
         slope.append(der.astype(BF16))
-    shrink_pieces = spread_corner(shrink_x, shrink_y, sizes)
+    shrink_pieces = [
+        [[over_x[j][k], over_y[k][j]] for j in range(sizes[X])] for k in range(n_t)
+    ]
     shrink = [g[0] for g in assemble(shrink_pieces, sizes, at, (hidden,))]
     branch = sum(dot(a, w, NT) for a, w in zip(active, shrink)) + shrink_bias
     unit2, scale2 = norm_parts(normed1 + branch)

time: 429 us -> 426 us (level)
  waiting for transfers between devices: 147 us -> 153 us
    ppermute x86 -> x83, waiting for transfers between devices: 147 us -> 153 us  [hop(): return lax.ppermute(value, ALL, pairs)]
    unnamed x132 -> x130, local copies, waits for them, and re-layouts: 14.9 us -> 11.4 us
    ppermute x86 -> x83, starting transfers between devices: 90 us -> 91.4 us  [hop(): return lax.ppermute(value, ALL, pairs)]
  transfers between devices with their start and end apart: 86 -> 83, of which waited for: 33 -> 31; matrix products, arithmetic and copies ran while one was open for 21% -> 18% of each run, Pallas kernels for 11% -> 11%
where the time goes in v5:
time: 426 us; the launch traced here: 422 us
  waiting for transfers between devices  153 us (36%)
  starting transfers between devices  91.4 us (21%)
  matrix products  55.4 us (13%)
  Pallas kernels  45.5 us (11%)
  local copies, waits for them, and re-layouts  37.9 us (9%)
  other arithmetic  34.9 us (8%)
    ppermute x83, waiting for transfers between devices, hop(): return lax.ppermute(value, ALL, pairs)  153 us
    ppermute x83, starting transfers between devices, hop(): return lax.ppermute(value, ALL, pairs)  91.4 us
    dot_general x23, matrix products, dot(): return lax.dot_general(a, b, (dims, ((), ())), preferred_element_type=F32)  55.4 us
    pallas_call x2, Pallas kernels, attention_back(): pl.pallas_call(attend_back_kernel, grid=(count,), in_specs=[block(third(c...  25.4 us
    pallas_call x2, Pallas kernels, attention(): pl.pallas_call(attend_kernel, grid=(count,), in_specs=[block(third(c * pa...  20.1 us
    squeeze x17, local copies, waits for them, and re-layouts, pick(): return lax.dynamic_index_in_dim(value, index, axis, keepdims=False)  12.6 us
    unnamed x130, local copies, waits for them, and re-layouts  11.4 us
  transfers between devices with their start and end apart: 83, of which 31 were waited for; matrix products, arithmetic and copies ran while one was open for 18% of the time, Pallas kernels for 11%

profile of v5, /device:TPU:0, one launch (start us, length us, event | category | flops | bytes accessed | tf_op | source)
XLA Modules:
  0.0 421.5 jit_solution(6169752692699670238)
XLA Ops:
  1.6 4.1 collective-permute-start.6
  21.3 3.5 collective-permute-done.8
  24.9 11.7 %collective-permute-done.2 = bf16[2,64,768]{2,1,0:T(8,128)(2,1)S(1)} collective-permute-done((bf16[2,64,768]{2,1,0:T(8,128)(2,1)S(1)}, bf16[2,64,768]{2,1,0:T(8,128)(2,1)S(1)}, u32[]{:S(2)}, u32[]{:S(2)}) %collective-permute-start.2) | collective-permute-done | bytes 196640 | tf_op jit(solution)/shard_map/ppermute | solution.py:50
  50.9 3.7 add_convert_fusion.q_ref.k_ref.v_ref
  57.5 10.0 %shard_map.254 = (bf16[1024,256]{1,0:T(8,128)(2,1)S(1)}, f32[1024,256]{1,0:T(8,128)S(1)}, f32[2,2,1024]{2,1,0:T(2,128)S(1)}) custom-call(bf16[1024,1536]{1,0:T(8,128)(2,1)S(1)} %add_convert_fusion.q_ref.k_ref.v_ref, bf16[1024,1536]{1,0:T(8,128)(2,1)S(1)} %add_convert_fusion.q_ref.k_ref.v_ref, bf16[1024,1536]{1,0:T(8,128)(2,1)S(1)} %add_convert_fusion.q_ref.k_ref.v_ref, ...), custom_call_target="tpu_custom_call" | custom-call | flops 4294967296 | bytes 4194304 | tf_op jit(solution)/shard_map/pallas_call | solution.py:341
  67.5 9.5 %collective-permute-done.13 = bf16[64,2560]{1,0:T(8,128)(2,1)S(1)} collective-permute-done((bf16[64,2560]{1,0:T(8,128)(2,1)S(1)}, bf16[64,2560]{1,0:T(8,128)(2,1)S(1)}, u32[]{:S(2)}, u32[]{:S(2)}) %collective-permute-start.13) | collective-permute-done | bytes 327712 | tf_op jit(solution)/shard_map/ppermute | solution.py:50
  81.4 10.0 %shard_map.255 = (bf16[1024,256]{1,0:T(8,128)(2,1)S(1)}, f32[1024,256]{1,0:T(8,128)S(1)}, f32[2,2,1024]{2,1,0:T(2,128)S(1)}) custom-call(bf16[1024,1536]{1,0:T(8,128)(2,1)S(1)} %add_convert_fusion.q_ref.k_ref.v_ref, bf16[1024,1536]{1,0:T(8,128)(2,1)S(1)} %add_convert_fusion.q_ref.k_ref.v_ref, bf16[1024,1536]{1,0:T(8,128)(2,1)S(1)} %add_convert_fusion.q_ref.k_ref.v_ref, ...), custom_call_target="tpu_custom_call" | custom-call | flops 4294967296 | bytes 4194304 | tf_op jit(solution)/shard_map/pallas_call | solution.py:341
  91.5 5.9 %collective-permute-start.19 = (bf16[2,64,1024]{2,1,0:T(8,128)(2,1)S(1)}, bf16[2,64,1024]{2,1,0:T(8,128)(2,1)S(1)}, u32[]{:S(2)}, u32[]{:S(2)}) collective-permute-start(bf16[2,64,1024]{2,1,0:T(8,128)(2,1)S(1)} %pad_maximum_fusion.11), channel_id=1, source_target_pairs={{0,8},{1,9},{2,10},{3,11},{4,12},{5,13},{6,14},{7,15},{8,16},{9,17... | collective-permute-start | bytes 786440 | tf_op jit(solution)/shard_map/ppermute | solution.py:50
  98.0 3.9 collective-permute-done.19
  103.4 4.1 collective-permute-start.25
  107.9 6.4 %collective-permute-start.23 = (bf16[2,64,1024]{2,1,0:T(8,128)(2,1)S(1)}, bf16[2,64,1024]{2,1,0:T(8,128)(2,1)S(1)}, u32[]{:S(2)}, u32[]{:S(2)}) collective-permute-start(bf16[2,64,1024]{2,1,0:T(8,128)(2,1)S(1)} %pad_maximum_fusion.12), channel_id=1, source_target_pairs={{0,8},{1,9},{2,10},{3,11},{4,12},{5,13},{6,14},{7,15},{8,16},{9,17... | collective-permute-start | bytes 786440 | tf_op jit(solution)/shard_map/ppermute | solution.py:50
  121.0 7.8 %collective-permute-done.24 = bf16[2,64,1024]{2,1,0:T(8,128)(2,1)S(1)} collective-permute-done((bf16[2,64,1024]{2,1,0:T(8,128)(2,1)S(1)}, bf16[2,64,1024]{2,1,0:T(8,128)(2,1)S(1)}, u32[]{:S(2)}, u32[]{:S(2)}) %collective-permute-start.24) | collective-permute-done | bytes 262176 | tf_op jit(solution)/shard_map/ppermute | solution.py:50
  129.4 3.1 collective-permute-done.22
  138.6 9.8 %collective-permute-done.29 = bf16[4,64,1280]{2,1,0:T(8,128)(2,1)S(1)} collective-permute-done((bf16[4,64,1280]{2,1,0:T(8,128)(2,1)S(1)}, bf16[4,64,1280]{2,1,0:T(8,128)(2,1)S(1)}, u32[]{:S(2)}, u32[]{:S(2)}) %collective-permute-start.29) | collective-permute-done | bytes 655392 | tf_op jit(solution)/shard_map/ppermute | solution.py:50
  150.7 13.9 %collective-permute-done.35 = bf16[4,2,64,1024]{3,2,0,1:T(8,128)(2,1)S(1)} collective-permute-done((bf16[4,2,64,1024]{3,2,0,1:T(8,128)(2,1)S(1)}, bf16[4,2,64,1024]{3,2,0,1:T(8,128)(2,1)S(1)}, u32[]{:S(2)}, u32[]{:S(2)}) %collective-permute-start.35) | collective-permute-done | bytes 1048608 | tf_op jit(solution)/shard_map/ppermute | solution.py:50
  171.3 3.0 collective-permute-done.41
  193.8 4.8 %convert_reduce_fusion.1 = (f32[2048]{0:T(1024)S(1)}, bf16[512,2048]{1,0:T(8,128)(2,1)}) fusion(f32[512,2048]{1,0:T(8,128)S(1)} %get-tuple-element.369, f32[2048]{0:T(1024)S(1)} %copy-done.50, bf16[512,1024]{1,0:T(8,128)(2,1)S(1)} %get-tuple-element.270, bf16[1024,2048]{1,0:T(8,128)(2,1)S(1)} %bitcast.532), kind=kOutput, calls=%fused_computation.14 | convolution fusion | flops 2163210240 | bytes 11550720 | tf_op jit(solution)/shard_map/dot_general | solution.py:249
  204.1 4.7 %convert_reduce_fusion = (f32[2048]{0:T(1024)S(1)}, bf16[512,2048]{1,0:T(8,128)(2,1)}) fusion(f32[512,2048]{1,0:T(8,128)S(1)} %get-tuple-element.371, f32[2048]{0:T(1024)S(1)} %collective-permute-done.40, bf16[512,1024]{1,0:T(8,128)(2,1)S(1)} %get-tuple-element.270, bf16[1024,2048]{1,0:T(8,128)(2,1)S(1)} %bitcast.530), kind=kOutput, calls=%fused_computation.13 | convolution fusion | flops 2163210240 | bytes 11550720 | tf_op jit(solution)/shard_map/dot_general | solution.py:249
  209.5 5.3 %fusion.79 = f32[512,1024]{1,0:T(8,128)S(1)} fusion(bf16[512,2048]{1,0:T(8,128)(2,1)} %get-tuple-element.373, bf16[1024,2048]{1,0:T(8,128)(2,1)} %bitcast.528), kind=kOutput, calls=%fused_computation.304 | convolution fusion | flops 2147483648 | bytes 8388608 | tf_op jit(solution)/shard_map/dot_general | solution.py:249
  237.6 9.5 %collective-permute-done.49 = bf16[4,64,1024]{2,1,0:T(8,128)(2,1)S(1)} collective-permute-done((bf16[4,64,1024]{2,1,0:T(8,128)(2,1)S(1)}, bf16[4,64,1024]{2,1,0:T(8,128)(2,1)S(1)}, u32[]{:S(2)}, u32[]{:S(2)}) %collective-permute-start.49) | collective-permute-done | bytes 524320 | tf_op jit(solution)/shard_map/ppermute | solution.py:50
  255.1 10.3 %collective-permute-done.45 = bf16[512,512]{1,0:T(8,128)(2,1)S(1)} collective-permute-done((bf16[512,512]{1,0:T(8,128)(2,1)S(1)}, bf16[512,512]{1,0:T(8,128)(2,1)S(1)}, u32[]{:S(2)}, u32[]{:S(2)}) %collective-permute-start.45) | collective-permute-done | bytes 524320 | tf_op jit(solution)/shard_map/ppermute | solution.py:50
  271.1 12.6 %shard_map.256 = bf16[3,1024,256]{2,1,0:T(8,128)(2,1)S(1)} custom-call(bf16[1024,1536]{1,0:T(8,128)(2,1)} %copy-done.4, bf16[1024,1536]{1,0:T(8,128)(2,1)} %copy-done.4, bf16[1024,1536]{1,0:T(8,128)(2,1)} %copy-done.4, s32[1024,1]{1,0:T(8,128)S(1)} %copy.86.down_ref, s32[1,1024]{1,0:T(1,128)S(1)} %bitcast.517, f32[1024,256]{1,0:T(8,128)S(1)} %get-tuple-element.161.full_ref, ...), custom_call_target="tpu_custom_call" | custom-call | flops 10737418240 | bytes 5242880 | tf_op jit(solution)/shard_map/pallas_call | solution.py:373
  285.9 5.8 %collective-permute-done.53 = bf16[4,64,2048]{2,1,0:T(8,128)(2,1)} collective-permute-done((bf16[4,64,2048]{2,1,0:T(8,128)(2,1)}, bf16[4,64,2048]{2,1,0:T(8,128)(2,1)}, u32[]{:S(2)}, u32[]{:S(2)}) %collective-permute-start.53) | collective-permute-done | bytes 1048608 | tf_op jit(solution)/shard_map/ppermute | solution.py:50
  292.4 11.5 %collective-permute-done.55 = bf16[4,64,1280]{2,1,0:T(8,128)(2,1)S(1)} collective-permute-done((bf16[4,64,1280]{2,1,0:T(8,128)(2,1)S(1)}, bf16[4,64,1280]{2,1,0:T(8,128)(2,1)S(1)}, u32[]{:S(2)}, u32[]{:S(2)}) %collective-permute-start.55) | collective-permute-done | bytes 655392 | tf_op jit(solution)/shard_map/ppermute | solution.py:50
  307.4 3.9 collective-permute-start.63
  322.8 12.8 %shard_map.257 = bf16[3,1024,256]{2,1,0:T(8,128)(2,1)S(1)} custom-call(bf16[1024,1536]{1,0:T(8,128)(2,1)} %copy-done.4, bf16[1024,1536]{1,0:T(8,128)(2,1)} %copy-done.4, bf16[1024,1536]{1,0:T(8,128)(2,1)} %copy-done.4, s32[1024,1]{1,0:T(8,128)S(1)} %copy-done.3, s32[1,1024]{1,0:T(1,128)S(1)} %bitcast.518, f32[1024,256]{1,0:T(8,128)S(1)} %copy-done.6, ...), custom_call_target="tpu_custom_call" | custom-call | flops 10737418240 | bytes 5242880 | tf_op jit(solution)/shard_map/pallas_call | solution.py:373
  337.2 3.2 convolution_convert_fusion.4
  351.9 7.1 %collective-permute-done.62 = bf16[64,2048]{1,0:T(8,128)(2,1)S(1)} collective-permute-done((bf16[64,2048]{1,0:T(8,128)(2,1)S(1)}, bf16[64,2048]{1,0:T(8,128)(2,1)S(1)}, u32[]{:S(2)}, u32[]{:S(2)}) %collective-permute-start.62) | collective-permute-done | bytes 262176 | tf_op jit(solution)/shard_map/ppermute | solution.py:50
  379.2 16.9 %collective-permute-done.71 = bf16[64,768]{1,0:T(8,128)(2,1)S(1)} collective-permute-done((bf16[64,768]{1,0:T(8,128)(2,1)S(1)}, bf16[64,768]{1,0:T(8,128)(2,1)S(1)}, u32[]{:S(2)}, u32[]{:S(2)}) %collective-permute-start.71) | collective-permute-done | bytes 98336 | tf_op jit(solution)/shard_map/ppermute | solution.py:50
  396.1 7.1 %collective-permute-done.69 = bf16[64,2560]{1,0:T(8,128)(2,1)S(1)} collective-permute-done((bf16[64,2560]{1,0:T(8,128)(2,1)S(1)}, bf16[64,2560]{1,0:T(8,128)(2,1)S(1)}, u32[]{:S(2)}, u32[]{:S(2)}) %collective-permute-start.69) | collective-permute-done | bytes 327712 | tf_op jit(solution)/shard_map/ppermute | solution.py:50
  410.2 3.6 collective-permute-start.79
  416.1 4.0 collective-permute-done.78
  (479 shorter events, 184.4 us)
Async XLA Ops:
  11.1 25.6 %collective-permute-start.4 = (bf16[512,1024]{1,0:T(8,128)(2,1)}, bf16[512,1024]{1,0:T(8,128)(2,1)S(1)}, u32[]{:S(2)}, u32[]{:S(2)}) collective-permute-start(bf16[512,1024]{1,0:T(8,128)(2,1)} %param.15), channel_id=1, source_target_pairs={{0,1},{1,0},{2,3},{3,2},{4,5},{5,4},{6,7},{7,6},{8,9},{9,8},{10,11... | collective-permute-start | bytes 3145736 | tf_op jit(solution)/shard_map/ppermute | solution.py:50
  18.1 18.6 %collective-permute-start.2 = (bf16[2,64,768]{2,1,0:T(8,128)(2,1)S(1)}, bf16[2,64,768]{2,1,0:T(8,128)(2,1)S(1)}, u32[]{:S(2)}, u32[]{:S(2)}) collective-permute-start(bf16[2,64,768]{2,1,0:T(8,128)(2,1)S(1)} %bitcast_dynamic-update-slice_fusion.43), channel_id=1, source_target_pairs={{0,16},{1,17},{2,18},{3,19},{4,20},{5,21},{6,22},{7,23},{8,24},{9,... | collective-permute-start | bytes 589832 | tf_op jit(solution)/shard_map/ppermute | solution.py:50
  41.0 26.5 %collective-permute-start.14 = (bf16[64,2560]{1,0:T(8,128)(2,1)S(1)}, bf16[64,2560]{1,0:T(8,128)(2,1)S(1)}, u32[]{:S(2)}, u32[]{:S(2)}) collective-permute-start(bf16[64,2560]{1,0:T(8,128)(2,1)S(1)} %pad_maximum_fusion.10), channel_id=1, source_target_pairs={{0,24},{1,25},{2,26},{3,27},{4,28},{5,29},{6,30},{7,31},{8,0},{9,1... | collective-permute-start | bytes 983048 | tf_op jit(solution)/shard_map/ppermute | solution.py:50
  41.1 35.9 %collective-permute-start.13 = (bf16[64,2560]{1,0:T(8,128)(2,1)S(1)}, bf16[64,2560]{1,0:T(8,128)(2,1)S(1)}, u32[]{:S(2)}, u32[]{:S(2)}) collective-permute-start(bf16[64,2560]{1,0:T(8,128)(2,1)S(1)} %pad_maximum_fusion.10), channel_id=1, source_target_pairs={{0,16},{1,17},{2,18},{3,19},{4,20},{5,21},{6,22},{7,23},{8,24},{9,... | collective-permute-start | bytes 983048 | tf_op jit(solution)/shard_map/ppermute | solution.py:50
  47.5 29.5 %collective-permute-start.12 = (bf16[64,2560]{1,0:T(8,128)(2,1)S(1)}, bf16[64,2560]{1,0:T(8,128)(2,1)S(1)}, u32[]{:S(2)}, u32[]{:S(2)}) collective-permute-start(bf16[64,2560]{1,0:T(8,128)(2,1)S(1)} %pad_maximum_fusion.10), channel_id=1, source_target_pairs={{0,8},{1,9},{2,10},{3,11},{4,12},{5,13},{6,14},{7,15},{8,16},{9,17... | collective-permute-start | bytes 983048 | tf_op jit(solution)/shard_map/ppermute | solution.py:50
  54.6 25.3 %collective-permute-start.21 = (bf16[2,64,1024]{2,1,0:T(8,128)(2,1)S(1)}, bf16[2,64,1024]{2,1,0:T(8,128)(2,1)S(1)}, u32[]{:S(2)}, u32[]{:S(2)}) collective-permute-start(bf16[2,64,1024]{2,1,0:T(8,128)(2,1)S(1)} %pad_maximum_fusion.11), channel_id=1, source_target_pairs={{0,24},{1,25},{2,26},{3,27},{4,28},{5,29},{6,30},{7,31},{8,0},{9,1... | collective-permute-start | bytes 786440 | tf_op jit(solution)/shard_map/ppermute | solution.py:50
  57.0 34.5 %collective-permute-start.20 = (bf16[2,64,1024]{2,1,0:T(8,128)(2,1)S(1)}, bf16[2,64,1024]{2,1,0:T(8,128)(2,1)S(1)}, u32[]{:S(2)}, u32[]{:S(2)}) collective-permute-start(bf16[2,64,1024]{2,1,0:T(8,128)(2,1)S(1)} %pad_maximum_fusion.11), channel_id=1, source_target_pairs={{0,16},{1,17},{2,18},{3,19},{4,20},{5,21},{6,22},{7,23},{8,24},{9,... | collective-permute-start | bytes 786440 | tf_op jit(solution)/shard_map/ppermute | solution.py:50
  77.3 26.2 %collective-permute-start.18 = (bf16[4,64,1280]{2,1,0:T(8,128)(2,1)S(1)}, bf16[4,64,1280]{2,1,0:T(8,128)(2,1)S(1)}, u32[]{:S(2)}, u32[]{:S(2)}) collective-permute-start(bf16[4,64,1280]{2,1,0:T(8,128)(2,1)S(1)} %get-tuple-element.341), channel_id=1, source_target_pairs={{0,1},{1,0},{2,3},{3,2},{4,5},{5,4},{6,7},{7,6},{8,9},{9,8},{10,11... | collective-permute-start | bytes 1966088 | tf_op jit(solution)/shard_map/ppermute | solution.py:50
  78.8 28.7 %collective-permute-start.16 = (bf16[4,64,1280]{2,1,0:T(8,128)(2,1)S(1)}, bf16[4,64,1280]{2,1,0:T(8,128)(2,1)S(1)}, u32[]{:S(2)}, u32[]{:S(2)}) collective-permute-start(bf16[4,64,1280]{2,1,0:T(8,128)(2,1)S(1)} %get-tuple-element.341), channel_id=1, source_target_pairs={{0,4},{1,5},{2,6},{3,7},{4,0},{5,1},{6,2},{7,3},{8,12},{9,13},{10,... | collective-permute-start | bytes 1966088 | tf_op jit(solution)/shard_map/ppermute | solution.py:50
  79.4 28.5 %collective-permute-start.17 = (bf16[4,64,1280]{2,1,0:T(8,128)(2,1)S(1)}, bf16[4,64,1280]{2,1,0:T(8,128)(2,1)S(1)}, u32[]{:S(2)}, u32[]{:S(2)}) collective-permute-start(bf16[4,64,1280]{2,1,0:T(8,128)(2,1)S(1)} %get-tuple-element.342), channel_id=1, source_target_pairs={{0,1},{1,0},{2,3},{3,2},{4,5},{5,4},{6,7},{7,6},{8,9},{9,8},{10,11... | collective-permute-start | bytes 1966088 | tf_op jit(solution)/shard_map/ppermute | solution.py:50
  79.9 34.4 %collective-permute-start.15 = (bf16[4,64,1280]{2,1,0:T(8,128)(2,1)S(1)}, bf16[4,64,1280]{2,1,0:T(8,128)(2,1)S(1)}, u32[]{:S(2)}, u32[]{:S(2)}) collective-permute-start(bf16[4,64,1280]{2,1,0:T(8,128)(2,1)S(1)} %get-tuple-element.342), channel_id=1, source_target_pairs={{0,4},{1,5},{2,6},{3,7},{4,0},{5,1},{6,2},{7,3},{8,12},{9,13},{10,... | collective-permute-start | bytes 1966088 | tf_op jit(solution)/shard_map/ppermute | solution.py:50
  101.9 72.4 %collective-permute-start.40 = (f32[2048]{0:T(1024)S(1)}, f32[2048]{0:T(1024)S(1)}, u32[]{:S(2)}, u32[]{:S(2)}) collective-permute-start(f32[2048]{0:T(1024)S(1)} %copy-done.50), channel_id=1, source_target_pairs={{0,1},{1,0},{2,3},{3,2},{4,5},{5,4},{6,7},{7,6},{8,9},{9,8},{10,11... | collective-permute-start | bytes 24584 | tf_op jit(solution)/shard_map/ppermute | solution.py:50
  107.5 21.3 %collective-permute-start.24 = (bf16[2,64,1024]{2,1,0:T(8,128)(2,1)S(1)}, bf16[2,64,1024]{2,1,0:T(8,128)(2,1)S(1)}, u32[]{:S(2)}, u32[]{:S(2)}) collective-permute-start(bf16[2,64,1024]{2,1,0:T(8,128)(2,1)S(1)} %pad_maximum_fusion.12), channel_id=1, source_target_pairs={{0,16},{1,17},{2,18},{3,19},{4,20},{5,21},{6,22},{7,23},{8,24},{9,... | collective-permute-start | bytes 786440 | tf_op jit(solution)/shard_map/ppermute | solution.py:50
  107.9 21.5 %collective-permute-start.23 = (bf16[2,64,1024]{2,1,0:T(8,128)(2,1)S(1)}, bf16[2,64,1024]{2,1,0:T(8,128)(2,1)S(1)}, u32[]{:S(2)}, u32[]{:S(2)}) collective-permute-start(bf16[2,64,1024]{2,1,0:T(8,128)(2,1)S(1)} %pad_maximum_fusion.12), channel_id=1, source_target_pairs={{0,8},{1,9},{2,10},{3,11},{4,12},{5,13},{6,14},{7,15},{8,16},{9,17... | collective-permute-start | bytes 786440 | tf_op jit(solution)/shard_map/ppermute | solution.py:50
  128.8 21.6 %collective-permute-start.38 = (bf16[4,64,1280]{2,1,0:T(8,128)(2,1)S(1)}, bf16[4,64,1280]{2,1,0:T(8,128)(2,1)S(1)}, u32[]{:S(2)}, u32[]{:S(2)}) collective-permute-start(bf16[4,64,1280]{2,1,0:T(8,128)(2,1)S(1)} %collective-permute-done.18), channel_id=1, source_target_pairs={{0,4},{1,5},{2,6},{3,7},{4,0},{5,1},{6,2},{7,3},{8,12},{9,13},{10,... | collective-permute-start | bytes 1966088 | tf_op jit(solution)/shard_map/ppermute | solution.py:50
  136.7 28.0 %collective-permute-start.35 = (bf16[4,2,64,1024]{3,2,0,1:T(8,128)(2,1)S(1)}, bf16[4,2,64,1024]{3,2,0,1:T(8,128)(2,1)S(1)}, u32[]{:S(2)}, u32[]{:S(2)}) collective-permute-start(bf16[4,2,64,1024]{3,2,0,1:T(8,128)(2,1)S(1)} %bitcast_dynamic-update-slice_fusion.20), channel_id=1, source_target_pairs={{0,4},{1,5},{2,6},{3,7},{4,0},{5,1},{6,2},{7,3},{8,12},{9,13},{10,... | collective-permute-start | bytes 3145736 | tf_op jit(solution)/shard_map/ppermute | solution.py:50
  148.7 25.6 %collective-permute-start.41 = (bf16[4,2,64,1024]{3,2,0,1:T(8,128)(2,1)S(1)}, bf16[4,2,64,1024]{3,2,0,1:T(8,128)(2,1)S(1)}, u32[]{:S(2)}, u32[]{:S(2)}) collective-permute-start(bf16[4,2,64,1024]{3,2,0,1:T(8,128)(2,1)S(1)} %bitcast_dynamic-update-slice_fusion.26), channel_id=1, source_target_pairs={{0,1},{1,0},{2,3},{3,2},{4,5},{5,4},{6,7},{7,6},{8,9},{9,8},{10,11... | collective-permute-start | bytes 3145736 | tf_op jit(solution)/shard_map/ppermute | solution.py:50
  150.4 26.9 %collective-permute-start.34 = (bf16[4,2,64,1024]{3,2,0,1:T(8,128)(2,1)S(1)}, bf16[4,2,64,1024]{3,2,0,1:T(8,128)(2,1)S(1)}, u32[]{:S(2)}, u32[]{:S(2)}) collective-permute-start(bf16[4,2,64,1024]{3,2,0,1:T(8,128)(2,1)S(1)} %bitcast_dynamic-update-slice_fusion.26), channel_id=1, source_target_pairs={{0,2},{1,3},{2,0},{3,1},{4,6},{5,7},{6,4},{7,5},{8,10},{9,11},{10,... | collective-permute-start | bytes 3145736 | tf_op jit(solution)/shard_map/ppermute | solution.py:50
  265.3 26.4 %collective-permute-start.53 = (bf16[4,64,2048]{2,1,0:T(8,128)(2,1)}, bf16[4,64,2048]{2,1,0:T(8,128)(2,1)}, u32[]{:S(2)}, u32[]{:S(2)}) collective-permute-start(bf16[4,64,2048]{2,1,0:T(8,128)(2,1)} %pad_maximum_fusion.7), channel_id=1, source_target_pairs={{0,1},{1,0},{2,3},{3,2},{4,5},{5,4},{6,7},{7,6},{8,9},{9,8},{10,11... | collective-permute-start | bytes 3145736 | tf_op jit(solution)/shard_map/ppermute | solution.py:50
  265.9 26.5 %collective-permute-start.52 = (bf16[4,64,2048]{2,1,0:T(8,128)(2,1)}, bf16[4,64,2048]{2,1,0:T(8,128)(2,1)}, u32[]{:S(2)}, u32[]{:S(2)}) collective-permute-start(bf16[4,64,2048]{2,1,0:T(8,128)(2,1)} %pad_maximum_fusion.6), channel_id=1, source_target_pairs={{0,4},{1,5},{2,6},{3,7},{4,0},{5,1},{6,2},{7,3},{8,12},{9,13},{10,... | collective-permute-start | bytes 3145736 | tf_op jit(solution)/shard_map/ppermute | solution.py:50
  266.5 19.4 %collective-permute-start.56 = (f32[10240]{0:T(1024)S(1)}, f32[10240]{0:T(1024)S(1)}, u32[]{:S(2)}, u32[]{:S(2)}) collective-permute-start(f32[10240]{0:T(1024)S(1)} %constant_dynamic-update-slice_fusion.11), channel_id=1, source_target_pairs={{0,2},{1,3},{2,0},{3,1},{4,6},{5,7},{6,4},{7,5},{8,10},{9,11},{10,... | collective-permute-start | bytes 122888 | tf_op jit(solution)/shard_map/ppermute | solution.py:50
  268.0 35.9 %collective-permute-start.55 = (bf16[4,64,1280]{2,1,0:T(8,128)(2,1)S(1)}, bf16[4,64,1280]{2,1,0:T(8,128)(2,1)S(1)}, u32[]{:S(2)}, u32[]{:S(2)}) collective-permute-start(bf16[4,64,1280]{2,1,0:T(8,128)(2,1)S(1)} %get-tuple-element.308), channel_id=1, source_target_pairs={{0,1},{1,0},{2,3},{3,2},{4,5},{5,4},{6,7},{7,6},{8,9},{9,8},{10,11... | collective-permute-start | bytes 1966088 | tf_op jit(solution)/shard_map/ppermute | solution.py:50
  269.6 34.7 %collective-permute-start.54 = (bf16[4,64,1280]{2,1,0:T(8,128)(2,1)S(1)}, bf16[4,64,1280]{2,1,0:T(8,128)(2,1)S(1)}, u32[]{:S(2)}, u32[]{:S(2)}) collective-permute-start(bf16[4,64,1280]{2,1,0:T(8,128)(2,1)S(1)} %get-tuple-element.309), channel_id=1, source_target_pairs={{0,4},{1,5},{2,6},{3,7},{4,0},{5,1},{6,2},{7,3},{8,12},{9,13},{10,... | collective-permute-start | bytes 1966088 | tf_op jit(solution)/shard_map/ppermute | solution.py:50
  307.4 40.8 %collective-permute-start.64 = (bf16[64,2048]{1,0:T(8,128)(2,1)}, bf16[64,2048]{1,0:T(8,128)(2,1)}, u32[]{:S(2)}, u32[]{:S(2)}) collective-permute-start(bf16[64,2048]{1,0:T(8,128)(2,1)} %get-tuple-element.310), channel_id=1, source_target_pairs={{0,24},{1,25},{2,26},{3,27},{4,28},{5,29},{6,30},{7,31},{8,0},{9,1... | collective-permute-start | bytes 786440 | tf_op jit(solution)/shard_map/ppermute | solution.py:50
  307.4 41.2 %collective-permute-start.63 = (bf16[64,2048]{1,0:T(8,128)(2,1)}, bf16[64,2048]{1,0:T(8,128)(2,1)}, u32[]{:S(2)}, u32[]{:S(2)}) collective-permute-start(bf16[64,2048]{1,0:T(8,128)(2,1)} %get-tuple-element.311), channel_id=1, source_target_pairs={{0,16},{1,17},{2,18},{3,19},{4,20},{5,21},{6,22},{7,23},{8,24},{9,... | collective-permute-start | bytes 786440 | tf_op jit(solution)/shard_map/ppermute | solution.py:50
  312.6 48.5 %collective-permute-start.61 = (bf16[4,64,2560]{2,1,0:T(8,128)(2,1)}, bf16[4,64,2560]{2,1,0:T(8,128)(2,1)}, u32[]{:S(2)}, u32[]{:S(2)}) collective-permute-start(bf16[4,64,2560]{2,1,0:T(8,128)(2,1)} %pad_maximum_fusion.4), channel_id=1, source_target_pairs={{0,1},{1,0},{2,3},{3,2},{4,5},{5,4},{6,7},{7,6},{8,9},{9,8},{10,11... | collective-permute-start | bytes 3932168 | tf_op jit(solution)/shard_map/ppermute | solution.py:50
  321.3 39.8 %collective-permute-start.60 = (bf16[4,64,2560]{2,1,0:T(8,128)(2,1)}, bf16[4,64,2560]{2,1,0:T(8,128)(2,1)}, u32[]{:S(2)}, u32[]{:S(2)}) collective-permute-start(bf16[4,64,2560]{2,1,0:T(8,128)(2,1)} %pad_maximum_fusion.3), channel_id=1, source_target_pairs={{0,4},{1,5},{2,6},{3,7},{4,0},{5,1},{6,2},{7,3},{8,12},{9,13},{10,... | collective-permute-start | bytes 3932168 | tf_op jit(solution)/shard_map/ppermute | solution.py:50
  342.3 18.8 %collective-permute-start.58 = (bf16[4,2,64,768]{3,2,1,0:T(8,128)(2,1)S(1)}, bf16[4,2,64,768]{3,2,1,0:T(8,128)(2,1)S(1)}, u32[]{:S(2)}, u32[]{:S(2)}) collective-permute-start(bf16[4,2,64,768]{3,2,1,0:T(8,128)(2,1)S(1)} %get-tuple-element.291), channel_id=1, source_target_pairs={{0,2},{1,3},{2,0},{3,1},{4,6},{5,7},{6,4},{7,5},{8,10},{9,11},{10,... | collective-permute-start | bytes 2359304 | tf_op jit(solution)/shard_map/ppermute | solution.py:50
  366.2 37.0 %collective-permute-start.74 = (bf16[512,1024]{1,0:T(8,128)(2,1)S(1)}, bf16[512,1024]{1,0:T(8,128)(2,1)S(1)}, u32[]{:S(2)}, u32[]{:S(2)}) collective-permute-start(bf16[512,1024]{1,0:T(8,128)(2,1)S(1)} %fusion.18), channel_id=1, source_target_pairs={{0,1},{1,0},{2,3},{3,2},{4,5},{5,4},{6,7},{7,6},{8,9},{9,8},{10,11... | collective-permute-start | bytes 3145736 | tf_op jit(solution)/shard_map/ppermute | solution.py:50
  370.5 25.6 %collective-permute-start.70 = (bf16[64,2560]{1,0:T(8,128)(2,1)S(1)}, bf16[64,2560]{1,0:T(8,128)(2,1)S(1)}, u32[]{:S(2)}, u32[]{:S(2)}) collective-permute-start(bf16[64,2560]{1,0:T(8,128)(2,1)S(1)} %get-tuple-element.300), channel_id=1, source_target_pairs={{0,24},{1,25},{2,26},{3,27},{4,28},{5,29},{6,30},{7,31},{8,0},{9,1... | collective-permute-start | bytes 983048 | tf_op jit(solution)/shard_map/ppermute | solution.py:50
  372.4 30.7 %collective-permute-start.69 = (bf16[64,2560]{1,0:T(8,128)(2,1)S(1)}, bf16[64,2560]{1,0:T(8,128)(2,1)S(1)}, u32[]{:S(2)}, u32[]{:S(2)}) collective-permute-start(bf16[64,2560]{1,0:T(8,128)(2,1)S(1)} %get-tuple-element.301), channel_id=1, source_target_pairs={{0,16},{1,17},{2,18},{3,19},{4,20},{5,21},{6,22},{7,23},{8,24},{9,... | collective-permute-start | bytes 983048 | tf_op jit(solution)/shard_map/ppermute | solution.py:50
  373.9 29.3 %collective-permute-start.68 = (bf16[64,2560]{1,0:T(8,128)(2,1)S(1)}, bf16[64,2560]{1,0:T(8,128)(2,1)S(1)}, u32[]{:S(2)}, u32[]{:S(2)}) collective-permute-start(bf16[64,2560]{1,0:T(8,128)(2,1)S(1)} %get-tuple-element.302), channel_id=1, source_target_pairs={{0,8},{1,9},{2,10},{3,11},{4,12},{5,13},{6,14},{7,15},{8,16},{9,17... | collective-permute-start | bytes 983048 | tf_op jit(solution)/shard_map/ppermute | solution.py:50
  (108 other events, 1119.8 us)
